TPU v7x, 512 devices: a whole 4x8x8 slice. The times are simulated.
512 devices in a mesh: wide: 32 (over y_hi, x, core), narrow: 16 (over z, y_lo).
Axes of the slice: x: 4, y: 8 (y_hi: 4, y_lo: 2; y = y_hi * 2 + y_lo), z: 8, core: 2. Of those that a mesh axis runs over, the one named last changes fastest.
Arguments:
- layer_input: bfloat16 [1536, 10240], P('wide', 'narrow'), may hold values from -3 to 3
- output_grad: bfloat16 [1536, 10240], P('wide', 'narrow'), may hold values from -0.75 to 0.75
- pre_activation: bfloat16 [1536, 20480], P('narrow', 'wide'), may hold values from -6 to 6
- w_up: bfloat16 [10240, 20480], P('narrow', 'wide'), may hold values from -0.15625 to 0.15625
- w_down: bfloat16 [20480, 10240], P('wide', 'narrow'), may hold values from -0.25 to 0.25
Outputs:
- input_grad: bfloat16 [1536, 10240], P('wide', 'narrow')
- up_grad: float32 [10240, 20480], P('narrow', 'wide')
- down_grad: float32 [20480, 10240], P('wide', 'narrow')
All inputs are finite; a program needn't handle non-finite values.
Results may differ from a plain program's by a relative error of at most 0.03.
Values may be sent and summed in bfloat16 or wider, within the bound.
No kernel may reach another device: no remote copies, remote signals or barrier semaphores. Data moves between devices by JAX's collectives and lax.ppermute only.
A program may use at most 64 MiB of HBM per device.

v0:
```python
import math

import jax
import jax.numpy as jnp
from jax import lax
from jax.sharding import PartitionSpec as P


def gelu_parts(pre_values):
    values = pre_values.astype(jnp.float32)
    normal_cdf = 0.5 * (1.0 + jax.scipy.special.erf(values / math.sqrt(2.0)))
    normal_pdf = jnp.exp(-0.5 * values * values) / math.sqrt(2.0 * math.pi)
    return (values * normal_cdf, normal_cdf + values * normal_pdf)


def times_transposed(left, right):
    return lax.dot_general(
        left, right, (((1,), (1,)), ((), ())), preferred_element_type=jnp.float32
    )


def over_tokens(left, right):
    return lax.dot_general(
        left, right, (((0,), (0,)), ((), ())), preferred_element_type=jnp.float32
    )


def per_device(layer_input, output_grad, pre_activation, w_up, w_down):
    input_cols, grad_cols = (
        lax.all_gather(layer_input, "wide", axis=0, tiled=True),
        lax.all_gather(output_grad, "wide", axis=0, tiled=True),
    )
    gelu_value, gelu_slope = gelu_parts(pre_activation)
    act_tile = gelu_value.astype(jnp.bfloat16)
    act_all = lax.all_gather(act_tile, "narrow", axis=0, tiled=True)
    row_block = grad_cols
    act_grad = lax.psum_scatter(
        times_transposed(row_block, w_down).astype(jnp.bfloat16),
        "narrow",
        scatter_dimension=0,
        tiled=True,
    ).astype(jnp.float32)
    slope_tile = (act_grad * gelu_slope).astype(jnp.bfloat16)
    slope_grad = lax.all_gather(slope_tile, "narrow", axis=0, tiled=True)
    down_grad = over_tokens(act_all, grad_cols)
    up_grad = over_tokens(input_cols, slope_grad)
    row_block = slope_grad
    input_grad = lax.psum_scatter(
        times_transposed(row_block, w_up).astype(jnp.bfloat16),
        "wide",
        scatter_dimension=0,
        tiled=True,
    )
    return (input_grad, up_grad, down_grad)


def solution(mesh):
    placed = (
        P("wide", "narrow"),
        P("wide", "narrow"),
        P("narrow", "wide"),
        P("narrow", "wide"),
        P("wide", "narrow"),
    )
    return jax.shard_map(
        per_device,
        mesh=mesh,
        in_specs=placed,
        out_specs=(P("wide", "narrow"), P("narrow", "wide"), P("wide", "narrow")),
        check_vma=False,
    )
```

profile of v0, /device:TPU:1, one launch (start us, length us, event | category | flops | bytes accessed | tf_op | source)
XLA Modules:
  0.0 486.9 jit_solution(4600899023487702191)
XLA Ops:
  7.2 0.0 all-gather.5.cloned.1.call-start
  7.2 0.7 all-gather.5.cloned.1.call-update
  7.9 0.0 reduce-scatter.3.cloned.1.call-start
  8.0 68.3 %all-gather.5.cloned.1.call-done = bf16[1536,640]{1,0:T(8,128)(2,1)} async-done(((bf16[48,640]{1,0:T(8,128)(2,1)}), bf16[1536,640]{1,0:T(8,128)(2,1)}) %all-gather.5.cloned.1.call-update) | async-done | bytes 1966096 | tf_op jit(solution)/shard_map/all_gather | solution.py:31
  76.3 4.7 convolution_convert_fusion.1
  81.0 0.0 reduce-scatter.3.cloned.1.call-update
  81.0 0.0 all-gather.7.cloned.1.call-start
  81.0 66.8 %reduce-scatter.3.cloned.1.call-done = bf16[96,640]{1,0:T(8,128)(2,1)} async-done(((bf16[1536,640]{1,0:T(8,128)(2,1)}), bf16[96,640]{1,0:T(8,128)(2,1)}) %reduce-scatter.3.cloned.1.call-update) | async-done | bytes 122896 | tf_op jit(solution)/shard_map/reduce_scatter | solution.py:37
  147.8 1.7 fusion.8
  149.5 0.0 all-gather.7.cloned.1.call-update
  149.6 0.0 all-gather.9.cloned.1.call-start
  149.6 0.5 all-gather.9.cloned.1.call-update
  150.1 0.0 all-gather.11.cloned.1.call-start
  150.2 0.5 all-gather.11.cloned.1.call-update
  150.7 0.0 reduce-scatter.5.cloned.1.call-start
  150.8 77.7 %all-gather.7.cloned.1.call-done = bf16[1536,640]{1,0:T(8,128)(2,1)} async-done(((bf16[96,640]{1,0:T(8,128)(2,1)}), bf16[1536,640]{1,0:T(8,128)(2,1)}) %all-gather.7.cloned.1.call-update) | async-done | bytes 1966096 | tf_op jit(solution)/shard_map/all_gather | solution.py:44
  228.5 4.8 convolution_convert_fusion
  233.2 0.0 reduce-scatter.5.cloned.1.call-update
  233.3 67.0 %all-gather.9.cloned.1.call-done = bf16[1536,640]{1,0:T(8,128)(2,1)} async-done(((bf16[48,640]{1,0:T(8,128)(2,1)}), bf16[1536,640]{1,0:T(8,128)(2,1)}) %all-gather.9.cloned.1.call-update) | async-done | bytes 1966096 | tf_op jit(solution)/shard_map/all_gather | solution.py:30
  300.3 3.9 convolution_bitcast_fusion
  304.1 1.7 copy.8
  305.8 63.6 %all-gather.11.cloned.1.call-done = bf16[1536,640]{1,0:T(8,128)(2,1)} async-done(((bf16[96,640]{1,0:T(8,128)(2,1)}), bf16[1536,640]{1,0:T(8,128)(2,1)}) %all-gather.11.cloned.1.call-update) | async-done | bytes 1966096 | tf_op jit(solution)/shard_map/all_gather | solution.py:35
  369.4 5.0 %fusion.9 = f32[640,640]{1,0:T(8,128)} fusion(bf16[1536,640]{1,0:T(8,128)(2,1)} %all-gather.11.cloned.1.call-done, bf16[1536,640]{1,0:T(8,128)(2,1)} %all-gather.5.cloned.1.call-done), kind=kOutput, calls=%fused_computation.17 | convolution fusion | flops 1258291200 | bytes 5570560 | tf_op jit(solution)/shard_map/dot_general | solution.py:23
  374.5 105.6 %reduce-scatter.5.cloned.1.call-done = bf16[48,640]{1,0:T(8,128)(2,1)} async-done(((bf16[1536,640]{1,0:T(8,128)(2,1)}), bf16[48,640]{1,0:T(8,128)(2,1)}) %reduce-scatter.5.cloned.1.call-update) | async-done | bytes 61456 | tf_op jit(solution)/shard_map/reduce_scatter | solution.py:48
  (6 shorter events, 0.0 us)
Async XLA Ops:
  7.2 69.1 %copy-start = (bf16[640,640]{1,0:T(8,128)(2,1)S(1)}, bf16[640,640]{1,0:T(8,128)(2,1)}, u32[]{:S(2)}) copy-start(bf16[640,640]{1,0:T(8,128)(2,1)} %param.9) | copy-start | bytes 2457604
  7.2 69.1 %all-gather.5.cloned.1.call-start = ((), (), s32[]{:S(2)}) async-start(), calls=%async_computation.2 | async-start | bytes 2027520 | tf_op jit(solution)/shard_map/all_gather | solution.py:31
  7.9 139.9 %reduce-scatter.3.cloned.1.call-start = ((), (), s32[]{:S(2)}) async-start(), calls=%async_computation.3 | async-start | bytes 2088960 | tf_op jit(solution)/shard_map/reduce_scatter | solution.py:37
  81.0 66.8 %copy-start.1 = (bf16[96,640]{1,0:T(8,128)(2,1)S(1)}, bf16[96,640]{1,0:T(8,128)(2,1)}, u32[]{:S(2)}) copy-start(bf16[96,640]{1,0:T(8,128)(2,1)} %param.7) | copy-start | bytes 368644
  81.0 147.5 %copy-start.2 = (bf16[640,640]{1,0:T(8,128)(2,1)S(1)}, bf16[640,640]{1,0:T(8,128)(2,1)}, u32[]{:S(2)}) copy-start(bf16[640,640]{1,0:T(8,128)(2,1)} %param.8) | copy-start | bytes 2457604
  81.0 147.5 %all-gather.7.cloned.1.call-start = ((), (), s32[]{:S(2)}) async-start(), calls=%async_computation.4 | async-start | bytes 2088960 | tf_op jit(solution)/shard_map/all_gather | solution.py:44
  149.6 150.7 %all-gather.9.cloned.1.call-start = ((), (), s32[]{:S(2)}) async-start(), calls=%async_computation.6 | async-start | bytes 2027520 | tf_op jit(solution)/shard_map/all_gather | solution.py:30
  150.1 219.3 %all-gather.11.cloned.1.call-start = ((), (), s32[]{:S(2)}) async-start(), calls=%async_computation.7 | async-start | bytes 2088960 | tf_op jit(solution)/shard_map/all_gather | solution.py:35
  150.7 329.3 %reduce-scatter.5.cloned.1.call-start = ((), (), s32[]{:S(2)}) async-start(), calls=%async_computation.5 | async-start | bytes 2027520 | tf_op jit(solution)/shard_map/reduce_scatter | solution.py:48
Sparse Core Ops, SparseCore 0:
  11.2 64.9 all-gather.4
  81.1 66.6 reduce-scatter.2
  150.7 77.7 all-gather.6
  232.0 68.1 all-gather.8
  303.0 66.4 all-gather.10
  375.0 105.0 reduce-scatter.4
where the time goes:
time: 488 us; the launch traced here: 487 us
  waiting for transfers between devices  451 us (92%)
  matrix products  18.4 us (4%)
  between operations  14.1 us (3%)
    reduce_scatter x1, waiting for transfers between devices, per_device(): lax.psum_scatter(times_transposed(row_block, w_up).astype(jnp.bfloat16),...  106 us
    all_gather x1, waiting for transfers between devices, per_device(): slope_grad = lax.all_gather(slope_tile, 'narrow', axis=0, tiled=True)  77.7 us
    all_gather x1, waiting for transfers between devices, per_device(): lax.all_gather(output_grad, 'wide', axis=0, tiled=True)  68.3 us
    all_gather x1, waiting for transfers between devices, per_device(): lax.all_gather(layer_input, 'wide', axis=0, tiled=True)  67 us
    reduce_scatter x1, waiting for transfers between devices, per_device(): lax.psum_scatter(times_transposed(row_block, w_down).astype(jnp.bfloat16)...  66.8 us
    all_gather x1, waiting for transfers between devices, per_device(): act_all = lax.all_gather(act_tile, 'narrow', axis=0, tiled=True)  63.6 us
  transfers between devices with their start and end apart: 6, of which 6 were waited for; matrix products, arithmetic and copies ran while one was open for 3% of the time, Pallas kernels for 0%

commit v1 on v0

v1 whole, which is shorter than its diff:
```python
import math

import jax
import jax.numpy as jnp
from jax import lax
from jax.sharding import Mesh, PartitionSpec as P

WIDE = ("yh", "x", "c")
NARROW = ("z", "yl")
CHIPS = ("yh", "x")


def gelu_parts(pre_values):
    values = pre_values.astype(jnp.float32)
    normal_cdf = 0.5 * (1.0 + jax.scipy.special.erf(values / math.sqrt(2.0)))
    normal_pdf = jnp.exp(-0.5 * values * values) / math.sqrt(2.0 * math.pi)
    return (values * normal_cdf, normal_cdf + values * normal_pdf)


def times_transposed(left, right):
    return lax.dot_general(
        left, right, (((1,), (1,)), ((), ())), preferred_element_type=jnp.float32
    )


def over_tokens(left, right):
    dims = tuple(range(left.ndim - 1))
    return lax.dot_general(
        left, right, ((dims, dims), ((), ())), preferred_element_type=jnp.float32
    )


def swap(values, axis):
    return lax.ppermute(values, axis, [(0, 1), (1, 0)])


def scattered(values, axis):
    blocks = lax.all_to_all(values, axis, 0, 0)
    return jnp.sum(blocks.astype(jnp.float32), axis=0)


def per_device(layer_input, output_grad, pre_activation, w_up, w_down):
    core = lax.axis_index("c")
    rows, width = layer_input.shape
    w_down_pair = swap(w_down, "c")
    grad_own = lax.all_to_all(
        jnp.broadcast_to(output_grad, (16, rows, width)), CHIPS, 0, 0
    )
    low, high = pre_activation[:rows], pre_activation[rows:]
    pre_own = jnp.where(core == 0, low, high)
    pre_pair = swap(jnp.where(core == 0, high, low), "c")
    _, slope_own_f = gelu_parts(pre_own)
    _, slope_pair_f = gelu_parts(pre_pair)
    act_tile = gelu_parts(pre_activation)[0].astype(jnp.bfloat16)
    act_all = lax.all_gather(act_tile, NARROW, axis=0, tiled=True)
    input_all = lax.all_gather(layer_input, ("c",) + CHIPS, axis=0, tiled=True)
    w_up_pair = swap(w_up, "c")

    grad_rows = grad_own.reshape(16 * rows, width)
    part_own = times_transposed(grad_rows, w_down).astype(jnp.bfloat16)
    part_pair = times_transposed(grad_rows, w_down_pair).astype(jnp.bfloat16)
    act_grad_own = scattered(part_own.reshape(16, rows, -1), NARROW)
    act_grad_pair = scattered(part_pair.reshape(16, rows, -1), NARROW)
    slope_own = (act_grad_own * slope_own_f).astype(jnp.bfloat16)
    slope_pair = (act_grad_pair * slope_pair_f).astype(jnp.bfloat16)

    def gathered(tile):
        both = lax.all_gather(tile, "yl", axis=0, tiled=True)
        return lax.all_gather(both, "z", axis=0, tiled=True)

    slopes_own = gathered(slope_own)
    slopes_pair = gathered(slope_pair)
    slopes_other = swap(slopes_pair, "c")
    grad_other = swap(grad_rows, "c")

    part_in = times_transposed(slopes_own, w_up) + times_transposed(
        slopes_pair, w_up_pair
    )
    input_grad = scattered(
        part_in.astype(jnp.bfloat16).reshape(16, rows, width), CHIPS
    ).astype(jnp.bfloat16)

    act_parts = act_all.reshape(16, 2, rows, -1)
    grad_parts = [
        jnp.where(core == 0, grad_rows, grad_other),
        jnp.where(core == 0, grad_other, grad_rows),
    ]
    down_grad = sum(
        over_tokens(act_parts[:, i], grad_parts[i].reshape(16, rows, width))
        for i in range(2)
    )
    slope_parts = [
        jnp.where(core == 0, slopes_own, slopes_other),
        jnp.where(core == 0, slopes_other, slopes_own),
    ]
    half = 16 * rows
    up_grad = over_tokens(input_all[:half], slope_parts[0]) + over_tokens(
        input_all[half:], slope_parts[1]
    )
    return (input_grad, up_grad, down_grad)


def solution(mesh):
    fine = Mesh(mesh.devices.reshape(4, 4, 2, 8, 2), WIDE + NARROW)
    tokens = P(WIDE, NARROW)
    hidden = P(NARROW, WIDE)
    return jax.shard_map(
        per_device,
        mesh=fine,
        in_specs=(tokens, tokens, hidden, hidden, tokens),
        out_specs=(tokens, hidden, tokens),
        check_vma=False,
    )
```

time: 488 us -> 231 us (0.47)
  the two profiles are of different devices: /device:TPU:1 before, /device:TPU:8 now
where the time goes in v1:
time: 231 us; the launch traced here: 230 us
  blocking collectives  74.7 us (32%)
  waiting for transfers between devices  62.2 us (27%)
  starting transfers between devices  51.6 us (22%)
  matrix products  17.7 us (8%)
  between operations  14.2 us (6%)
  other arithmetic  5.76 us (2%)
  local copies, waits for them, and re-layouts  3.64 us (2%)
    all_gather x2, blocking collectives, gathered(): return lax.all_gather(both, 'z', axis=0, tiled=True)  53.2 us
    all_to_all x3, waiting for transfers between devices, scattered(): blocks = lax.all_to_all(values, axis, 0, 0)  42 us
    all_to_all x3, starting transfers between devices, scattered(): blocks = lax.all_to_all(values, axis, 0, 0)  32.7 us
    all_gather x2, blocking collectives, gathered(): both = lax.all_gather(tile, 'yl', axis=0, tiled=True)  21.5 us
    all_to_all x1, waiting for transfers between devices, per_device(): lax.all_to_all(jnp.broadcast_to(output_grad, (16, rows, width)), CHIPS, 0...  18 us
    ppermute x5, starting transfers between devices, swap(): return lax.ppermute(values, axis, [(0, 1), (1, 0)])  10.1 us
    dot_general x4, matrix products, times_transposed(): lax.dot_general(left, right, (((1,), (1,)), ((), ())), preferred_element_...  9.32 us
    all_to_all x1, starting transfers between devices, per_device(): lax.all_to_all(jnp.broadcast_to(output_grad, (16, rows, width)), CHIPS, 0...  8.77 us
  transfers between devices with their start and end apart: 11, of which 5 were waited for; matrix products, arithmetic and copies ran while one was open for 10% of the time, Pallas kernels for 0%

profile of v1, /device:TPU:8, one launch (start us, length us, event | category | flops | bytes accessed | tf_op | source)
XLA Modules:
  0.0 230.0 jit_solution(15347332394858979287)
XLA Ops:
  7.2 1.9 broadcast_in_dim.3
  9.1 8.8 %all-to-all-start = ((bf16[16,48,640]{2,1,0:T(8,128)(2,1)}), bf16[16,48,640]{2,1,0:T(8,128)(2,1)S(1)}, u32[]{:S(2)}, u32[]{:S(2)}) async-start(bf16[16,48,640]{2,1,0:T(8,128)(2,1)} %broadcast_in_dim.3), calls=%async_computation | async-start | bytes 1966080 | tf_op jit(solution)/shard_map/all_to_all | solution.py:46
  22.2 18.0 %all-to-all-done = bf16[16,48,640]{2,1,0:T(8,128)(2,1)S(1)} async-done(((bf16[16,48,640]{2,1,0:T(8,128)(2,1)}), bf16[16,48,640]{2,1,0:T(8,128)(2,1)S(1)}, u32[]{:S(2)}, u32[]{:S(2)}) %all-to-all-start) | async-done | bytes 983072 | tf_op jit(solution)/shard_map/all_to_all | solution.py:46
  40.2 2.0 convolution_convert_fusion
  42.2 20.5 %all-to-all-start.2 = ((bf16[16,48,640]{2,1,0:T(8,128)(2,1)}), bf16[16,48,640]{2,1,0:T(8,128)(2,1)S(1)}, u32[]{:S(2)}, u32[]{:S(2)}) async-start(bf16[16,48,640]{2,1,0:T(8,128)(2,1)} %bitcast.2), calls=%async_computation.2 | async-start | bytes 1966080 | tf_op jit(solution)/shard_map/all_to_all | solution.py:38
  62.6 2.0 convolution_convert_fusion.1
  64.6 26.7 %all-to-all-done.2 = bf16[16,48,640]{2,1,0:T(8,128)(2,1)S(1)} async-done(((bf16[16,48,640]{2,1,0:T(8,128)(2,1)}), bf16[16,48,640]{2,1,0:T(8,128)(2,1)S(1)}, u32[]{:S(2)}, u32[]{:S(2)}) %all-to-all-start.2) | async-done | bytes 983072 | tf_op jit(solution)/shard_map/all_to_all | solution.py:38
  91.3 7.2 %all-to-all-start.1 = ((bf16[16,48,640]{2,1,0:T(8,128)(2,1)}), bf16[16,48,640]{2,1,0:T(8,128)(2,1)S(1)}, u32[]{:S(2)}, u32[]{:S(2)}) async-start(bf16[16,48,640]{2,1,0:T(8,128)(2,1)} %bitcast.38), calls=%async_computation.1 | async-start | bytes 1966080 | tf_op jit(solution)/shard_map/all_to_all | solution.py:38
  101.2 2.4 %collective-permute-start.2 = (bf16[640,640]{1,0:T(8,128)(2,1)}, bf16[640,640]{1,0:T(8,128)(2,1)}, u32[]{:S(2)}, u32[]{:S(2)}) collective-permute-start(bf16[640,640]{1,0:T(8,128)(2,1)} %param.8), channel_id=1, source_target_pairs={{0,16},{16,0},{1,17},{17,1},{2,18},{18,2},{3,19},{19,3},{4,20},{20... | collective-permute-start | bytes 2457608 | tf_op jit(solution)/shard_map/ppermute | solution.py:34
  103.7 1.9 collective-permute-start.4
  105.8 16.4 %all_gather.20 = bf16[96,640]{1,0:T(8,128)(2,1)S(1)} all-gather(bf16[48,640]{1,0:T(8,128)(2,1)S(1)} %fusion.26), channel_id=1, replica_groups=mesh['yh'=4,'x'=4,'c'=2,'z'=8,'yl'=2] {'yl'}, dimensions={0}, use_global_device_ids=true | all-gather | bytes 184320 | tf_op jit(solution)/shard_map/all_gather | solution.py:68
  122.2 3.6 %all-to-all-done.1 = bf16[16,48,640]{2,1,0:T(8,128)(2,1)S(1)} async-done(((bf16[16,48,640]{2,1,0:T(8,128)(2,1)}), bf16[16,48,640]{2,1,0:T(8,128)(2,1)S(1)}, u32[]{:S(2)}, u32[]{:S(2)}) %all-to-all-start.1) | async-done | bytes 983072 | tf_op jit(solution)/shard_map/all_to_all | solution.py:38
  126.0 26.6 %all_gather.21 = bf16[768,640]{1,0:T(8,128)(2,1)S(1)} all-gather(bf16[96,640]{1,0:T(8,128)(2,1)S(1)} %all_gather.20), channel_id=1, replica_groups=mesh['yh'=4,'x'=4,'c'=2,'z'=8,'yl'=2] {'z'}, dimensions={0}, use_global_device_ids=true | all-gather | bytes 1105920 | tf_op jit(solution)/shard_map/all_gather | solution.py:69
  154.6 5.1 %all_gather.18 = bf16[96,640]{1,0:T(8,128)(2,1)S(1)} all-gather(bf16[48,640]{1,0:T(8,128)(2,1)S(1)} %fusion.27), channel_id=1, replica_groups=mesh['yh'=4,'x'=4,'c'=2,'z'=8,'yl'=2] {'yl'}, dimensions={0}, use_global_device_ids=true | all-gather | bytes 184320 | tf_op jit(solution)/shard_map/all_gather | solution.py:68
  159.7 26.6 %all_gather.19 = bf16[768,640]{1,0:T(8,128)(2,1)S(1)} all-gather(bf16[96,640]{1,0:T(8,128)(2,1)S(1)} %all_gather.18), channel_id=1, replica_groups=mesh['yh'=4,'x'=4,'c'=2,'z'=8,'yl'=2] {'z'}, dimensions={0}, use_global_device_ids=true | all-gather | bytes 1105920 | tf_op jit(solution)/shard_map/all_gather | solution.py:69
  186.3 2.2 fusion.28
  188.5 3.2 %add_convert_fusion = bf16[768,640]{1,0:T(8,128)(2,1)} fusion(f32[768,640]{1,0:T(8,128)S(1)} %fusion.28, bf16[768,640]{1,0:T(8,128)(2,1)S(1)} %all_gather.21, bf16[640,640]{1,0:T(8,128)(2,1)} %collective-permute-done.2), kind=kOutput, calls=%fused_computation | convolution fusion | flops 630128640 | bytes 4751360 | tf_op jit(solution)/shard_map/dot_general | solution.py:21
  191.7 5.0 %all-to-all-start.3 = ((bf16[16,48,640]{2,1,0:T(8,128)(2,1)}), bf16[16,48,640]{2,1,0:T(8,128)(2,1)}, u32[]{:S(2)}, u32[]{:S(2)}) async-start(bf16[16,48,640]{2,1,0:T(8,128)(2,1)} %bitcast.3), calls=%async_computation.3 | async-start | bytes 1966080 | tf_op jit(solution)/shard_map/all_to_all | solution.py:38
  196.7 2.7 %broadcast_select_fusion = (bf16[768,640]{1,0:T(8,128)(2,1)}, bf16[768,640]{1,0:T(8,128)(2,1)}) fusion(bf16[768,640]{1,0:T(8,128)(2,1)} %collective-permute-done.4, pred[]{:T(512)S(6)} %eq.2, bf16[16,48,640]{2,1,0:T(8,128)(2,1)S(1)} %all-to-all-done), kind=kLoop, calls=%fused_computation.15 | loop fusion | flops 983040 | bytes 3932161 | tf_op jit(solution)/shard_map/jit(_where)/select_n | solution.py:86
  199.4 2.6 %fusion = f32[640,640,1]{1,0,2:T(8,128)S(1)} fusion(bf16[16,48,640]{2,1,0:T(8,128)(2,1)} %bitcast.40, bf16[16,2,48,640]{3,2,1,0:T(8,128)(2,1)} %bitcast.41), kind=kOutput, calls=%fused_computation.9 | convolution fusion | flops 629145600 | bytes 3604480 | tf_op jit(solution)/shard_map/dot_general | solution.py:28
  202.0 2.2 bitcast_add_fusion
  204.1 2.6 %fusion.1 = f32[640,640]{1,0:T(8,128)S(1)} fusion(bf16[1536,640]{1,0:T(8,128)(2,1)} %all-gather.3.cloned.1.call-done, bf16[768,640]{1,0:T(8,128)(2,1)} %collective-permute-done.3, bf16[768,640]{1,0:T(8,128)(2,1)S(1)} %all_gather.19, pred[]{:T(512)S(6)} %eq.2), kind=kOutput, calls=%fused_computation.10 | convolution fusion | flops 629637120 | bytes 4587521 | tf_op jit(solution)/shard_map/dot_general | solution.py:28
  209.5 11.7 %all-to-all-done.3 = bf16[16,48,640]{2,1,0:T(8,128)(2,1)} async-done(((bf16[16,48,640]{2,1,0:T(8,128)(2,1)}), bf16[16,48,640]{2,1,0:T(8,128)(2,1)}, u32[]{:S(2)}, u32[]{:S(2)}) %all-to-all-start.3) | async-done | bytes 983072 | tf_op jit(solution)/shard_map/all_to_all | solution.py:38
  221.2 2.0 reduce_sum.32
  (32 shorter events, 12.0 us)
Async XLA Ops:
  7.2 10.8 %copy-start.4 = (bf16[640,640]{1,0:T(8,128)(2,1)S(1)}, bf16[640,640]{1,0:T(8,128)(2,1)}, u32[]{:S(2)}) copy-start(bf16[640,640]{1,0:T(8,128)(2,1)} %param.9) | copy-start | bytes 2457604
  7.2 12.7 %copy-start = (bf16[96,640]{1,0:T(8,128)(2,1)S(1)}, bf16[96,640]{1,0:T(8,128)(2,1)}, u32[]{:S(2)}) copy-start(bf16[96,640]{1,0:T(8,128)(2,1)} %param.7) | copy-start | bytes 368644
  9.1 31.1 %all-to-all-start = ((bf16[16,48,640]{2,1,0:T(8,128)(2,1)}), bf16[16,48,640]{2,1,0:T(8,128)(2,1)S(1)}, u32[]{:S(2)}, u32[]{:S(2)}) async-start(bf16[16,48,640]{2,1,0:T(8,128)(2,1)} %broadcast_in_dim.3), calls=%async_computation | async-start | bytes 1966080 | tf_op jit(solution)/shard_map/all_to_all | solution.py:46
  17.9 181.5 %all-gather.5.cloned.1.call-start = ((), (), s32[]{:S(2)}) async-start(), calls=%async_computation.5 | async-start | bytes 2088960 | tf_op jit(solution)/shard_map/all_gather | solution.py:55
  17.9 4.2 %collective-permute-start = (bf16[640,640]{1,0:T(8,128)(2,1)S(1)}, bf16[640,640]{1,0:T(8,128)(2,1)S(1)}, u32[]{:S(2)}, u32[]{:S(2)}) collective-permute-start(bf16[640,640]{1,0:T(8,128)(2,1)S(1)} %copy-done.4), channel_id=1, source_target_pairs={{0,16},{16,0},{1,17},{17,1},{2,18},{18,2},{3,19},{19,3},{4,20},{20... | collective-permute-start | bytes 2457608 | tf_op jit(solution)/shard_map/ppermute | solution.py:34
  42.2 49.2 %all-to-all-start.2 = ((bf16[16,48,640]{2,1,0:T(8,128)(2,1)}), bf16[16,48,640]{2,1,0:T(8,128)(2,1)S(1)}, u32[]{:S(2)}, u32[]{:S(2)}) async-start(bf16[16,48,640]{2,1,0:T(8,128)(2,1)} %bitcast.2), calls=%async_computation.2 | async-start | bytes 1966080 | tf_op jit(solution)/shard_map/all_to_all | solution.py:38
  91.3 34.5 %all-to-all-start.1 = ((bf16[16,48,640]{2,1,0:T(8,128)(2,1)}), bf16[16,48,640]{2,1,0:T(8,128)(2,1)S(1)}, u32[]{:S(2)}, u32[]{:S(2)}) async-start(bf16[16,48,640]{2,1,0:T(8,128)(2,1)} %bitcast.38), calls=%async_computation.1 | async-start | bytes 1966080 | tf_op jit(solution)/shard_map/all_to_all | solution.py:38
  98.5 105.6 %all-gather.3.cloned.1.call-start = ((), (), s32[]{:S(2)}) async-start(), calls=%async_computation.4 | async-start | bytes 2027520 | tf_op jit(solution)/shard_map/all_gather | solution.py:56
  99.3 6.4 %collective-permute-start.1 = (bf16[48,640]{1,0:T(8,128)(2,1)S(1)}, bf16[48,640]{1,0:T(8,128)(2,1)S(1)}, u32[]{:S(2)}, u32[]{:S(2)}) collective-permute-start(bf16[48,640]{1,0:T(8,128)(2,1)S(1)} %broadcast_select_fusion.2), channel_id=1, source_target_pairs={{0,16},{16,0},{1,17},{17,1},{2,18},{18,2},{3,19},{19,3},{4,20},{20... | collective-permute-start | bytes 184328 | tf_op jit(solution)/shard_map/ppermute | solution.py:34
  101.2 87.2 %collective-permute-start.2 = (bf16[640,640]{1,0:T(8,128)(2,1)}, bf16[640,640]{1,0:T(8,128)(2,1)}, u32[]{:S(2)}, u32[]{:S(2)}) collective-permute-start(bf16[640,640]{1,0:T(8,128)(2,1)} %param.8), channel_id=1, source_target_pairs={{0,16},{16,0},{1,17},{17,1},{2,18},{18,2},{3,19},{19,3},{4,20},{20... | collective-permute-start | bytes 2457608 | tf_op jit(solution)/shard_map/ppermute | solution.py:34
  103.7 93.0 %collective-permute-start.4 = (bf16[768,640]{1,0:T(8,128)(2,1)S(1)}, bf16[768,640]{1,0:T(8,128)(2,1)}, u32[]{:S(2)}, u32[]{:S(2)}) collective-permute-start(bf16[768,640]{1,0:T(8,128)(2,1)S(1)} %bitcast.37), channel_id=1, source_target_pairs={{0,16},{16,0},{1,17},{17,1},{2,18},{18,2},{3,19},{19,3},{4,20},{20... | collective-permute-start | bytes 2949128 | tf_op jit(solution)/shard_map/ppermute | solution.py:34
  152.7 51.5 %collective-permute-start.3 = (bf16[768,640]{1,0:T(8,128)(2,1)S(1)}, bf16[768,640]{1,0:T(8,128)(2,1)}, u32[]{:S(2)}, u32[]{:S(2)}) collective-permute-start(bf16[768,640]{1,0:T(8,128)(2,1)S(1)} %all_gather.21), channel_id=1, source_target_pairs={{0,16},{16,0},{1,17},{17,1},{2,18},{18,2},{3,19},{19,3},{4,20},{20... | collective-permute-start | bytes 2949128 | tf_op jit(solution)/shard_map/ppermute | solution.py:34
  191.7 29.5 %all-to-all-start.3 = ((bf16[16,48,640]{2,1,0:T(8,128)(2,1)}), bf16[16,48,640]{2,1,0:T(8,128)(2,1)}, u32[]{:S(2)}, u32[]{:S(2)}) async-start(bf16[16,48,640]{2,1,0:T(8,128)(2,1)} %bitcast.3), calls=%async_computation.3 | async-start | bytes 1966080 | tf_op jit(solution)/shard_map/all_to_all | solution.py:38
  199.3 2.6 %copy-start.1 = (bf16[768,640]{1,0:T(8,128)(2,1)S(1)}, bf16[768,640]{1,0:T(8,128)(2,1)}, u32[]{:S(2)}) copy-start(bf16[768,640]{1,0:T(8,128)(2,1)} %get-tuple-element.9) | copy-start | bytes 2949124
  199.3 2.6 %copy-start.3 = (bf16[1536,640]{1,0:T(8,128)(2,1)S(1)}, bf16[1536,640]{1,0:T(8,128)(2,1)}, u32[]{:S(2)}) copy-start(bf16[1536,640]{1,0:T(8,128)(2,1)} %all-gather.5.cloned.1.call-done) | copy-start | bytes 5898244
  204.1 2.6 %copy-start.2 = (bf16[1536,640]{1,0:T(8,128)(2,1)S(1)}, bf16[1536,640]{1,0:T(8,128)(2,1)}, u32[]{:S(2)}) copy-start(bf16[1536,640]{1,0:T(8,128)(2,1)} %all-gather.3.cloned.1.call-done) | copy-start | bytes 5898244
Sparse Core Ops, SparseCore 0:
  20.8 100.5 all-gather.4
  124.5 56.6 all-gather.2

commit v2 on v0

v2 whole, which is shorter than its diff:
```python
import math

import jax
import jax.numpy as jnp
from jax import lax
from jax.sharding import Mesh, PartitionSpec as P

WIDE = ("yh", "x", "c")
NARROW = ("z", "yl")
BF16 = jnp.bfloat16
F32 = jnp.float32


def gelu_parts(pre_values):
    values = pre_values.astype(F32)
    normal_cdf = 0.5 * (1.0 + jax.scipy.special.erf(values / math.sqrt(2.0)))
    normal_pdf = jnp.exp(-0.5 * values * values) / math.sqrt(2.0 * math.pi)
    return (values * normal_cdf, normal_cdf + values * normal_pdf)


def times_transposed(left, right):
    return lax.dot_general(
        left, right, (((1,), (1,)), ((), ())), preferred_element_type=F32
    )


def over_tokens(left, right):
    return lax.dot_general(
        left, right, (((0,), (0,)), ((), ())), preferred_element_type=F32
    )


def swap(values, axis):
    return lax.ppermute(values, axis, [(0, 1), (1, 0)])


def in_order(index, own, other):
    return (jnp.where(index == 0, own, other), jnp.where(index == 0, other, own))


def per_device(layer_input, output_grad, pre_activation, w_up, w_down):
    core, lane = lax.axis_index("c"), lax.axis_index("yl")
    rows, width = layer_input.shape
    half = rows // 2
    hidden = pre_activation.shape[1]

    down_lane = swap(w_down, "yl")
    down_core = swap(w_down, "c")
    pre_lane = swap(pre_activation, "yl")

    pieces = jnp.broadcast_to(output_grad.reshape(2, half, width), (4, 2, half, width))
    grad_y = lax.all_to_all(pieces.reshape(8, half, width), ("yh", "yl"), 0, 0)
    grad_xy = lax.all_to_all(
        jnp.broadcast_to(grad_y, (4, 8, half, width)), "x", 0, 0
    ).reshape(4, 4, 2, half, width)
    grad_xy = jnp.swapaxes(grad_xy, 0, 1)
    grad_own, grad_pair = in_order(lane, grad_xy[:, :, 0], grad_xy[:, :, 1])
    down_both = swap(down_lane, "c")

    pre_both = jnp.stack(in_order(lane, pre_activation, pre_lane))
    pre_cut = pre_both.reshape(2, 2, 2, half, hidden)
    pre_half = jnp.where(lane == 0, pre_cut[:, :, 0], pre_cut[:, :, 1])
    pre_own = jnp.where(core == 0, pre_half[:, 0], pre_half[:, 1])
    pre_sent = jnp.where(core == 0, pre_half[:, 1], pre_half[:, 0])
    pre_pair = swap(pre_sent, "c")
    pre_tile = jnp.concatenate([pre_own, pre_pair], axis=-1).reshape(rows, 2 * hidden)
    slope_factor = gelu_parts(pre_tile)[1]
    act_tile = gelu_parts(pre_both)[0].astype(BF16).reshape(-1, hidden)
    act_all = lax.all_gather(act_tile, "z", axis=0, tiled=True)
    input_all = lax.all_gather(layer_input, WIDE, axis=0, tiled=True)

    up_lane = swap(w_up, "yl")
    up_core = swap(w_up, "c")

    grad_rows = jnp.concatenate([grad_own, grad_pair], axis=-1).reshape(-1, 2 * width)
    down_cat = jnp.concatenate(
        [
            jnp.concatenate([w_down, down_lane], axis=1),
            jnp.concatenate([down_core, down_both], axis=1),
        ],
        axis=0,
    )
    part = times_transposed(grad_rows, down_cat).astype(BF16)
    blocks = lax.all_to_all(part.reshape(8, rows, 2 * hidden), "z", 0, 0)
    act_grad = jnp.sum(blocks.astype(F32), axis=0)
    slope_tile = (act_grad * slope_factor).astype(BF16)
    slopes = lax.all_gather(slope_tile, "z", axis=0, tiled=True)
    up_both = swap(up_lane, "c")
    up_cat = jnp.concatenate(
        [
            jnp.concatenate([w_up, up_core], axis=1),
            jnp.concatenate([up_lane, up_both], axis=1),
        ],
        axis=0,
    )

    grad_lane = swap(grad_pair, "yl")
    shards = grad_own.shape[0] * grad_own.shape[1]
    grad_core = jnp.stack(in_order(lane, grad_own, grad_lane), axis=2)
    grad_other = swap(grad_core, "c")
    grad_all = jnp.stack(in_order(core, grad_core, grad_other), axis=2)
    down_grad = over_tokens(act_all, grad_all.reshape(-1, width))

    part_in = times_transposed(slopes, up_cat).astype(BF16)
    part_in = jnp.swapaxes(part_in.reshape(4, 4, half, 2 * width), 0, 1)
    blocks = lax.all_to_all(part_in, "x", 0, 0)
    part_y = jnp.sum(blocks.astype(F32), axis=0).astype(BF16)
    part_y = jnp.stack(
        in_order(lane, part_y[..., :width], part_y[..., width:]), axis=1
    )
    blocks = lax.all_to_all(part_y.reshape(8, half, width), ("yh", "yl"), 0, 0)
    input_grad = (
        jnp.sum(blocks.reshape(4, rows, width).astype(F32), axis=0)
    ).astype(BF16)

    slopes_lane = swap(slopes, "yl")
    by_shard = [
        jnp.stack(
            in_order(
                lane,
                slopes[:, cut].reshape(shards, half, hidden),
                slopes_lane[:, cut].reshape(shards, half, hidden),
            ),
            axis=1,
        )
        for cut in (slice(0, hidden), slice(hidden, 2 * hidden))
    ]
    slopes_other = swap(by_shard[1], "c")
    slopes_all = jnp.stack(in_order(core, by_shard[0], slopes_other), axis=1)
    up_grad = over_tokens(input_all, slopes_all.reshape(-1, hidden))
    return (input_grad, up_grad, down_grad)


def solution(mesh):
    fine = Mesh(mesh.devices.reshape(4, 4, 2, 8, 2), WIDE + NARROW)
    tokens = P(WIDE, NARROW)
    hidden = P(NARROW, WIDE)
    return jax.shard_map(
        per_device,
        mesh=fine,
        in_specs=(tokens, tokens, hidden, hidden, tokens),
        out_specs=(tokens, hidden, tokens),
        check_vma=False,
    )
```

time: 488 us -> 204 us (0.42)
  waiting for transfers between devices: 451 us -> 48.4 us
  starting transfers between devices: 0.24 us -> 80.9 us
  blocking collectives: 0 us -> 23 us
  other arithmetic: 1.72 us -> 12.8 us
  local copies, waits for them, and re-layouts: 1.71 us -> 6.6 us
    all_gather x4 -> x2, waiting for transfers between devices: 277 us -> 0.04 us  [the longest x1 0.02 us: per_device(): input_all = lax.all_gather(layer_input, WIDE, axis=0, tiled=True)]
    reduce_scatter x2 -> x0, waiting for transfers between devices: 172 us -> none  [the longest x1 106 us: per_device(): lax.psum_scatter(times_transposed(row_block, w_up).astype(jnp.bfloat16),...]
    ppermute x0 -> x12, starting transfers between devices: none -> 47.5 us  [swap(): return lax.ppermute(values, axis, [(0, 1), (1, 0)])]
    all_to_all x0 -> x5, starting transfers between devices: none -> 33.3 us  [the longest x1 10.2 us: per_device(): blocks = lax.all_to_all(part.reshape(8, rows, 2 * hidden), 'z', 0, 0)]
    ppermute x0 -> x12, waiting for transfers between devices: none -> 28.8 us  [swap(): return lax.ppermute(values, axis, [(0, 1), (1, 0)])]
    all_gather x0 -> x1, blocking collectives: none -> 23 us  [per_device(): slopes = lax.all_gather(slope_tile, 'z', axis=0, tiled=True)]
    all_to_all x0 -> x5, waiting for transfers between devices: none -> 19.5 us  [the longest x1 7.04 us: per_device(): blocks = lax.all_to_all(part_y.reshape(8, half, width), ('yh', 'yl'), 0, 0)]
    another operation x0 -> x11, other arithmetic: none -> 7.57 us  [the longest x2 2.91 us: per_device(): grad_all = jnp.stack(in_order(core, grad_core, grad_other), axis=2)]
  transfers between devices with their start and end apart: 6 -> 19, of which waited for: 6 -> 9; matrix products, arithmetic and copies ran while one was open for 3% -> 13% of each run, Pallas kernels for 0% -> 0%
where the time goes in v2:
time: 204 us; the launch traced here: 203 us
  starting transfers between devices  80.9 us (40%)
  waiting for transfers between devices  48.4 us (24%)
  blocking collectives  23 us (11%)
  matrix products  16.5 us (8%)
  between operations  14.4 us (7%)
  other arithmetic  12.8 us (6%)
  local copies, waits for them, and re-layouts  6.6 us (3%)
    ppermute x12, starting transfers between devices, swap(): return lax.ppermute(values, axis, [(0, 1), (1, 0)])  47.5 us
    ppermute x12, waiting for transfers between devices, swap(): return lax.ppermute(values, axis, [(0, 1), (1, 0)])  28.8 us
    all_gather x1, blocking collectives, per_device(): slopes = lax.all_gather(slope_tile, 'z', axis=0, tiled=True)  23 us
    all_to_all x1, starting transfers between devices, per_device(): blocks = lax.all_to_all(part.reshape(8, rows, 2 * hidden), 'z', 0, 0)  10.2 us
    dot_general x2, matrix products, over_tokens(): lax.dot_general(left, right, (((0,), (0,)), ((), ())), preferred_element_...  8.99 us
    dot_general x2, matrix products, times_transposed(): lax.dot_general(left, right, (((1,), (1,)), ((), ())), preferred_element_...  7.52 us
    all_to_all x1, starting transfers between devices, per_device(): grad_y = lax.all_to_all(pieces.reshape(8, half, width), ('yh', 'yl'), 0, 0)  7.44 us
    all_to_all x1, waiting for transfers between devices, per_device(): blocks = lax.all_to_all(part_y.reshape(8, half, width), ('yh', 'yl'), 0, 0)  7.04 us
  transfers between devices with their start and end apart: 19, of which 9 were waited for; matrix products, arithmetic and copies ran while one was open for 13% of the time, Pallas kernels for 0%

profile of v2, /device:TPU:1, one launch (start us, length us, event | category | flops | bytes accessed | tf_op | source)
XLA Modules:
  0.0 202.6 jit_solution(8056855557108263510)
XLA Ops:
  7.2 4.2 %collective-permute-start.3 = (bf16[96,640]{1,0:T(8,128)(2,1)}, bf16[96,640]{1,0:T(8,128)(2,1)S(1)}, u32[]{:S(2)}, u32[]{:S(2)}) collective-permute-start(bf16[96,640]{1,0:T(8,128)(2,1)} %param.7), channel_id=1, source_target_pairs={{0,1},{1,0},{2,3},{3,2},{4,5},{5,4},{6,7},{7,6},{8,9},{9,8},{10,11... | collective-permute-start | bytes 368648 | tf_op jit(solution)/shard_map/ppermute | solution.py:34
  17.2 7.4 %all-to-all-start = ((bf16[8,24,640]{2,1,0:T(8,128)(2,1)}), bf16[8,24,640]{2,1,0:T(8,128)(2,1)S(1)}, u32[]{:S(2)}, u32[]{:S(2)}) async-start(bf16[8,24,640]{2,1,0:T(8,128)(2,1)} %bitcast.1), calls=%async_computation | async-start | bytes 491520 | tf_op jit(solution)/shard_map/all_to_all | solution.py:52
  24.7 3.4 %collective-permute-start = (bf16[640,640]{1,0:T(8,128)(2,1)S(1)}, bf16[640,640]{1,0:T(8,128)(2,1)}, u32[]{:S(2)}, u32[]{:S(2)}) collective-permute-start(bf16[640,640]{1,0:T(8,128)(2,1)S(1)} %copy-done.3), channel_id=1, source_target_pairs={{0,1},{1,0},{2,3},{3,2},{4,5},{5,4},{6,7},{7,6},{8,9},{9,8},{10,11... | collective-permute-start | bytes 2457608 | tf_op jit(solution)/shard_map/ppermute | solution.py:34
  28.0 5.8 %all-to-all-done = bf16[8,24,640]{2,1,0:T(8,128)(2,1)S(1)} async-done(((bf16[8,24,640]{2,1,0:T(8,128)(2,1)}), bf16[8,24,640]{2,1,0:T(8,128)(2,1)S(1)}, u32[]{:S(2)}, u32[]{:S(2)}) %all-to-all-start) | async-done | bytes 245792 | tf_op jit(solution)/shard_map/all_to_all | solution.py:52
  34.9 3.9 %all-to-all-start.1 = ((bf16[4,8,24,640]{3,2,1,0:T(8,128)(2,1)}), bf16[4,8,24,640]{3,2,1,0:T(8,128)(2,1)S(1)}, u32[]{:S(2)}, u32[]{:S(2)}) async-start(bf16[4,8,24,640]{3,2,1,0:T(8,128)(2,1)} %broadcast_in_dim.7), calls=%async_computation.1 | async-start | bytes 1966080 | tf_op jit(solution)/shard_map/all_to_all | solution.py:53
  38.7 7.3 %collective-permute-start.1 = (bf16[640,640]{1,0:T(8,128)(2,1)S(1)}, bf16[640,640]{1,0:T(8,128)(2,1)}, u32[]{:S(2)}, u32[]{:S(2)}) collective-permute-start(bf16[640,640]{1,0:T(8,128)(2,1)S(1)} %copy-done.3), channel_id=1, source_target_pairs={{0,16},{16,0},{1,17},{17,1},{2,18},{18,2},{3,19},{19,3},{4,20},{20... | collective-permute-start | bytes 2457608 | tf_op jit(solution)/shard_map/ppermute | solution.py:34
  48.1 4.7 %collective-permute-start.2 = (bf16[640,640]{1,0:T(8,128)(2,1)}, bf16[640,640]{1,0:T(8,128)(2,1)}, u32[]{:S(2)}, u32[]{:S(2)}) collective-permute-start(bf16[640,640]{1,0:T(8,128)(2,1)} %collective-permute-done), channel_id=1, source_target_pairs={{0,16},{16,0},{1,17},{17,1},{2,18},{18,2},{3,19},{19,3},{4,20},{20... | collective-permute-start | bytes 2457608 | tf_op jit(solution)/shard_map/ppermute | solution.py:34
  56.1 9.7 %collective-permute-done.10 = bf16[4,4,24,640]{3,2,0,1:T(8,128)(2,1)S(1)} collective-permute-done((bf16[4,4,24,640]{3,2,0,1:T(8,128)(2,1)S(1)}, bf16[4,4,24,640]{3,2,0,1:T(8,128)(2,1)S(1)}, u32[]{:S(2)}, u32[]{:S(2)}) %collective-permute-start.10) | collective-permute-done | bytes 491552 | tf_op jit(solution)/shard_map/ppermute | solution.py:34
  66.0 4.1 %fusion.19 = bf16[384,1280]{1,0:T(8,128)(2,1)} fusion(bf16[640,640]{1,0:T(8,128)(2,1)} %collective-permute-done.2, bf16[640,640]{1,0:T(8,128)(2,1)} %collective-permute-done.1, bf16[640,640]{1,0:T(8,128)(2,1)} %collective-permute-done, bf16[640,640]{1,0:T(8,128)(2,1)S(1)} %copy-done.3, bf16[384,640]{1,0:T(8,128)(2,1)S(1)} %bitcast.114, ...), kind=kOutput, calls=%fused_computation.17 | convolution fusion | flops 1273856000 | bytes 5242880 | tf_op jit(solution)/shard_map/dot_general | solution.py:22
  70.0 10.2 %all-to-all-start.2 = ((bf16[8,48,1280]{2,1,0:T(8,128)(2,1)}), bf16[8,48,1280]{2,1,0:T(8,128)(2,1)S(1)}, u32[]{:S(2)}, u32[]{:S(2)}) async-start(bf16[8,48,1280]{2,1,0:T(8,128)(2,1)} %bitcast.111), calls=%async_computation.2 | async-start | bytes 1966080 | tf_op jit(solution)/shard_map/all_to_all | solution.py:84
  80.3 3.3 %collective-permute-start.6 = (bf16[640,640]{1,0:T(8,128)(2,1)}, bf16[640,640]{1,0:T(8,128)(2,1)}, u32[]{:S(2)}, u32[]{:S(2)}) collective-permute-start(bf16[640,640]{1,0:T(8,128)(2,1)} %param.8), channel_id=1, source_target_pairs={{0,1},{1,0},{2,3},{3,2},{4,5},{5,4},{6,7},{7,6},{8,9},{9,8},{10,11... | collective-permute-start | bytes 2457608 | tf_op jit(solution)/shard_map/ppermute | solution.py:34
  83.6 4.2 %collective-permute-start.5 = (bf16[640,640]{1,0:T(8,128)(2,1)}, bf16[640,640]{1,0:T(8,128)(2,1)}, u32[]{:S(2)}, u32[]{:S(2)}) collective-permute-start(bf16[640,640]{1,0:T(8,128)(2,1)} %param.8), channel_id=1, source_target_pairs={{0,16},{16,0},{1,17},{17,1},{2,18},{18,2},{3,19},{19,3},{4,20},{20... | collective-permute-start | bytes 2457608 | tf_op jit(solution)/shard_map/ppermute | solution.py:34
  91.1 8.4 %collective-permute-done.6 = bf16[640,640]{1,0:T(8,128)(2,1)} collective-permute-done((bf16[640,640]{1,0:T(8,128)(2,1)}, bf16[640,640]{1,0:T(8,128)(2,1)}, u32[]{:S(2)}, u32[]{:S(2)}) %collective-permute-start.6) | collective-permute-done | bytes 819232 | tf_op jit(solution)/shard_map/ppermute | solution.py:34
  99.5 5.6 %collective-permute-start.7 = (bf16[640,640]{1,0:T(8,128)(2,1)}, bf16[640,640]{1,0:T(8,128)(2,1)}, u32[]{:S(2)}, u32[]{:S(2)}) collective-permute-start(bf16[640,640]{1,0:T(8,128)(2,1)} %collective-permute-done.6), channel_id=1, source_target_pairs={{0,16},{16,0},{1,17},{17,1},{2,18},{18,2},{3,19},{19,3},{4,20},{20... | collective-permute-start | bytes 2457608 | tf_op jit(solution)/shard_map/ppermute | solution.py:34
  108.4 23.0 %all_gather.9 = bf16[384,1280]{1,0:T(8,128)(2,1)S(1)} all-gather(bf16[48,1280]{1,0:T(8,128)(2,1)S(1)} %fusion.38), channel_id=1, replica_groups=mesh['yh'=4,'x'=4,'c'=2,'z'=8,'yl'=2] {'z'}, dimensions={0}, use_global_device_ids=true | all-gather | bytes 1105920 | tf_op jit(solution)/shard_map/all_gather | solution.py:87
  134.3 3.5 %fusion.16 = bf16[384,1280]{1,0:T(8,128)(2,1)S(1)} fusion(bf16[384,1280]{1,0:T(8,128)(2,1)S(1)} %all_gather.9, bf16[640,640]{1,0:T(8,128)(2,1)} %collective-permute-done.7, bf16[640,640]{1,0:T(8,128)(2,1)} %collective-permute-done.6, bf16[640,640]{1,0:T(8,128)(2,1)} %collective-permute-done.5, bf16[640,640]{1,0:T(8,128)(2,1)} %param.8), kind=kOutput, calls=%fused_computation.16 | convolution fusion | flops 1271889920 | bytes 5242880 | tf_op jit(solution)/shard_map/dot_general | solution.py:22
  138.7 6.0 %all-to-all-start.3 = ((bf16[4,4,24,1280]{3,2,1,0:T(8,128)(2,1)}), bf16[4,4,24,1280]{3,2,1,0:T(8,128)(2,1)S(1)}, u32[]{:S(2)}, u32[]{:S(2)}) async-start(bf16[4,4,24,1280]{3,2,1,0:T(8,128)(2,1)} %bitcast.96), calls=%async_computation.3 | async-start | bytes 1966080 | tf_op jit(solution)/shard_map/all_to_all | solution.py:106
  147.5 6.7 %all-to-all-done.3 = bf16[4,4,24,1280]{3,2,1,0:T(8,128)(2,1)S(1)} async-done(((bf16[4,4,24,1280]{3,2,1,0:T(8,128)(2,1)}), bf16[4,4,24,1280]{3,2,1,0:T(8,128)(2,1)S(1)}, u32[]{:S(2)}, u32[]{:S(2)}) %all-to-all-start.3) | async-done | bytes 983072 | tf_op jit(solution)/shard_map/all_to_all | solution.py:106
  154.3 5.1 %collective-permute-done.8 = bf16[384,1280]{1,0:T(8,128)(2,1)} collective-permute-done((bf16[384,1280]{1,0:T(8,128)(2,1)S(1)}, bf16[384,1280]{1,0:T(8,128)(2,1)}, u32[]{:S(2)}, u32[]{:S(2)}) %collective-permute-start.8) | collective-permute-done | bytes 983072 | tf_op jit(solution)/shard_map/ppermute | solution.py:34
  162.6 5.1 %collective-permute-start.9 = (bf16[16,2,24,640]{3,2,1,0:T(8,128)(2,1)}, bf16[16,2,24,640]{3,2,1,0:T(8,128)(2,1)}, u32[]{:S(2)}, u32[]{:S(2)}) collective-permute-start(bf16[16,2,24,640]{3,2,1,0:T(8,128)(2,1)} %pad_maximum_fusion.3), channel_id=1, source_target_pairs={{0,16},{16,0},{1,17},{17,1},{2,18},{18,2},{3,19},{19,3},{4,20},{20... | collective-permute-start | bytes 2949128 | tf_op jit(solution)/shard_map/ppermute | solution.py:34
  168.4 5.8 %all-to-all-start.4 = ((bf16[8,24,640]{2,1,0:T(8,128)(2,1)}), bf16[8,24,640]{2,1,0:T(8,128)(2,1)S(1)}, u32[]{:S(2)}, u32[]{:S(2)}) async-start(bf16[8,24,640]{2,1,0:T(8,128)(2,1)} %bitcast.26), calls=%async_computation.4 | async-start | bytes 491520 | tf_op jit(solution)/shard_map/all_to_all | solution.py:111
  174.7 4.5 %fusion.46 = f32[640,640]{1,0:T(8,128)} fusion(bf16[1536,640]{1,0:T(8,128)(2,1)} %all-gather.5.cloned.1.call-done, bf16[1536,640]{1,0:T(8,128)(2,1)S(1)} %bitcast.101), kind=kOutput, calls=%fused_computation.81 | convolution fusion | flops 1258291200 | bytes 5570560 | tf_op jit(solution)/shard_map/dot_general | solution.py:28
  179.2 7.0 %all-to-all-done.4 = bf16[8,24,640]{2,1,0:T(8,128)(2,1)S(1)} async-done(((bf16[8,24,640]{2,1,0:T(8,128)(2,1)}), bf16[8,24,640]{2,1,0:T(8,128)(2,1)S(1)}, u32[]{:S(2)}, u32[]{:S(2)}) %all-to-all-start.4) | async-done | bytes 245792 | tf_op jit(solution)/shard_map/all_to_all | solution.py:111
  188.5 4.5 %convolution_bitcast_fusion = f32[640,640]{0,1:T(8,128)} fusion(bf16[1536,640]{1,0:T(8,128)(2,1)S(1)} %bitcast.102, bf16[1536,640]{1,0:T(8,128)(2,1)} %all-gather.3.cloned.1.call-done), kind=kOutput, calls=%fused_computation.21 | convolution fusion | flops 1258291200 | bytes 5570560 | tf_op jit(solution)/shard_map/dot_general | solution.py:28
  (60 shorter events, 34.9 us)
Async XLA Ops:
  7.2 17.5 %copy-start.3 = (bf16[640,640]{1,0:T(8,128)(2,1)S(1)}, bf16[640,640]{1,0:T(8,128)(2,1)}, u32[]{:S(2)}) copy-start(bf16[640,640]{1,0:T(8,128)(2,1)} %param.9) | copy-start | bytes 2457604
  7.2 167.5 %all-gather.5.cloned.1.call-start = ((), (), s32[]{:S(2)}) async-start(), calls=%async_computation.6 | async-start | bytes 2211840 | tf_op jit(solution)/shard_map/all_gather | solution.py:69
  7.2 6.6 %collective-permute-start.3 = (bf16[96,640]{1,0:T(8,128)(2,1)}, bf16[96,640]{1,0:T(8,128)(2,1)S(1)}, u32[]{:S(2)}, u32[]{:S(2)}) collective-permute-start(bf16[96,640]{1,0:T(8,128)(2,1)} %param.7), channel_id=1, source_target_pairs={{0,1},{1,0},{2,3},{3,2},{4,5},{5,4},{6,7},{7,6},{8,9},{9,8},{10,11... | collective-permute-start | bytes 368648 | tf_op jit(solution)/shard_map/ppermute | solution.py:34
  17.2 16.6 %all-to-all-start = ((bf16[8,24,640]{2,1,0:T(8,128)(2,1)}), bf16[8,24,640]{2,1,0:T(8,128)(2,1)S(1)}, u32[]{:S(2)}, u32[]{:S(2)}) async-start(bf16[8,24,640]{2,1,0:T(8,128)(2,1)} %bitcast.1), calls=%async_computation | async-start | bytes 491520 | tf_op jit(solution)/shard_map/all_to_all | solution.py:52
  24.7 23.4 %collective-permute-start = (bf16[640,640]{1,0:T(8,128)(2,1)S(1)}, bf16[640,640]{1,0:T(8,128)(2,1)}, u32[]{:S(2)}, u32[]{:S(2)}) collective-permute-start(bf16[640,640]{1,0:T(8,128)(2,1)S(1)} %copy-done.3), channel_id=1, source_target_pairs={{0,1},{1,0},{2,3},{3,2},{4,5},{5,4},{6,7},{7,6},{8,9},{9,8},{10,11... | collective-permute-start | bytes 2457608 | tf_op jit(solution)/shard_map/ppermute | solution.py:34
  34.9 18.0 %all-to-all-start.1 = ((bf16[4,8,24,640]{3,2,1,0:T(8,128)(2,1)}), bf16[4,8,24,640]{3,2,1,0:T(8,128)(2,1)S(1)}, u32[]{:S(2)}, u32[]{:S(2)}) async-start(bf16[4,8,24,640]{3,2,1,0:T(8,128)(2,1)} %broadcast_in_dim.7), calls=%async_computation.1 | async-start | bytes 1966080 | tf_op jit(solution)/shard_map/all_to_all | solution.py:53
  38.7 27.2 %collective-permute-start.1 = (bf16[640,640]{1,0:T(8,128)(2,1)S(1)}, bf16[640,640]{1,0:T(8,128)(2,1)}, u32[]{:S(2)}, u32[]{:S(2)}) collective-permute-start(bf16[640,640]{1,0:T(8,128)(2,1)S(1)} %copy-done.3), channel_id=1, source_target_pairs={{0,16},{16,0},{1,17},{17,1},{2,18},{18,2},{3,19},{19,3},{4,20},{20... | collective-permute-start | bytes 2457608 | tf_op jit(solution)/shard_map/ppermute | solution.py:34
  48.1 17.9 %collective-permute-start.2 = (bf16[640,640]{1,0:T(8,128)(2,1)}, bf16[640,640]{1,0:T(8,128)(2,1)}, u32[]{:S(2)}, u32[]{:S(2)}) collective-permute-start(bf16[640,640]{1,0:T(8,128)(2,1)} %collective-permute-done), channel_id=1, source_target_pairs={{0,16},{16,0},{1,17},{17,1},{2,18},{18,2},{3,19},{19,3},{4,20},{20... | collective-permute-start | bytes 2457608 | tf_op jit(solution)/shard_map/ppermute | solution.py:34
  52.9 12.9 %collective-permute-start.10 = (bf16[4,4,24,640]{3,2,0,1:T(8,128)(2,1)S(1)}, bf16[4,4,24,640]{3,2,0,1:T(8,128)(2,1)S(1)}, u32[]{:S(2)}, u32[]{:S(2)}) collective-permute-start(bf16[4,4,24,640]{3,2,0,1:T(8,128)(2,1)S(1)} %fusion.52), channel_id=1, source_target_pairs={{0,1},{1,0},{2,3},{3,2},{4,5},{5,4},{6,7},{7,6},{8,9},{9,8},{10,11... | collective-permute-start | bytes 1474568 | tf_op jit(solution)/shard_map/ppermute | solution.py:34
  70.0 38.1 %all-to-all-start.2 = ((bf16[8,48,1280]{2,1,0:T(8,128)(2,1)}), bf16[8,48,1280]{2,1,0:T(8,128)(2,1)S(1)}, u32[]{:S(2)}, u32[]{:S(2)}) async-start(bf16[8,48,1280]{2,1,0:T(8,128)(2,1)} %bitcast.111), calls=%async_computation.2 | async-start | bytes 1966080 | tf_op jit(solution)/shard_map/all_to_all | solution.py:84
  80.2 108.3 %all-gather.3.cloned.1.call-start = ((), (), s32[]{:S(2)}) async-start(), calls=%async_computation.5 | async-start | bytes 2027520 | tf_op jit(solution)/shard_map/all_gather | solution.py:70
  80.3 19.2 %collective-permute-start.6 = (bf16[640,640]{1,0:T(8,128)(2,1)}, bf16[640,640]{1,0:T(8,128)(2,1)}, u32[]{:S(2)}, u32[]{:S(2)}) collective-permute-start(bf16[640,640]{1,0:T(8,128)(2,1)} %param.8), channel_id=1, source_target_pairs={{0,1},{1,0},{2,3},{3,2},{4,5},{5,4},{6,7},{7,6},{8,9},{9,8},{10,11... | collective-permute-start | bytes 2457608 | tf_op jit(solution)/shard_map/ppermute | solution.py:34
  83.6 50.6 %collective-permute-start.5 = (bf16[640,640]{1,0:T(8,128)(2,1)}, bf16[640,640]{1,0:T(8,128)(2,1)}, u32[]{:S(2)}, u32[]{:S(2)}) collective-permute-start(bf16[640,640]{1,0:T(8,128)(2,1)} %param.8), channel_id=1, source_target_pairs={{0,16},{16,0},{1,17},{17,1},{2,18},{18,2},{3,19},{19,3},{4,20},{20... | collective-permute-start | bytes 2457608 | tf_op jit(solution)/shard_map/ppermute | solution.py:34
  87.9 3.1 %collective-permute-start.4 = (bf16[2,24,640]{2,1,0:T(8,128)(2,1)S(1)}, bf16[2,24,640]{2,1,0:T(8,128)(2,1)S(1)}, u32[]{:S(2)}, u32[]{:S(2)}) collective-permute-start(bf16[2,24,640]{2,1,0:T(8,128)(2,1)S(1)} %fusion.42), channel_id=1, source_target_pairs={{0,16},{16,0},{1,17},{17,1},{2,18},{18,2},{3,19},{19,3},{4,20},{20... | collective-permute-start | bytes 184328 | tf_op jit(solution)/shard_map/ppermute | solution.py:34
  99.5 34.8 %collective-permute-start.7 = (bf16[640,640]{1,0:T(8,128)(2,1)}, bf16[640,640]{1,0:T(8,128)(2,1)}, u32[]{:S(2)}, u32[]{:S(2)}) collective-permute-start(bf16[640,640]{1,0:T(8,128)(2,1)} %collective-permute-done.6), channel_id=1, source_target_pairs={{0,16},{16,0},{1,17},{17,1},{2,18},{18,2},{3,19},{19,3},{4,20},{20... | collective-permute-start | bytes 2457608 | tf_op jit(solution)/shard_map/ppermute | solution.py:34
  106.2 38.6 %collective-permute-start.11 = (bf16[4,4,2,24,640]{4,3,0,1,2:T(8,128)(2,1)}, bf16[4,4,2,24,640]{4,3,0,1,2:T(8,128)(2,1)}, u32[]{:S(2)}, u32[]{:S(2)}) collective-permute-start(bf16[4,4,2,24,640]{4,3,0,1,2:T(8,128)(2,1)} %pad_maximum_fusion.4), channel_id=1, source_target_pairs={{0,16},{16,0},{1,17},{17,1},{2,18},{18,2},{3,19},{19,3},{4,20},{20... | collective-permute-start | bytes 2949128 | tf_op jit(solution)/shard_map/ppermute | solution.py:34
  131.4 28.0 %collective-permute-start.8 = (bf16[384,1280]{1,0:T(8,128)(2,1)S(1)}, bf16[384,1280]{1,0:T(8,128)(2,1)}, u32[]{:S(2)}, u32[]{:S(2)}) collective-permute-start(bf16[384,1280]{1,0:T(8,128)(2,1)S(1)} %all_gather.9), channel_id=1, source_target_pairs={{0,1},{1,0},{2,3},{3,2},{4,5},{5,4},{6,7},{7,6},{8,9},{9,8},{10,11... | collective-permute-start | bytes 2949128 | tf_op jit(solution)/shard_map/ppermute | solution.py:34
  138.7 15.4 %all-to-all-start.3 = ((bf16[4,4,24,1280]{3,2,1,0:T(8,128)(2,1)}), bf16[4,4,24,1280]{3,2,1,0:T(8,128)(2,1)S(1)}, u32[]{:S(2)}, u32[]{:S(2)}) async-start(bf16[4,4,24,1280]{3,2,1,0:T(8,128)(2,1)} %bitcast.96), calls=%async_computation.3 | async-start | bytes 1966080 | tf_op jit(solution)/shard_map/all_to_all | solution.py:106
  161.5 12.7 %copy-start = (bf16[4,4,1,2,24,640]{5,4,0,1,3,2:T(8,128)(2,1)S(1)}, bf16[4,4,1,2,24,640]{5,4,0,1,3,2:T(8,128)(2,1)}, u32[]{:S(2)}) copy-start(bf16[4,4,1,2,24,640]{5,4,0,1,3,2:T(8,128)(2,1)} %get-tuple-element.17) | copy-start | bytes 2949124
  161.5 12.7 %copy-start.1 = (bf16[4,4,1,2,24,640]{5,4,0,1,3,2:T(8,128)(2,1)S(1)}, bf16[4,4,1,2,24,640]{5,4,0,1,3,2:T(8,128)(2,1)}, u32[]{:S(2)}) copy-start(bf16[4,4,1,2,24,640]{5,4,0,1,3,2:T(8,128)(2,1)} %get-tuple-element.18) | copy-start | bytes 2949124
  162.6 24.3 %collective-permute-start.9 = (bf16[16,2,24,640]{3,2,1,0:T(8,128)(2,1)}, bf16[16,2,24,640]{3,2,1,0:T(8,128)(2,1)}, u32[]{:S(2)}, u32[]{:S(2)}) collective-permute-start(bf16[16,2,24,640]{3,2,1,0:T(8,128)(2,1)} %pad_maximum_fusion.3), channel_id=1, source_target_pairs={{0,16},{16,0},{1,17},{17,1},{2,18},{18,2},{3,19},{19,3},{4,20},{20... | collective-permute-start | bytes 2949128 | tf_op jit(solution)/shard_map/ppermute | solution.py:34
  168.4 17.8 %all-to-all-start.4 = ((bf16[8,24,640]{2,1,0:T(8,128)(2,1)}), bf16[8,24,640]{2,1,0:T(8,128)(2,1)S(1)}, u32[]{:S(2)}, u32[]{:S(2)}) async-start(bf16[8,24,640]{2,1,0:T(8,128)(2,1)} %bitcast.26), calls=%async_computation.4 | async-start | bytes 491520 | tf_op jit(solution)/shard_map/all_to_all | solution.py:111
  174.6 12.2 %copy-start.2 = (bf16[384,640]{1,0:T(8,128)(2,1)S(1)}, bf16[384,640]{1,0:T(8,128)(2,1)}, u32[]{:S(2)}) copy-start(bf16[384,640]{1,0:T(8,128)(2,1)} %get-tuple-element.22) | copy-start | bytes 1474564
Sparse Core Ops, SparseCore 0:
  15.8 46.3 all-gather.4
  88.0 60.1 all-gather.2

commit v3 on v2

v3 whole, which is shorter than its diff:
```python
import math

import jax
import jax.numpy as jnp
from jax import lax
from jax.sharding import Mesh, PartitionSpec as P

WIDE = ("yh", "x", "c")
NARROW = ("z", "yl")
BF16 = jnp.bfloat16
F32 = jnp.float32


def gelu_parts(pre_values):
    values = pre_values.astype(F32)
    normal_cdf = 0.5 * (1.0 + jax.scipy.special.erf(values / math.sqrt(2.0)))
    normal_pdf = jnp.exp(-0.5 * values * values) / math.sqrt(2.0 * math.pi)
    return (values * normal_cdf, normal_cdf + values * normal_pdf)


def times_transposed(left, right):
    return lax.dot_general(
        left, right, (((1,), (1,)), ((), ())), preferred_element_type=F32
    )


def over_tokens(left, right):
    return lax.dot_general(
        left, right, (((0,), (0,)), ((), ())), preferred_element_type=F32
    )


def swap(values, axis):
    return lax.ppermute(values, axis, [(0, 1), (1, 0)])


def in_order(index, own, other):
    return (jnp.where(index == 0, own, other), jnp.where(index == 0, other, own))


def opposite(values):
    return lax.ppermute(values, ("c", "yl"), [(0, 3), (1, 2), (2, 1), (3, 0)])


def after(values, *results):
    return lax.optimization_barrier((values, *results))[0]


def whole(top, bottom):
    return lax.optimization_barrier(
        jnp.concatenate(
            [jnp.concatenate(top, axis=1), jnp.concatenate(bottom, axis=1)], axis=0
        )
    )


def per_device(layer_input, output_grad, pre_activation, w_up, w_down):
    core, lane = lax.axis_index("c"), lax.axis_index("yl")
    rows, width = layer_input.shape
    half = rows // 2
    hidden = pre_activation.shape[1]

    input_all = lax.all_gather(layer_input, WIDE, axis=0, tiled=True)

    down_lane = swap(w_down, "yl")
    down_core = swap(w_down, "c")
    pieces = jnp.broadcast_to(output_grad.reshape(2, half, width), (4, 2, half, width))
    grad_y = lax.all_to_all(pieces.reshape(8, half, width), ("yh", "yl"), 0, 0)
    grad_y = jnp.swapaxes(grad_y.reshape(4, 2, half, width), 1, 2)
    grad_y = grad_y.reshape(4, half, 2 * width)
    grad_y = after(grad_y, down_lane, down_core)
    grad_xy = lax.all_to_all(
        jnp.broadcast_to(grad_y, (4, 4, half, 2 * width)), "x", 0, 0
    )
    grad_xy = jnp.swapaxes(grad_xy, 0, 1)
    down_both = swap(down_lane, "c")
    down_cat = whole(
        in_order(lane, w_down, down_lane), in_order(lane, down_core, down_both)
    )
    grad_rows = grad_xy.reshape(-1, 2 * width)
    part = times_transposed(grad_rows, down_cat).astype(BF16)
    blocks = lax.all_to_all(part.reshape(8, rows, 2 * hidden), "z", 0, 0)

    up_after = after(w_up, part)
    up_lane = swap(up_after, "yl")
    up_core = swap(up_after, "c")
    up_both = opposite(up_after)
    up_cat = jnp.concatenate(
        [
            jnp.concatenate([w_up, up_core], axis=1),
            jnp.concatenate([up_lane, up_both], axis=1),
        ],
        axis=0,
    )

    pre_lane = swap(pre_activation, "yl")
    pre_both = jnp.stack(in_order(lane, pre_activation, after(pre_lane, grad_y)))
    pre_cut = pre_both.reshape(2, 2, 2, half, hidden)
    pre_half = jnp.where(lane == 0, pre_cut[:, :, 0], pre_cut[:, :, 1])
    pre_own, pre_sent = (
        jnp.where(core == 0, pre_half[:, i], pre_half[:, 1 - i]) for i in range(2)
    )
    pre_pair = swap(pre_sent, "c")
    pre_tile = jnp.concatenate([pre_own, pre_pair], axis=-1).reshape(rows, 2 * hidden)
    slope_factor = gelu_parts(pre_tile)[1]
    act_tile = gelu_parts(pre_both)[0].astype(BF16).reshape(-1, hidden)
    act_all = lax.all_gather(act_tile, "z", axis=0, tiled=True)

    act_grad = jnp.sum(blocks.astype(F32), axis=0)
    slope_tile = (act_grad * slope_factor).astype(BF16)
    slopes = lax.all_gather(slope_tile, "z", axis=0, tiled=True)

    part_in = times_transposed(slopes, up_cat).astype(BF16)
    part_in = jnp.swapaxes(part_in.reshape(4, 4, half, 2 * width), 0, 1)
    blocks = lax.all_to_all(part_in, "x", 0, 0)
    part_y = jnp.sum(blocks.astype(F32), axis=0).astype(BF16)
    part_y = jnp.stack(
        in_order(lane, part_y[..., :width], part_y[..., width:]), axis=1
    )
    blocks = lax.all_to_all(part_y.reshape(8, half, width), ("yh", "yl"), 0, 0)
    input_grad = jnp.sum(blocks.reshape(4, rows, width).astype(F32), axis=0).astype(BF16)

    grad_own, grad_pair = in_order(lane, grad_xy[..., :width], grad_xy[..., width:])
    grad_lane = swap(after(grad_pair, part), "yl")
    grad_core = jnp.stack(in_order(lane, grad_own, grad_lane), axis=2)
    grad_other = swap(after(grad_core, slopes), "c")
    grad_all = jnp.stack(in_order(core, grad_core, grad_other), axis=2)
    down_grad = over_tokens(act_all, grad_all.reshape(-1, width))

    slopes_core = swap(slopes[:, hidden:], "c")
    by_core = [
        jnp.stack(
            in_order(
                lane,
                kept.reshape(16, half, hidden),
                swap(kept, "yl").reshape(16, half, hidden),
            ),
            axis=1,
        )
        for kept in (slopes[:, :hidden], slopes_core)
    ]
    slopes_all = jnp.stack(in_order(core, by_core[0], by_core[1]), axis=1)
    up_grad = over_tokens(input_all, slopes_all.reshape(-1, hidden))
    return (input_grad, up_grad, down_grad)


def solution(mesh):
    fine = Mesh(mesh.devices.reshape(4, 4, 2, 8, 2), WIDE + NARROW)
    tokens = P(WIDE, NARROW)
    hidden = P(NARROW, WIDE)
    return jax.shard_map(
        per_device,
        mesh=fine,
        in_specs=(tokens, tokens, hidden, hidden, tokens),
        out_specs=(tokens, hidden, tokens),
        check_vma=False,
    )
```

time: 204 us -> 211 us (1.034)
  other arithmetic: 12.8 us -> 27.5 us
  starting transfers between devices: 80.9 us -> 76.3 us
  waiting for transfers between devices: 48.4 us -> 45.8 us
    ppermute x12, waiting for transfers between devices: 28.8 us -> 10.7 us  [swap(): return lax.ppermute(values, axis, [(0, 1), (1, 0)])]
    concatenate x0 -> x1, other arithmetic: none -> 13.3 us  [whole(): jnp.concatenate([jnp.concatenate(top, axis=1), jnp.concatenate(bottom, ax...]
    all_to_all x1, waiting for transfers between devices: 0.01 us -> 11.8 us  [per_device(): lax.all_to_all(jnp.broadcast_to(grad_y, (4, 4, half, 2 * width)), 'x', 0, 0)]
    all_to_all x1, waiting for transfers between devices: 0.01 us -> 11.3 us  [per_device(): blocks = lax.all_to_all(part.reshape(8, rows, 2 * hidden), 'z', 0, 0)]
    all_to_all x1, waiting for transfers between devices: 7.04 us -> 0.01 us  [per_device(): blocks = lax.all_to_all(part_y.reshape(8, half, width), ('yh', 'yl'), 0, 0)]
    all_to_all x1, waiting for transfers between devices: 6.68 us -> 0.01 us  [per_device(): blocks = lax.all_to_all(part_in, 'x', 0, 0)]
    all_to_all x1, waiting for transfers between devices: 5.79 us -> 11.3 us  [per_device(): grad_y = lax.all_to_all(pieces.reshape(8, half, width), ('yh', 'yl'), 0, 0)]
    select_n x1 -> x5, other arithmetic: 2.16 us -> 7.29 us  [in_order(): jnp.where(index == 0, own, other)]
  transfers between devices with their start and end apart: 19 -> 20, of which waited for: 9 -> 6; matrix products, arithmetic and copies ran while one was open for 13% -> 19% of each run, Pallas kernels for 0% -> 0%
where the time goes in v3:
time: 211 us; the launch traced here: 208 us
  starting transfers between devices  76.3 us (36%)
  waiting for transfers between devices  45.8 us (22%)
  other arithmetic  27.5 us (13%)
  blocking collectives  21.4 us (10%)
  matrix products  14.5 us (7%)
  between operations  14.4 us (7%)
  local copies, waits for them, and re-layouts  7.68 us (4%)
    ppermute x12, starting transfers between devices, swap(): return lax.ppermute(values, axis, [(0, 1), (1, 0)])  48.9 us
    all_gather x1, blocking collectives, per_device(): slopes = lax.all_gather(slope_tile, 'z', axis=0, tiled=True)  21.4 us
    concatenate x1, other arithmetic, whole(): jnp.concatenate([jnp.concatenate(top, axis=1), jnp.concatenate(bottom, ax...  13.3 us
    all_to_all x1, waiting for transfers between devices, per_device(): lax.all_to_all(jnp.broadcast_to(grad_y, (4, 4, half, 2 * width)), 'x', 0, 0)  11.8 us
    all_to_all x1, waiting for transfers between devices, per_device(): blocks = lax.all_to_all(part.reshape(8, rows, 2 * hidden), 'z', 0, 0)  11.3 us
    all_to_all x1, waiting for transfers between devices, per_device(): grad_y = lax.all_to_all(pieces.reshape(8, half, width), ('yh', 'yl'), 0, 0)  11.3 us
    ppermute x12, waiting for transfers between devices, swap(): return lax.ppermute(values, axis, [(0, 1), (1, 0)])  10.7 us
    all_to_all x1, starting transfers between devices, per_device(): blocks = lax.all_to_all(part.reshape(8, rows, 2 * hidden), 'z', 0, 0)  10 us
  transfers between devices with their start and end apart: 20, of which 6 were waited for; matrix products, arithmetic and copies ran while one was open for 19% of the time, Pallas kernels for 0%

profile of v3, /device:TPU:1, one launch (start us, length us, event | category | flops | bytes accessed | tf_op | source)
XLA Modules:
  0.0 207.5 jit_solution(6581976147437796343)
XLA Ops:
  7.2 4.0 %collective-permute-start = (bf16[640,640]{1,0:T(8,128)(2,1)}, bf16[640,640]{1,0:T(8,128)(2,1)}, u32[]{:S(2)}, u32[]{:S(2)}) collective-permute-start(bf16[640,640]{1,0:T(8,128)(2,1)} %param.9), channel_id=1, source_target_pairs={{0,1},{1,0},{2,3},{3,2},{4,5},{5,4},{6,7},{7,6},{8,9},{9,8},{10,11... | collective-permute-start | bytes 2457608 | tf_op jit(solution)/shard_map/ppermute | solution.py:34
  11.2 6.7 %collective-permute-start.1 = (bf16[640,640]{1,0:T(8,128)(2,1)}, bf16[640,640]{1,0:T(8,128)(2,1)S(1)}, u32[]{:S(2)}, u32[]{:S(2)}) collective-permute-start(bf16[640,640]{1,0:T(8,128)(2,1)} %param.9), channel_id=1, source_target_pairs={{0,16},{16,0},{1,17},{17,1},{2,18},{18,2},{3,19},{19,3},{4,20},{20... | collective-permute-start | bytes 2457608 | tf_op jit(solution)/shard_map/ppermute | solution.py:34
  19.4 3.4 %all-to-all-start = ((bf16[8,24,640]{2,1,0:T(8,128)(2,1)}), bf16[8,24,640]{2,1,0:T(8,128)(2,1)S(1)}, u32[]{:S(2)}, u32[]{:S(2)}) async-start(bf16[8,24,640]{2,1,0:T(8,128)(2,1)} %bitcast.1), calls=%async_computation | async-start | bytes 491520 | tf_op jit(solution)/shard_map/all_to_all | solution.py:68
  22.9 3.6 %collective-permute-start.3 = (bf16[96,640]{1,0:T(8,128)(2,1)}, bf16[96,640]{1,0:T(8,128)(2,1)S(1)}, u32[]{:S(2)}, u32[]{:S(2)}) collective-permute-start(bf16[96,640]{1,0:T(8,128)(2,1)} %param.7), channel_id=1, source_target_pairs={{0,1},{1,0},{2,3},{3,2},{4,5},{5,4},{6,7},{7,6},{8,9},{9,8},{10,11... | collective-permute-start | bytes 368648 | tf_op jit(solution)/shard_map/ppermute | solution.py:34
  26.5 11.3 %all-to-all-done = bf16[8,24,640]{2,1,0:T(8,128)(2,1)S(1)} async-done(((bf16[8,24,640]{2,1,0:T(8,128)(2,1)}), bf16[8,24,640]{2,1,0:T(8,128)(2,1)S(1)}, u32[]{:S(2)}, u32[]{:S(2)}) %all-to-all-start) | async-done | bytes 245792 | tf_op jit(solution)/shard_map/all_to_all | solution.py:68
  39.8 5.5 %collective-permute-start.2 = (bf16[640,640]{1,0:T(8,128)(2,1)}, bf16[640,640]{1,0:T(8,128)(2,1)}, u32[]{:S(2)}, u32[]{:S(2)}) collective-permute-start(bf16[640,640]{1,0:T(8,128)(2,1)} %collective-permute-done), channel_id=1, source_target_pairs={{0,16},{16,0},{1,17},{17,1},{2,18},{18,2},{3,19},{19,3},{4,20},{20... | collective-permute-start | bytes 2457608 | tf_op jit(solution)/shard_map/ppermute | solution.py:34
  46.3 4.0 %all-to-all-start.1 = ((bf16[4,4,24,1280]{3,2,1,0:T(8,128)(2,1)}), bf16[4,4,24,1280]{3,2,1,0:T(8,128)(2,1)S(1)}, u32[]{:S(2)}, u32[]{:S(2)}) async-start(bf16[4,4,24,1280]{3,2,1,0:T(8,128)(2,1)} %broadcast_in_dim.7), calls=%async_computation.1 | async-start | bytes 1966080 | tf_op jit(solution)/shard_map/all_to_all | solution.py:72
  52.8 11.8 %all-to-all-done.1 = bf16[4,4,24,1280]{3,2,1,0:T(8,128)(2,1)S(1)} async-done(((bf16[4,4,24,1280]{3,2,1,0:T(8,128)(2,1)}), bf16[4,4,24,1280]{3,2,1,0:T(8,128)(2,1)S(1)}, u32[]{:S(2)}, u32[]{:S(2)}) %all-to-all-start.1) | async-done | bytes 983072 | tf_op jit(solution)/shard_map/all_to_all | solution.py:72
  67.0 13.3 %maximum_maximum_fusion = bf16[1280,1280]{1,0:T(8,128)(2,1)S(1)} fusion(bf16[640,640]{1,0:T(8,128)(2,1)S(1)} %get-tuple-element.32, bf16[640,640]{1,0:T(8,128)(2,1)S(1)} %get-tuple-element.31, bf16[640,640]{1,0:T(8,128)(2,1)S(1)} %copy-done, bf16[640,640]{1,0:T(8,128)(2,1)S(1)} %get-tuple-element.29), kind=kLoop, calls=%fused_computation | loop fusion | flops 13107200 | bytes 6553600 | tf_op jit(solution)/shard_map/concatenate | solution.py:51
  82.7 10.0 %all-to-all-start.2 = ((bf16[8,48,1280]{2,1,0:T(8,128)(2,1)}), bf16[8,48,1280]{2,1,0:T(8,128)(2,1)S(1)}, u32[]{:S(2)}, u32[]{:S(2)}) async-start(bf16[8,48,1280]{2,1,0:T(8,128)(2,1)} %bitcast.6), calls=%async_computation.2 | async-start | bytes 1966080 | tf_op jit(solution)/shard_map/all_to_all | solution.py:82
  93.6 3.1 %collective-permute-start.11 = (bf16[4,4,24,640]{3,2,1,0:T(8,128)(2,1)S(1)}, bf16[4,4,24,640]{3,2,1,0:T(8,128)(2,1)S(1)}, u32[]{:S(2)}, u32[]{:S(2)}) collective-permute-start(bf16[4,4,24,640]{3,2,1,0:T(8,128)(2,1)S(1)} %broadcast_select_fusion.6), channel_id=1, source_target_pairs={{0,1},{1,0},{2,3},{3,2},{4,5},{5,4},{6,7},{7,6},{8,9},{9,8},{10,11... | collective-permute-start | bytes 1474568 | tf_op jit(solution)/shard_map/ppermute | solution.py:34
  96.7 3.6 %collective-permute-start.4 = (bf16[2,24,640]{2,1,0:T(8,128)(2,1)S(1)}, bf16[2,24,640]{2,1,0:T(8,128)(2,1)S(1)}, u32[]{:S(2)}, u32[]{:S(2)}) collective-permute-start(bf16[2,24,640]{2,1,0:T(8,128)(2,1)S(1)} %fusion.26), channel_id=1, source_target_pairs={{0,16},{16,0},{1,17},{17,1},{2,18},{18,2},{3,19},{19,3},{4,20},{20... | collective-permute-start | bytes 184328 | tf_op jit(solution)/shard_map/ppermute | solution.py:34
  109.3 11.3 %all-to-all-done.2 = bf16[8,48,1280]{2,1,0:T(8,128)(2,1)S(1)} async-done(((bf16[8,48,1280]{2,1,0:T(8,128)(2,1)}), bf16[8,48,1280]{2,1,0:T(8,128)(2,1)S(1)}, u32[]{:S(2)}, u32[]{:S(2)}) %all-to-all-start.2) | async-done | bytes 983072 | tf_op jit(solution)/shard_map/all_to_all | solution.py:82
  120.8 21.4 %all_gather.9 = bf16[384,1280]{1,0:T(8,128)(2,1)S(1)} all-gather(bf16[48,1280]{1,0:T(8,128)(2,1)S(1)} %fusion.22), channel_id=1, replica_groups=mesh['yh'=4,'x'=4,'c'=2,'z'=8,'yl'=2] {'z'}, dimensions={0}, use_global_device_ids=true | all-gather | bytes 1105920 | tf_op jit(solution)/shard_map/all_gather | solution.py:111
  142.2 3.2 %collective-permute-start.8 = (bf16[384,640]{1,0:T(8,128)(2,1)S(1)}, bf16[384,640]{1,0:T(8,128)(2,1)}, u32[]{:S(2)}, u32[]{:S(2)}) collective-permute-start(bf16[384,640]{1,0:T(8,128)(2,1)S(1)} %slice.48), channel_id=1, source_target_pairs={{0,1},{1,0},{2,3},{3,2},{4,5},{5,4},{6,7},{7,6},{8,9},{9,8},{10,11... | collective-permute-start | bytes 1474568 | tf_op jit(solution)/shard_map/ppermute | solution.py:34
  145.4 4.0 %collective-permute-done.6 = bf16[640,640]{1,0:T(8,128)(2,1)} collective-permute-done((bf16[640,640]{1,0:T(8,128)(2,1)}, bf16[640,640]{1,0:T(8,128)(2,1)}, u32[]{:S(2)}, u32[]{:S(2)}) %collective-permute-start.6) | collective-permute-done | bytes 819232 | tf_op jit(solution)/shard_map/ppermute | solution.py:34
  149.5 3.1 %fusion.8 = bf16[384,1280]{1,0:T(8,128)(2,1)S(1)} fusion(bf16[384,1280]{1,0:T(8,128)(2,1)S(1)} %all_gather.9, bf16[640,640]{1,0:T(8,128)(2,1)} %collective-permute-done.7, bf16[640,640]{1,0:T(8,128)(2,1)} %collective-permute-done.6, bf16[640,640]{1,0:T(8,128)(2,1)} %collective-permute-done.5, bf16[640,640]{1,0:T(8,128)(2,1)S(1)} %copy-done.4), kind=kOutput, calls=%fused_computation.9 | convolution fusion | flops 1271889920 | bytes 5242880 | tf_op jit(solution)/shard_map/dot_general | solution.py:22
  153.6 3.5 %all-to-all-start.3 = ((bf16[4,4,24,1280]{3,2,1,0:T(8,128)(2,1)}), bf16[4,4,24,1280]{3,2,1,0:T(8,128)(2,1)S(1)}, u32[]{:S(2)}, u32[]{:S(2)}) async-start(bf16[4,4,24,1280]{3,2,1,0:T(8,128)(2,1)} %bitcast.83), calls=%async_computation.3 | async-start | bytes 1966080 | tf_op jit(solution)/shard_map/all_to_all | solution.py:115
  158.2 8.6 %collective-permute-start.12 = (bf16[4,4,2,24,640]{4,3,1,0,2:T(8,128)(2,1)}, bf16[4,4,2,24,640]{4,3,1,0,2:T(8,128)(2,1)}, u32[]{:S(2)}, u32[]{:S(2)}) collective-permute-start(bf16[4,4,2,24,640]{4,3,1,0,2:T(8,128)(2,1)} %pad_maximum_fusion.4), channel_id=1, source_target_pairs={{0,16},{16,0},{1,17},{17,1},{2,18},{18,2},{3,19},{19,3},{4,20},{20... | collective-permute-start | bytes 2949128 | tf_op jit(solution)/shard_map/ppermute | solution.py:34
  171.8 3.9 %all-to-all-start.4 = ((bf16[8,24,640]{2,1,0:T(8,128)(2,1)}), bf16[8,24,640]{2,1,0:T(8,128)(2,1)S(1)}, u32[]{:S(2)}, u32[]{:S(2)}) async-start(bf16[8,24,640]{2,1,0:T(8,128)(2,1)} %bitcast.22), calls=%async_computation.4 | async-start | bytes 491520 | tf_op jit(solution)/shard_map/all_to_all | solution.py:120
  175.7 3.4 %collective-permute-start.10 = (bf16[384,640]{1,0:T(8,128)(2,1)}, bf16[384,640]{1,0:T(8,128)(2,1)S(1)}, u32[]{:S(2)}, u32[]{:S(2)}) collective-permute-start(bf16[384,640]{1,0:T(8,128)(2,1)} %collective-permute-done.9), channel_id=1, source_target_pairs={{0,1},{1,0},{2,3},{3,2},{4,5},{5,4},{6,7},{7,6},{8,9},{9,8},{10,11... | collective-permute-start | bytes 1474568 | tf_op jit(solution)/shard_map/ppermute | solution.py:34
  180.9 4.4 %fusion.29 = f32[640,640]{1,0:T(8,128)} fusion(bf16[1536,640]{1,0:T(8,128)(2,1)} %all-gather.5.cloned.1.call-done, bf16[1536,640]{1,0:T(8,128)(2,1)S(1)} %bitcast.81), kind=kOutput, calls=%fused_computation.73 | convolution fusion | flops 1258291200 | bytes 5570560 | tf_op jit(solution)/shard_map/dot_general | solution.py:28
  186.1 5.8 %collective-permute-done.10 = bf16[384,640]{1,0:T(8,128)(2,1)S(1)} collective-permute-done((bf16[384,640]{1,0:T(8,128)(2,1)}, bf16[384,640]{1,0:T(8,128)(2,1)S(1)}, u32[]{:S(2)}, u32[]{:S(2)}) %collective-permute-start.10) | collective-permute-done | bytes 491552 | tf_op jit(solution)/shard_map/ppermute | solution.py:34
  193.5 4.5 %convolution_bitcast_fusion = f32[640,640]{0,1:T(8,128)} fusion(bf16[1536,640]{1,0:T(8,128)(2,1)S(1)} %bitcast.82, bf16[1536,640]{1,0:T(8,128)(2,1)} %all-gather.3.cloned.1.call-done), kind=kOutput, calls=%fused_computation.14 | convolution fusion | flops 1258291200 | bytes 5570560 | tf_op jit(solution)/shard_map/dot_general | solution.py:28
  (66 shorter events, 35.8 us)
Async XLA Ops:
  7.2 30.6 %collective-permute-start = (bf16[640,640]{1,0:T(8,128)(2,1)}, bf16[640,640]{1,0:T(8,128)(2,1)}, u32[]{:S(2)}, u32[]{:S(2)}) collective-permute-start(bf16[640,640]{1,0:T(8,128)(2,1)} %param.9), channel_id=1, source_target_pairs={{0,1},{1,0},{2,3},{3,2},{4,5},{5,4},{6,7},{7,6},{8,9},{9,8},{10,11... | collective-permute-start | bytes 2457608 | tf_op jit(solution)/shard_map/ppermute | solution.py:34
  11.2 26.6 %collective-permute-start.1 = (bf16[640,640]{1,0:T(8,128)(2,1)}, bf16[640,640]{1,0:T(8,128)(2,1)S(1)}, u32[]{:S(2)}, u32[]{:S(2)}) collective-permute-start(bf16[640,640]{1,0:T(8,128)(2,1)} %param.9), channel_id=1, source_target_pairs={{0,16},{16,0},{1,17},{17,1},{2,18},{18,2},{3,19},{19,3},{4,20},{20... | collective-permute-start | bytes 2457608 | tf_op jit(solution)/shard_map/ppermute | solution.py:34
  19.4 18.3 %all-to-all-start = ((bf16[8,24,640]{2,1,0:T(8,128)(2,1)}), bf16[8,24,640]{2,1,0:T(8,128)(2,1)S(1)}, u32[]{:S(2)}, u32[]{:S(2)}) async-start(bf16[8,24,640]{2,1,0:T(8,128)(2,1)} %bitcast.1), calls=%async_computation | async-start | bytes 491520 | tf_op jit(solution)/shard_map/all_to_all | solution.py:68
  22.8 158.1 %all-gather.5.cloned.1.call-start = ((), (), s32[]{:S(2)}) async-start(), calls=%async_computation.6 | async-start | bytes 2211840 | tf_op jit(solution)/shard_map/all_gather | solution.py:107
  22.9 14.9 %collective-permute-start.3 = (bf16[96,640]{1,0:T(8,128)(2,1)}, bf16[96,640]{1,0:T(8,128)(2,1)S(1)}, u32[]{:S(2)}, u32[]{:S(2)}) collective-permute-start(bf16[96,640]{1,0:T(8,128)(2,1)} %param.7), channel_id=1, source_target_pairs={{0,1},{1,0},{2,3},{3,2},{4,5},{5,4},{6,7},{7,6},{8,9},{9,8},{10,11... | collective-permute-start | bytes 368648 | tf_op jit(solution)/shard_map/ppermute | solution.py:34
  37.8 8.5 %copy-start.2 = (bf16[640,640]{1,0:T(8,128)(2,1)}, bf16[640,640]{1,0:T(8,128)(2,1)S(1)}, u32[]{:S(2)}) copy-start(bf16[640,640]{1,0:T(8,128)(2,1)S(1)} %collective-permute-done.1) | copy-start | bytes 2457604
  39.8 24.8 %collective-permute-start.2 = (bf16[640,640]{1,0:T(8,128)(2,1)}, bf16[640,640]{1,0:T(8,128)(2,1)}, u32[]{:S(2)}, u32[]{:S(2)}) collective-permute-start(bf16[640,640]{1,0:T(8,128)(2,1)} %collective-permute-done), channel_id=1, source_target_pairs={{0,16},{16,0},{1,17},{17,1},{2,18},{18,2},{3,19},{19,3},{4,20},{20... | collective-permute-start | bytes 2457608 | tf_op jit(solution)/shard_map/ppermute | solution.py:34
  46.3 18.2 %all-to-all-start.1 = ((bf16[4,4,24,1280]{3,2,1,0:T(8,128)(2,1)}), bf16[4,4,24,1280]{3,2,1,0:T(8,128)(2,1)S(1)}, u32[]{:S(2)}, u32[]{:S(2)}) async-start(bf16[4,4,24,1280]{3,2,1,0:T(8,128)(2,1)} %broadcast_in_dim.7), calls=%async_computation.1 | async-start | bytes 1966080 | tf_op jit(solution)/shard_map/all_to_all | solution.py:72
  64.6 2.4 %copy-start = (bf16[640,640]{1,0:T(8,128)(2,1)S(1)}, bf16[640,640]{1,0:T(8,128)(2,1)}, u32[]{:S(2)}) copy-start(bf16[640,640]{1,0:T(8,128)(2,1)} %get-tuple-element.30) | copy-start | bytes 2457604
  82.7 37.8 %all-to-all-start.2 = ((bf16[8,48,1280]{2,1,0:T(8,128)(2,1)}), bf16[8,48,1280]{2,1,0:T(8,128)(2,1)S(1)}, u32[]{:S(2)}, u32[]{:S(2)}) async-start(bf16[8,48,1280]{2,1,0:T(8,128)(2,1)} %bitcast.6), calls=%async_computation.2 | async-start | bytes 1966080 | tf_op jit(solution)/shard_map/all_to_all | solution.py:82
  92.8 100.7 %all-gather.3.cloned.1.call-start = ((), (), s32[]{:S(2)}) async-start(), calls=%async_computation.5 | async-start | bytes 2027520 | tf_op jit(solution)/shard_map/all_gather | solution.py:63
  93.6 15.5 %collective-permute-start.11 = (bf16[4,4,24,640]{3,2,1,0:T(8,128)(2,1)S(1)}, bf16[4,4,24,640]{3,2,1,0:T(8,128)(2,1)S(1)}, u32[]{:S(2)}, u32[]{:S(2)}) collective-permute-start(bf16[4,4,24,640]{3,2,1,0:T(8,128)(2,1)S(1)} %broadcast_select_fusion.6), channel_id=1, source_target_pairs={{0,1},{1,0},{2,3},{3,2},{4,5},{5,4},{6,7},{7,6},{8,9},{9,8},{10,11... | collective-permute-start | bytes 1474568 | tf_op jit(solution)/shard_map/ppermute | solution.py:34
  96.7 4.5 %collective-permute-start.4 = (bf16[2,24,640]{2,1,0:T(8,128)(2,1)S(1)}, bf16[2,24,640]{2,1,0:T(8,128)(2,1)S(1)}, u32[]{:S(2)}, u32[]{:S(2)}) collective-permute-start(bf16[2,24,640]{2,1,0:T(8,128)(2,1)S(1)} %fusion.26), channel_id=1, source_target_pairs={{0,16},{16,0},{1,17},{17,1},{2,18},{18,2},{3,19},{19,3},{4,20},{20... | collective-permute-start | bytes 184328 | tf_op jit(solution)/shard_map/ppermute | solution.py:34
  101.2 44.2 %collective-permute-start.7 = (bf16[640,640]{1,0:T(8,128)(2,1)}, bf16[640,640]{1,0:T(8,128)(2,1)}, u32[]{:S(2)}, u32[]{:S(2)}) collective-permute-start(bf16[640,640]{1,0:T(8,128)(2,1)} %param.8), channel_id=1, source_target_pairs={{0,17},{1,16},{16,1},{17,0},{2,19},{3,18},{18,3},{19,2},{4,21},{5,... | collective-permute-start | bytes 2457608 | tf_op jit(solution)/shard_map/ppermute | solution.py:42
  103.7 45.8 %collective-permute-start.6 = (bf16[640,640]{1,0:T(8,128)(2,1)}, bf16[640,640]{1,0:T(8,128)(2,1)}, u32[]{:S(2)}, u32[]{:S(2)}) collective-permute-start(bf16[640,640]{1,0:T(8,128)(2,1)} %param.8), channel_id=1, source_target_pairs={{0,1},{1,0},{2,3},{3,2},{4,5},{5,4},{6,7},{7,6},{8,9},{9,8},{10,11... | collective-permute-start | bytes 2457608 | tf_op jit(solution)/shard_map/ppermute | solution.py:34
  106.8 42.7 %collective-permute-start.5 = (bf16[640,640]{1,0:T(8,128)(2,1)}, bf16[640,640]{1,0:T(8,128)(2,1)}, u32[]{:S(2)}, u32[]{:S(2)}) collective-permute-start(bf16[640,640]{1,0:T(8,128)(2,1)} %param.8), channel_id=1, source_target_pairs={{0,16},{16,0},{1,17},{17,1},{2,18},{18,2},{3,19},{19,3},{4,20},{20... | collective-permute-start | bytes 2457608 | tf_op jit(solution)/shard_map/ppermute | solution.py:34
  120.6 28.9 %copy-start.4 = (bf16[640,640]{1,0:T(8,128)(2,1)S(1)}, bf16[640,640]{1,0:T(8,128)(2,1)}, u32[]{:S(2)}) copy-start(bf16[640,640]{1,0:T(8,128)(2,1)} %param.8) | copy-start | bytes 2457604
  142.2 24.6 %collective-permute-start.8 = (bf16[384,640]{1,0:T(8,128)(2,1)S(1)}, bf16[384,640]{1,0:T(8,128)(2,1)}, u32[]{:S(2)}, u32[]{:S(2)}) collective-permute-start(bf16[384,640]{1,0:T(8,128)(2,1)S(1)} %slice.48), channel_id=1, source_target_pairs={{0,1},{1,0},{2,3},{3,2},{4,5},{5,4},{6,7},{7,6},{8,9},{9,8},{10,11... | collective-permute-start | bytes 1474568 | tf_op jit(solution)/shard_map/ppermute | solution.py:34
  153.6 17.2 %all-to-all-start.3 = ((bf16[4,4,24,1280]{3,2,1,0:T(8,128)(2,1)}), bf16[4,4,24,1280]{3,2,1,0:T(8,128)(2,1)S(1)}, u32[]{:S(2)}, u32[]{:S(2)}) async-start(bf16[4,4,24,1280]{3,2,1,0:T(8,128)(2,1)} %bitcast.83), calls=%async_computation.3 | async-start | bytes 1966080 | tf_op jit(solution)/shard_map/all_to_all | solution.py:115
  158.2 20.9 %collective-permute-start.12 = (bf16[4,4,2,24,640]{4,3,1,0,2:T(8,128)(2,1)}, bf16[4,4,2,24,640]{4,3,1,0,2:T(8,128)(2,1)}, u32[]{:S(2)}, u32[]{:S(2)}) collective-permute-start(bf16[4,4,2,24,640]{4,3,1,0,2:T(8,128)(2,1)} %pad_maximum_fusion.4), channel_id=1, source_target_pairs={{0,16},{16,0},{1,17},{17,1},{2,18},{18,2},{3,19},{19,3},{4,20},{20... | collective-permute-start | bytes 2949128 | tf_op jit(solution)/shard_map/ppermute | solution.py:34
  168.9 6.8 %collective-permute-start.9 = (bf16[384,640]{1,0:T(8,128)(2,1)}, bf16[384,640]{1,0:T(8,128)(2,1)}, u32[]{:S(2)}, u32[]{:S(2)}) collective-permute-start(bf16[384,640]{1,0:T(8,128)(2,1)} %get-tuple-element.39), channel_id=1, source_target_pairs={{0,16},{16,0},{1,17},{17,1},{2,18},{18,2},{3,19},{19,3},{4,20},{20... | collective-permute-start | bytes 1474568 | tf_op jit(solution)/shard_map/ppermute | solution.py:34
  171.8 13.6 %all-to-all-start.4 = ((bf16[8,24,640]{2,1,0:T(8,128)(2,1)}), bf16[8,24,640]{2,1,0:T(8,128)(2,1)S(1)}, u32[]{:S(2)}, u32[]{:S(2)}) async-start(bf16[8,24,640]{2,1,0:T(8,128)(2,1)} %bitcast.22), calls=%async_computation.4 | async-start | bytes 491520 | tf_op jit(solution)/shard_map/all_to_all | solution.py:120
  175.7 16.1 %collective-permute-start.10 = (bf16[384,640]{1,0:T(8,128)(2,1)}, bf16[384,640]{1,0:T(8,128)(2,1)S(1)}, u32[]{:S(2)}, u32[]{:S(2)}) collective-permute-start(bf16[384,640]{1,0:T(8,128)(2,1)} %collective-permute-done.9), channel_id=1, source_target_pairs={{0,1},{1,0},{2,3},{3,2},{4,5},{5,4},{6,7},{7,6},{8,9},{9,8},{10,11... | collective-permute-start | bytes 1474568 | tf_op jit(solution)/shard_map/ppermute | solution.py:34
  185.4 7.5 %copy-start.1 = (bf16[384,640]{1,0:T(8,128)(2,1)S(1)}, bf16[384,640]{1,0:T(8,128)(2,1)}, u32[]{:S(2)}) copy-start(bf16[384,640]{1,0:T(8,128)(2,1)} %get-tuple-element.36) | copy-start | bytes 1474564
  (1 other events, 1.2 us)
Sparse Core Ops, SparseCore 0:
  40.0 44.8 all-gather.4
  96.8 59.5 all-gather.2

commit v4 on v3

--- a/solution.py
+++ b/solution.py
@@ -38,19 +38,13 @@
     return (jnp.where(index == 0, own, other), jnp.where(index == 0, other, own))
 
 
-def opposite(values):
-    return lax.ppermute(values, ("c", "yl"), [(0, 3), (1, 2), (2, 1), (3, 0)])
-
-
 def after(values, *results):
     return lax.optimization_barrier((values, *results))[0]
 
 
-def whole(top, bottom):
-    return lax.optimization_barrier(
-        jnp.concatenate(
-            [jnp.concatenate(top, axis=1), jnp.concatenate(bottom, axis=1)], axis=0
-        )
+def tiled(top, bottom):
+    return jnp.concatenate(
+        [jnp.concatenate(top, axis=1), jnp.concatenate(bottom, axis=1)], axis=0
     )
 
 
@@ -62,36 +56,32 @@
 
     input_all = lax.all_gather(layer_input, WIDE, axis=0, tiled=True)
 
+    down_core = swap(w_down, "c")
     down_lane = swap(w_down, "yl")
-    down_core = swap(w_down, "c")
     pieces = jnp.broadcast_to(output_grad.reshape(2, half, width), (4, 2, half, width))
     grad_y = lax.all_to_all(pieces.reshape(8, half, width), ("yh", "yl"), 0, 0)
-    grad_y = jnp.swapaxes(grad_y.reshape(4, 2, half, width), 1, 2)
-    grad_y = grad_y.reshape(4, half, 2 * width)
-    grad_y = after(grad_y, down_lane, down_core)
+    grad_y = grad_y.reshape(4, 2, half, width)
+    grad_y = jnp.concatenate(in_order(lane, grad_y[:, 0], grad_y[:, 1]), axis=-1)
     grad_xy = lax.all_to_all(
         jnp.broadcast_to(grad_y, (4, 4, half, 2 * width)), "x", 0, 0
     )
     grad_xy = jnp.swapaxes(grad_xy, 0, 1)
     down_both = swap(down_lane, "c")
-    down_cat = whole(
-        in_order(lane, w_down, down_lane), in_order(lane, down_core, down_both)
+    grad_rows = grad_xy.reshape(-1, 2 * width)
+    part = times_transposed(
+        grad_rows[:, :width], jnp.concatenate([w_down, down_core], axis=0)
     )
-    grad_rows = grad_xy.reshape(-1, 2 * width)
-    part = times_transposed(grad_rows, down_cat).astype(BF16)
+    part = part + times_transposed(
+        grad_rows[:, width:], jnp.concatenate([down_lane, down_both], axis=0)
+    )
+    part = part.astype(BF16)
     blocks = lax.all_to_all(part.reshape(8, rows, 2 * hidden), "z", 0, 0)
 
     up_after = after(w_up, part)
     up_lane = swap(up_after, "yl")
     up_core = swap(up_after, "c")
-    up_both = opposite(up_after)
-    up_cat = jnp.concatenate(
-        [
-            jnp.concatenate([w_up, up_core], axis=1),
-            jnp.concatenate([up_lane, up_both], axis=1),
-        ],
-        axis=0,
-    )
+    up_both = swap(up_lane, "c")
+    up_cat = tiled((w_up, up_core), (up_lane, up_both))
 
     pre_lane = swap(pre_activation, "yl")
     pre_both = jnp.stack(in_order(lane, pre_activation, after(pre_lane, grad_y)))
@@ -120,24 +110,22 @@
     blocks = lax.all_to_all(part_y.reshape(8, half, width), ("yh", "yl"), 0, 0)
     input_grad = jnp.sum(blocks.reshape(4, rows, width).astype(F32), axis=0).astype(BF16)
 
-    grad_own, grad_pair = in_order(lane, grad_xy[..., :width], grad_xy[..., width:])
+    grad_own, grad_pair = grad_xy[..., :width], grad_xy[..., width:]
     grad_lane = swap(after(grad_pair, part), "yl")
     grad_core = jnp.stack(in_order(lane, grad_own, grad_lane), axis=2)
     grad_other = swap(after(grad_core, slopes), "c")
     grad_all = jnp.stack(in_order(core, grad_core, grad_other), axis=2)
     down_grad = over_tokens(act_all, grad_all.reshape(-1, width))
 
-    slopes_core = swap(slopes[:, hidden:], "c")
+    slopes_lane = swap(slopes, "yl")
+    own = (slopes[:, :hidden], slopes_lane[:, :hidden])
+    other = (
+        swap(slopes[:, hidden:], "c"),
+        swap(after(slopes_lane[:, hidden:], part_y), "c"),
+    )
     by_core = [
-        jnp.stack(
-            in_order(
-                lane,
-                kept.reshape(16, half, hidden),
-                swap(kept, "yl").reshape(16, half, hidden),
-            ),
-            axis=1,
-        )
-        for kept in (slopes[:, :hidden], slopes_core)
+        jnp.stack(in_order(lane, *(p.reshape(16, half, hidden) for p in pair)), axis=1)
+        for pair in (own, other)
     ]
     slopes_all = jnp.stack(in_order(core, by_core[0], by_core[1]), axis=1)
     up_grad = over_tokens(input_all, slopes_all.reshape(-1, hidden))

time: 211 us -> 204 us (0.967)
  other arithmetic: 27.5 us -> 10.7 us
  waiting for transfers between devices: 45.8 us -> 50.1 us
  matrix products: 14.5 us -> 17.7 us
  starting transfers between devices: 76.3 us -> 79.4 us
    ppermute x12 -> x13, waiting for transfers between devices: 10.7 us -> 39.7 us  [swap(): return lax.ppermute(values, axis, [(0, 1), (1, 0)])]
    concatenate x1, other arithmetic: 13.3 us -> 0.02 us  [per_device(): jnp.concatenate(in_order(lane, grad_y[:, 0], grad_y[:, 1]), axis=-1)]
    all_to_all x1, waiting for transfers between devices: 11.3 us -> 0.01 us  [per_device(): blocks = lax.all_to_all(part.reshape(8, rows, 2 * hidden), 'z', 0, 0)]
    all_to_all x1, waiting for transfers between devices: 11.8 us -> 3.79 us  [per_device(): lax.all_to_all(jnp.broadcast_to(grad_y, (4, 4, half, 2 * width)), 'x', 0, 0)]
    all_to_all x1, waiting for transfers between devices: 11.3 us -> 5.84 us  [per_device(): grad_y = lax.all_to_all(pieces.reshape(8, half, width), ('yh', 'yl'), 0, 0)]
    all_to_all x1, starting transfers between devices: 3.41 us -> 7.65 us  [per_device(): grad_y = lax.all_to_all(pieces.reshape(8, half, width), ('yh', 'yl'), 0, 0)]
    select_n x5 -> x4, other arithmetic: 7.29 us -> 3.88 us  [in_order(): jnp.where(index == 0, own, other)]
    dot_general x2 -> x3, matrix products: 5.58 us -> 8.83 us  [times_transposed(): lax.dot_general(left, right, (((1,), (1,)), ((), ())), preferred_element_...]
  transfers between devices with their start and end apart: 20 -> 20, of which waited for: 6 -> 7; matrix products, arithmetic and copies ran while one was open for 19% -> 13% of each run, Pallas kernels for 0% -> 0%
where the time goes in v4:
time: 204 us; the launch traced here: 202 us
  starting transfers between devices  79.4 us (39%)
  waiting for transfers between devices  50.1 us (25%)
  blocking collectives  22.2 us (11%)
  matrix products  17.7 us (9%)
  between operations  14.4 us (7%)
  other arithmetic  10.7 us (5%)
  local copies, waits for them, and re-layouts  7.45 us (4%)
    ppermute x13, starting transfers between devices, swap(): return lax.ppermute(values, axis, [(0, 1), (1, 0)])  51.4 us
    ppermute x13, waiting for transfers between devices, swap(): return lax.ppermute(values, axis, [(0, 1), (1, 0)])  39.7 us
    all_gather x1, blocking collectives, per_device(): slopes = lax.all_gather(slope_tile, 'z', axis=0, tiled=True)  22.2 us
    all_to_all x1, starting transfers between devices, per_device(): blocks = lax.all_to_all(part.reshape(8, rows, 2 * hidden), 'z', 0, 0)  9.29 us
    dot_general x2, matrix products, over_tokens(): lax.dot_general(left, right, (((0,), (0,)), ((), ())), preferred_element_...  8.88 us
    dot_general x3, matrix products, times_transposed(): lax.dot_general(left, right, (((1,), (1,)), ((), ())), preferred_element_...  8.83 us
    all_to_all x1, starting transfers between devices, per_device(): grad_y = lax.all_to_all(pieces.reshape(8, half, width), ('yh', 'yl'), 0, 0)  7.65 us
    all_to_all x1, waiting for transfers between devices, per_device(): grad_y = lax.all_to_all(pieces.reshape(8, half, width), ('yh', 'yl'), 0, 0)  5.84 us
  transfers between devices with their start and end apart: 20, of which 7 were waited for; matrix products, arithmetic and copies ran while one was open for 13% of the time, Pallas kernels for 0%

profile of v4, /device:TPU:1, one launch (start us, length us, event | category | flops | bytes accessed | tf_op | source)
XLA Modules:
  0.0 202.1 jit_solution(15583242942243155393)
XLA Ops:
  8.8 7.7 %all-to-all-start = ((bf16[8,24,640]{2,1,0:T(8,128)(2,1)}), bf16[8,24,640]{2,1,0:T(8,128)(2,1)S(1)}, u32[]{:S(2)}, u32[]{:S(2)}) async-start(bf16[8,24,640]{2,1,0:T(8,128)(2,1)} %bitcast.1), calls=%async_computation | async-start | bytes 491520 | tf_op jit(solution)/shard_map/all_to_all | solution.py:62
  16.5 3.3 %collective-permute-start.3 = (bf16[96,640]{1,0:T(8,128)(2,1)}, bf16[96,640]{1,0:T(8,128)(2,1)S(1)}, u32[]{:S(2)}, u32[]{:S(2)}) collective-permute-start(bf16[96,640]{1,0:T(8,128)(2,1)} %param.7), channel_id=1, source_target_pairs={{0,1},{1,0},{2,3},{3,2},{4,5},{5,4},{6,7},{7,6},{8,9},{9,8},{10,11... | collective-permute-start | bytes 368648 | tf_op jit(solution)/shard_map/ppermute | solution.py:34
  19.8 5.8 %all-to-all-done = bf16[8,24,640]{2,1,0:T(8,128)(2,1)S(1)} async-done(((bf16[8,24,640]{2,1,0:T(8,128)(2,1)}), bf16[8,24,640]{2,1,0:T(8,128)(2,1)S(1)}, u32[]{:S(2)}, u32[]{:S(2)}) %all-to-all-start) | async-done | bytes 245792 | tf_op jit(solution)/shard_map/all_to_all | solution.py:62
  26.7 3.1 %collective-permute-start.1 = (bf16[640,640]{1,0:T(8,128)(2,1)S(1)}, bf16[640,640]{1,0:T(8,128)(2,1)}, u32[]{:S(2)}, u32[]{:S(2)}) collective-permute-start(bf16[640,640]{1,0:T(8,128)(2,1)S(1)} %copy-done.3), channel_id=1, source_target_pairs={{0,1},{1,0},{2,3},{3,2},{4,5},{5,4},{6,7},{7,6},{8,9},{9,8},{10,11... | collective-permute-start | bytes 2457608 | tf_op jit(solution)/shard_map/ppermute | solution.py:34
  29.9 6.2 %collective-permute-start = (bf16[640,640]{1,0:T(8,128)(2,1)S(1)}, bf16[640,640]{1,0:T(8,128)(2,1)}, u32[]{:S(2)}, u32[]{:S(2)}) collective-permute-start(bf16[640,640]{1,0:T(8,128)(2,1)S(1)} %copy-done.3), channel_id=1, source_target_pairs={{0,16},{16,0},{1,17},{17,1},{2,18},{18,2},{3,19},{19,3},{4,20},{20... | collective-permute-start | bytes 2457608 | tf_op jit(solution)/shard_map/ppermute | solution.py:34
  37.0 3.5 %all-to-all-start.1 = ((bf16[4,4,24,1280]{3,2,1,0:T(8,128)(2,1)}), bf16[4,4,24,1280]{3,2,1,0:T(8,128)(2,1)S(1)}, u32[]{:S(2)}, u32[]{:S(2)}) async-start(bf16[4,4,24,1280]{3,2,1,0:T(8,128)(2,1)} %broadcast_in_dim.7), calls=%async_computation.1 | async-start | bytes 1966080 | tf_op jit(solution)/shard_map/all_to_all | solution.py:65
  40.6 3.4 %collective-permute-done.1 = bf16[640,640]{1,0:T(8,128)(2,1)} collective-permute-done((bf16[640,640]{1,0:T(8,128)(2,1)S(1)}, bf16[640,640]{1,0:T(8,128)(2,1)}, u32[]{:S(2)}, u32[]{:S(2)}) %collective-permute-start.1) | collective-permute-done | bytes 819232 | tf_op jit(solution)/shard_map/ppermute | solution.py:34
  43.9 7.4 %collective-permute-start.2 = (bf16[640,640]{1,0:T(8,128)(2,1)}, bf16[640,640]{1,0:T(8,128)(2,1)}, u32[]{:S(2)}, u32[]{:S(2)}) collective-permute-start(bf16[640,640]{1,0:T(8,128)(2,1)} %collective-permute-done.1), channel_id=1, source_target_pairs={{0,16},{16,0},{1,17},{17,1},{2,18},{18,2},{3,19},{19,3},{4,20},{20... | collective-permute-start | bytes 2457608 | tf_op jit(solution)/shard_map/ppermute | solution.py:34
  51.3 3.8 %all-to-all-done.1 = bf16[4,4,24,1280]{3,2,1,0:T(8,128)(2,1)S(1)} async-done(((bf16[4,4,24,1280]{3,2,1,0:T(8,128)(2,1)}), bf16[4,4,24,1280]{3,2,1,0:T(8,128)(2,1)S(1)}, u32[]{:S(2)}, u32[]{:S(2)}) %all-to-all-start.1) | async-done | bytes 983072 | tf_op jit(solution)/shard_map/all_to_all | solution.py:65
  57.3 3.4 %fusion.8 = bf16[384,1280]{1,0:T(8,128)(2,1)} fusion(f32[384,1280]{1,0:T(8,128)S(1)} %fusion.12, bf16[640,640]{1,0:T(8,128)(2,1)} %collective-permute-done.2, bf16[640,640]{1,0:T(8,128)(2,1)} %collective-permute-done.1, bf16[384,1280]{1,0:T(8,128)(2,1)S(1)} %bitcast.91), kind=kOutput, calls=%fused_computation.9 | convolution fusion | flops 633405440 | bytes 5079040 | tf_op jit(solution)/shard_map/dot_general | solution.py:22
  60.7 9.3 %all-to-all-start.2 = ((bf16[8,48,1280]{2,1,0:T(8,128)(2,1)}), bf16[8,48,1280]{2,1,0:T(8,128)(2,1)S(1)}, u32[]{:S(2)}, u32[]{:S(2)}) async-start(bf16[8,48,1280]{2,1,0:T(8,128)(2,1)} %bitcast.11), calls=%async_computation.2 | async-start | bytes 1966080 | tf_op jit(solution)/shard_map/all_to_all | solution.py:78
  70.8 3.2 %collective-permute-start.11 = (bf16[4,4,24,640]{3,2,1,0:T(8,128)(2,1)S(1)}, bf16[4,4,24,640]{3,2,1,0:T(8,128)(2,1)S(1)}, u32[]{:S(2)}, u32[]{:S(2)}) collective-permute-start(bf16[4,4,24,640]{3,2,1,0:T(8,128)(2,1)S(1)} %slice.81), channel_id=1, source_target_pairs={{0,1},{1,0},{2,3},{3,2},{4,5},{5,4},{6,7},{7,6},{8,9},{9,8},{10,11... | collective-permute-start | bytes 1474568 | tf_op jit(solution)/shard_map/ppermute | solution.py:34
  76.1 3.9 %collective-permute-start.4 = (bf16[2,24,640]{2,1,0:T(8,128)(2,1)S(1)}, bf16[2,24,640]{2,1,0:T(8,128)(2,1)S(1)}, u32[]{:S(2)}, u32[]{:S(2)}) collective-permute-start(bf16[2,24,640]{2,1,0:T(8,128)(2,1)S(1)} %fusion.38), channel_id=1, source_target_pairs={{0,16},{16,0},{1,17},{17,1},{2,18},{18,2},{3,19},{19,3},{4,20},{20... | collective-permute-start | bytes 184328 | tf_op jit(solution)/shard_map/ppermute | solution.py:34
  84.1 17.6 %collective-permute-done.6 = bf16[640,640]{1,0:T(8,128)(2,1)} collective-permute-done((bf16[640,640]{1,0:T(8,128)(2,1)}, bf16[640,640]{1,0:T(8,128)(2,1)}, u32[]{:S(2)}, u32[]{:S(2)}) %collective-permute-start.6) | collective-permute-done | bytes 819232 | tf_op jit(solution)/shard_map/ppermute | solution.py:34
  101.7 4.5 %collective-permute-start.7 = (bf16[640,640]{1,0:T(8,128)(2,1)}, bf16[640,640]{1,0:T(8,128)(2,1)}, u32[]{:S(2)}, u32[]{:S(2)}) collective-permute-start(bf16[640,640]{1,0:T(8,128)(2,1)} %collective-permute-done.6), channel_id=1, source_target_pairs={{0,16},{16,0},{1,17},{17,1},{2,18},{18,2},{3,19},{19,3},{4,20},{20... | collective-permute-start | bytes 2457608 | tf_op jit(solution)/shard_map/ppermute | solution.py:34
  106.5 22.2 %all_gather.9 = bf16[384,1280]{1,0:T(8,128)(2,1)S(1)} all-gather(bf16[48,1280]{1,0:T(8,128)(2,1)S(1)} %fusion.32), channel_id=1, replica_groups=mesh['yh'=4,'x'=4,'c'=2,'z'=8,'yl'=2] {'z'}, dimensions={0}, use_global_device_ids=true | all-gather | bytes 1105920 | tf_op jit(solution)/shard_map/all_gather | solution.py:101
  128.7 3.3 %fusion.9 = bf16[384,1280]{1,0:T(8,128)(2,1)S(1)} fusion(bf16[384,1280]{1,0:T(8,128)(2,1)S(1)} %all_gather.9, bf16[640,640]{1,0:T(8,128)(2,1)} %collective-permute-done.7, bf16[640,640]{1,0:T(8,128)(2,1)} %collective-permute-done.6, bf16[640,640]{1,0:T(8,128)(2,1)} %collective-permute-done.5, bf16[640,640]{1,0:T(8,128)(2,1)} %param.8), kind=kOutput, calls=%fused_computation.10 | convolution fusion | flops 1271889920 | bytes 5242880 | tf_op jit(solution)/shard_map/dot_general | solution.py:22
  133.1 3.5 %all-to-all-start.3 = ((bf16[4,4,24,1280]{3,2,1,0:T(8,128)(2,1)}), bf16[4,4,24,1280]{3,2,1,0:T(8,128)(2,1)S(1)}, u32[]{:S(2)}, u32[]{:S(2)}) async-start(bf16[4,4,24,1280]{3,2,1,0:T(8,128)(2,1)} %bitcast.85), calls=%async_computation.3 | async-start | bytes 1966080 | tf_op jit(solution)/shard_map/all_to_all | solution.py:105
  137.7 7.2 %collective-permute-start.12 = (bf16[4,4,2,24,640]{4,3,1,0,2:T(8,128)(2,1)}, bf16[4,4,2,24,640]{4,3,1,0,2:T(8,128)(2,1)}, u32[]{:S(2)}, u32[]{:S(2)}) collective-permute-start(bf16[4,4,2,24,640]{4,3,1,0,2:T(8,128)(2,1)} %pad_maximum_fusion.4), channel_id=1, source_target_pairs={{0,16},{16,0},{1,17},{17,1},{2,18},{18,2},{3,19},{19,3},{4,20},{20... | collective-permute-start | bytes 2949128 | tf_op jit(solution)/shard_map/ppermute | solution.py:34
  144.9 3.5 %collective-permute-start.8 = (bf16[384,1280]{1,0:T(8,128)(2,1)S(1)}, bf16[384,1280]{1,0:T(8,128)(2,1)}, u32[]{:S(2)}, u32[]{:S(2)}) collective-permute-start(bf16[384,1280]{1,0:T(8,128)(2,1)S(1)} %all_gather.9), channel_id=1, source_target_pairs={{0,1},{1,0},{2,3},{3,2},{4,5},{5,4},{6,7},{7,6},{8,9},{9,8},{10,11... | collective-permute-start | bytes 2949128 | tf_op jit(solution)/shard_map/ppermute | solution.py:34
  149.3 4.0 %all-to-all-start.4 = ((bf16[8,24,640]{2,1,0:T(8,128)(2,1)}), bf16[8,24,640]{2,1,0:T(8,128)(2,1)}, u32[]{:S(2)}, u32[]{:S(2)}) async-start(bf16[8,24,640]{2,1,0:T(8,128)(2,1)} %bitcast.27), calls=%async_computation.4 | async-start | bytes 491520 | tf_op jit(solution)/shard_map/all_to_all | solution.py:110
  154.8 17.0 %collective-permute-done.8 = bf16[384,1280]{1,0:T(8,128)(2,1)} collective-permute-done((bf16[384,1280]{1,0:T(8,128)(2,1)S(1)}, bf16[384,1280]{1,0:T(8,128)(2,1)}, u32[]{:S(2)}, u32[]{:S(2)}) %collective-permute-start.8) | collective-permute-done | bytes 983072 | tf_op jit(solution)/shard_map/ppermute | solution.py:34
  179.4 4.4 %fusion.43 = f32[640,640]{1,0:T(8,128)} fusion(bf16[1536,640]{1,0:T(8,128)(2,1)} %all-gather.5.cloned.1.call-done, bf16[1536,640]{1,0:T(8,128)(2,1)S(1)} %bitcast.88), kind=kOutput, calls=%fused_computation.83 | convolution fusion | flops 1258291200 | bytes 5570560 | tf_op jit(solution)/shard_map/dot_general | solution.py:28
  188.1 4.4 %convolution_bitcast_fusion = f32[640,640]{0,1:T(8,128)} fusion(bf16[1536,640]{1,0:T(8,128)(2,1)S(1)} %bitcast.89, bf16[1536,640]{1,0:T(8,128)(2,1)} %all-gather.3.cloned.1.call-done), kind=kOutput, calls=%fused_computation.21 | convolution fusion | flops 1258291200 | bytes 5570560 | tf_op jit(solution)/shard_map/dot_general | solution.py:28
  (63 shorter events, 32.0 us)
Async XLA Ops:
  7.2 18.6 %copy-start.2 = (bf16[96,640]{1,0:T(8,128)(2,1)S(1)}, bf16[96,640]{1,0:T(8,128)(2,1)}, u32[]{:S(2)}) copy-start(bf16[96,640]{1,0:T(8,128)(2,1)} %param.7) | copy-start | bytes 368644
  7.2 19.5 %copy-start.3 = (bf16[640,640]{1,0:T(8,128)(2,1)S(1)}, bf16[640,640]{1,0:T(8,128)(2,1)}, u32[]{:S(2)}) copy-start(bf16[640,640]{1,0:T(8,128)(2,1)} %param.9) | copy-start | bytes 2457604
  8.8 16.9 %all-to-all-start = ((bf16[8,24,640]{2,1,0:T(8,128)(2,1)}), bf16[8,24,640]{2,1,0:T(8,128)(2,1)S(1)}, u32[]{:S(2)}, u32[]{:S(2)}) async-start(bf16[8,24,640]{2,1,0:T(8,128)(2,1)} %bitcast.1), calls=%async_computation | async-start | bytes 491520 | tf_op jit(solution)/shard_map/all_to_all | solution.py:62
  16.5 162.9 %all-gather.5.cloned.1.call-start = ((), (), s32[]{:S(2)}) async-start(), calls=%async_computation.6 | async-start | bytes 2211840 | tf_op jit(solution)/shard_map/all_gather | solution.py:97
  16.5 9.3 %collective-permute-start.3 = (bf16[96,640]{1,0:T(8,128)(2,1)}, bf16[96,640]{1,0:T(8,128)(2,1)S(1)}, u32[]{:S(2)}, u32[]{:S(2)}) collective-permute-start(bf16[96,640]{1,0:T(8,128)(2,1)} %param.7), channel_id=1, source_target_pairs={{0,1},{1,0},{2,3},{3,2},{4,5},{5,4},{6,7},{7,6},{8,9},{9,8},{10,11... | collective-permute-start | bytes 368648 | tf_op jit(solution)/shard_map/ppermute | solution.py:34
  26.7 17.2 %collective-permute-start.1 = (bf16[640,640]{1,0:T(8,128)(2,1)S(1)}, bf16[640,640]{1,0:T(8,128)(2,1)}, u32[]{:S(2)}, u32[]{:S(2)}) collective-permute-start(bf16[640,640]{1,0:T(8,128)(2,1)S(1)} %copy-done.3), channel_id=1, source_target_pairs={{0,1},{1,0},{2,3},{3,2},{4,5},{5,4},{6,7},{7,6},{8,9},{9,8},{10,11... | collective-permute-start | bytes 2457608 | tf_op jit(solution)/shard_map/ppermute | solution.py:34
  29.9 25.3 %collective-permute-start = (bf16[640,640]{1,0:T(8,128)(2,1)S(1)}, bf16[640,640]{1,0:T(8,128)(2,1)}, u32[]{:S(2)}, u32[]{:S(2)}) collective-permute-start(bf16[640,640]{1,0:T(8,128)(2,1)S(1)} %copy-done.3), channel_id=1, source_target_pairs={{0,16},{16,0},{1,17},{17,1},{2,18},{18,2},{3,19},{19,3},{4,20},{20... | collective-permute-start | bytes 2457608 | tf_op jit(solution)/shard_map/ppermute | solution.py:34
  37.0 18.0 %all-to-all-start.1 = ((bf16[4,4,24,1280]{3,2,1,0:T(8,128)(2,1)}), bf16[4,4,24,1280]{3,2,1,0:T(8,128)(2,1)S(1)}, u32[]{:S(2)}, u32[]{:S(2)}) async-start(bf16[4,4,24,1280]{3,2,1,0:T(8,128)(2,1)} %broadcast_in_dim.7), calls=%async_computation.1 | async-start | bytes 1966080 | tf_op jit(solution)/shard_map/all_to_all | solution.py:65
  43.9 13.4 %collective-permute-start.2 = (bf16[640,640]{1,0:T(8,128)(2,1)}, bf16[640,640]{1,0:T(8,128)(2,1)}, u32[]{:S(2)}, u32[]{:S(2)}) collective-permute-start(bf16[640,640]{1,0:T(8,128)(2,1)} %collective-permute-done.1), channel_id=1, source_target_pairs={{0,16},{16,0},{1,17},{17,1},{2,18},{18,2},{3,19},{19,3},{4,20},{20... | collective-permute-start | bytes 2457608 | tf_op jit(solution)/shard_map/ppermute | solution.py:34
  60.7 45.6 %all-to-all-start.2 = ((bf16[8,48,1280]{2,1,0:T(8,128)(2,1)}), bf16[8,48,1280]{2,1,0:T(8,128)(2,1)S(1)}, u32[]{:S(2)}, u32[]{:S(2)}) async-start(bf16[8,48,1280]{2,1,0:T(8,128)(2,1)} %bitcast.11), calls=%async_computation.2 | async-start | bytes 1966080 | tf_op jit(solution)/shard_map/all_to_all | solution.py:78
  70.0 118.1 %all-gather.3.cloned.1.call-start = ((), (), s32[]{:S(2)}) async-start(), calls=%async_computation.5 | async-start | bytes 2027520 | tf_op jit(solution)/shard_map/all_gather | solution.py:57
  70.8 13.2 %collective-permute-start.11 = (bf16[4,4,24,640]{3,2,1,0:T(8,128)(2,1)S(1)}, bf16[4,4,24,640]{3,2,1,0:T(8,128)(2,1)S(1)}, u32[]{:S(2)}, u32[]{:S(2)}) collective-permute-start(bf16[4,4,24,640]{3,2,1,0:T(8,128)(2,1)S(1)} %slice.81), channel_id=1, source_target_pairs={{0,1},{1,0},{2,3},{3,2},{4,5},{5,4},{6,7},{7,6},{8,9},{9,8},{10,11... | collective-permute-start | bytes 1474568 | tf_op jit(solution)/shard_map/ppermute | solution.py:34
  74.0 27.7 %collective-permute-start.6 = (bf16[640,640]{1,0:T(8,128)(2,1)}, bf16[640,640]{1,0:T(8,128)(2,1)}, u32[]{:S(2)}, u32[]{:S(2)}) collective-permute-start(bf16[640,640]{1,0:T(8,128)(2,1)} %param.8), channel_id=1, source_target_pairs={{0,1},{1,0},{2,3},{3,2},{4,5},{5,4},{6,7},{7,6},{8,9},{9,8},{10,11... | collective-permute-start | bytes 2457608 | tf_op jit(solution)/shard_map/ppermute | solution.py:34
  76.1 4.7 %collective-permute-start.4 = (bf16[2,24,640]{2,1,0:T(8,128)(2,1)S(1)}, bf16[2,24,640]{2,1,0:T(8,128)(2,1)S(1)}, u32[]{:S(2)}, u32[]{:S(2)}) collective-permute-start(bf16[2,24,640]{2,1,0:T(8,128)(2,1)S(1)} %fusion.38), channel_id=1, source_target_pairs={{0,16},{16,0},{1,17},{17,1},{2,18},{18,2},{3,19},{19,3},{4,20},{20... | collective-permute-start | bytes 184328 | tf_op jit(solution)/shard_map/ppermute | solution.py:34
  80.9 47.9 %collective-permute-start.5 = (bf16[640,640]{1,0:T(8,128)(2,1)}, bf16[640,640]{1,0:T(8,128)(2,1)}, u32[]{:S(2)}, u32[]{:S(2)}) collective-permute-start(bf16[640,640]{1,0:T(8,128)(2,1)} %param.8), channel_id=1, source_target_pairs={{0,16},{16,0},{1,17},{17,1},{2,18},{18,2},{3,19},{19,3},{4,20},{20... | collective-permute-start | bytes 2457608 | tf_op jit(solution)/shard_map/ppermute | solution.py:34
  101.7 27.1 %collective-permute-start.7 = (bf16[640,640]{1,0:T(8,128)(2,1)}, bf16[640,640]{1,0:T(8,128)(2,1)}, u32[]{:S(2)}, u32[]{:S(2)}) collective-permute-start(bf16[640,640]{1,0:T(8,128)(2,1)} %collective-permute-done.6), channel_id=1, source_target_pairs={{0,16},{16,0},{1,17},{17,1},{2,18},{18,2},{3,19},{19,3},{4,20},{20... | collective-permute-start | bytes 2457608 | tf_op jit(solution)/shard_map/ppermute | solution.py:34
  133.1 15.3 %all-to-all-start.3 = ((bf16[4,4,24,1280]{3,2,1,0:T(8,128)(2,1)}), bf16[4,4,24,1280]{3,2,1,0:T(8,128)(2,1)S(1)}, u32[]{:S(2)}, u32[]{:S(2)}) async-start(bf16[4,4,24,1280]{3,2,1,0:T(8,128)(2,1)} %bitcast.85), calls=%async_computation.3 | async-start | bytes 1966080 | tf_op jit(solution)/shard_map/all_to_all | solution.py:105
  137.7 15.7 %collective-permute-start.12 = (bf16[4,4,2,24,640]{4,3,1,0,2:T(8,128)(2,1)}, bf16[4,4,2,24,640]{4,3,1,0,2:T(8,128)(2,1)}, u32[]{:S(2)}, u32[]{:S(2)}) collective-permute-start(bf16[4,4,2,24,640]{4,3,1,0,2:T(8,128)(2,1)} %pad_maximum_fusion.4), channel_id=1, source_target_pairs={{0,16},{16,0},{1,17},{17,1},{2,18},{18,2},{3,19},{19,3},{4,20},{20... | collective-permute-start | bytes 2949128 | tf_op jit(solution)/shard_map/ppermute | solution.py:34
  144.9 26.9 %collective-permute-start.8 = (bf16[384,1280]{1,0:T(8,128)(2,1)S(1)}, bf16[384,1280]{1,0:T(8,128)(2,1)}, u32[]{:S(2)}, u32[]{:S(2)}) collective-permute-start(bf16[384,1280]{1,0:T(8,128)(2,1)S(1)} %all_gather.9), channel_id=1, source_target_pairs={{0,1},{1,0},{2,3},{3,2},{4,5},{5,4},{6,7},{7,6},{8,9},{9,8},{10,11... | collective-permute-start | bytes 2949128 | tf_op jit(solution)/shard_map/ppermute | solution.py:34
  149.3 34.5 %all-to-all-start.4 = ((bf16[8,24,640]{2,1,0:T(8,128)(2,1)}), bf16[8,24,640]{2,1,0:T(8,128)(2,1)}, u32[]{:S(2)}, u32[]{:S(2)}) async-start(bf16[8,24,640]{2,1,0:T(8,128)(2,1)} %bitcast.27), calls=%async_computation.4 | async-start | bytes 491520 | tf_op jit(solution)/shard_map/all_to_all | solution.py:110
  174.6 10.9 %collective-permute-start.10 = (bf16[384,640]{1,0:T(8,128)(2,1)}, bf16[384,640]{1,0:T(8,128)(2,1)S(1)}, u32[]{:S(2)}, u32[]{:S(2)}) collective-permute-start(bf16[384,640]{1,0:T(8,128)(2,1)} %get-tuple-element.10), channel_id=1, source_target_pairs={{0,16},{16,0},{1,17},{17,1},{2,18},{18,2},{3,19},{19,3},{4,20},{20... | collective-permute-start | bytes 1474568 | tf_op jit(solution)/shard_map/ppermute | solution.py:34
  177.4 8.9 %collective-permute-start.9 = (bf16[384,640]{1,0:T(8,128)(2,1)}, bf16[384,640]{1,0:T(8,128)(2,1)}, u32[]{:S(2)}, u32[]{:S(2)}) collective-permute-start(bf16[384,640]{1,0:T(8,128)(2,1)} %get-tuple-element.32), channel_id=1, source_target_pairs={{0,16},{16,0},{1,17},{17,1},{2,18},{18,2},{3,19},{19,3},{4,20},{20... | collective-permute-start | bytes 1474568 | tf_op jit(solution)/shard_map/ppermute | solution.py:34
  183.8 3.7 %copy-start = (bf16[384,640]{1,0:T(8,128)(2,1)S(1)}, bf16[384,640]{1,0:T(8,128)(2,1)}, u32[]{:S(2)}) copy-start(bf16[384,640]{1,0:T(8,128)(2,1)} %get-tuple-element.27) | copy-start | bytes 1474564
  185.5 0.8 copy-start.1
Sparse Core Ops, SparseCore 0:
  26.8 44.7 all-gather.4
  74.8 69.6 all-gather.2

commit v5 on v4

--- a/solution.py
+++ b/solution.py
@@ -36,6 +36,10 @@
 
 def in_order(index, own, other):
     return (jnp.where(index == 0, own, other), jnp.where(index == 0, other, own))
+
+
+def opposite(values):
+    return lax.ppermute(values, ("c", "yl"), [(0, 3), (1, 2), (2, 1), (3, 0)])
 
 
 def after(values, *results):
@@ -80,7 +84,7 @@
     up_after = after(w_up, part)
     up_lane = swap(up_after, "yl")
     up_core = swap(up_after, "c")
-    up_both = swap(up_lane, "c")
+    up_both = opposite(up_after)
     up_cat = tiled((w_up, up_core), (up_lane, up_both))
 
     pre_lane = swap(pre_activation, "yl")
@@ -121,14 +125,14 @@
     own = (slopes[:, :hidden], slopes_lane[:, :hidden])
     other = (
         swap(slopes[:, hidden:], "c"),
-        swap(after(slopes_lane[:, hidden:], part_y), "c"),
+        swap(slopes_lane[:, hidden:], "c"),
     )
     by_core = [
         jnp.stack(in_order(lane, *(p.reshape(16, half, hidden) for p in pair)), axis=1)
         for pair in (own, other)
     ]
     slopes_all = jnp.stack(in_order(core, by_core[0], by_core[1]), axis=1)
-    up_grad = over_tokens(input_all, slopes_all.reshape(-1, hidden))
+    up_grad = over_tokens(after(input_all, slopes_lane), slopes_all.reshape(-1, hidden))
     return (input_grad, up_grad, down_grad)
 
 

time: 204 us -> 178 us (0.87)
  waiting for transfers between devices: 50.1 us -> 25.1 us
  blocking collectives: 22.2 us -> 25.3 us
  local copies, waits for them, and re-layouts: 7.45 us -> 5.19 us
    ppermute x13 -> x12, waiting for transfers between devices: 39.7 us -> 21.6 us  [swap(): return lax.ppermute(values, axis, [(0, 1), (1, 0)])]
    ppermute x13 -> x12, starting transfers between devices: 51.4 us -> 45.3 us  [swap(): return lax.ppermute(values, axis, [(0, 1), (1, 0)])]
    all_to_all x1, waiting for transfers between devices: 5.84 us -> 0.36 us  [per_device(): grad_y = lax.all_to_all(pieces.reshape(8, half, width), ('yh', 'yl'), 0, 0)]
    all_to_all x1, waiting for transfers between devices: 3.79 us -> 0.01 us  [per_device(): lax.all_to_all(jnp.broadcast_to(grad_y, (4, 4, half, 2 * width)), 'x', 0, 0)]
    all_gather x1, blocking collectives: 22.2 us -> 25.3 us  [per_device(): slopes = lax.all_gather(slope_tile, 'z', axis=0, tiled=True)]
    ppermute x0 -> x1, starting transfers between devices: none -> 2.98 us  [opposite(): return lax.ppermute(values, ('c', 'yl'), [(0, 3), (1, 2), (2, 1), (3, 0)])]
    all_to_all x1, waiting for transfers between devices: 0.01 us -> 2.43 us  [per_device(): blocks = lax.all_to_all(part.reshape(8, rows, 2 * hidden), 'z', 0, 0)]
    unnamed x9 -> x6, local copies, waits for them, and re-layouts: 3.51 us -> 1.33 us
  transfers between devices with their start and end apart: 20 -> 20, of which waited for: 7 -> 6; matrix products, arithmetic and copies ran while one was open for 13% -> 14% of each run, Pallas kernels for 0% -> 0%
where the time goes in v5:
time: 178 us; the launch traced here: 177 us
  starting transfers between devices  79.4 us (45%)
  blocking collectives  25.3 us (14%)
  waiting for transfers between devices  25.1 us (14%)
  matrix products  16.5 us (9%)
  between operations  14.4 us (8%)
  other arithmetic  11 us (6%)
  local copies, waits for them, and re-layouts  5.19 us (3%)
    ppermute x12, starting transfers between devices, swap(): return lax.ppermute(values, axis, [(0, 1), (1, 0)])  45.3 us
    all_gather x1, blocking collectives, per_device(): slopes = lax.all_gather(slope_tile, 'z', axis=0, tiled=True)  25.3 us
    ppermute x12, waiting for transfers between devices, swap(): return lax.ppermute(values, axis, [(0, 1), (1, 0)])  21.6 us
    dot_general x3, matrix products, times_transposed(): lax.dot_general(left, right, (((1,), (1,)), ((), ())), preferred_element_...  9.13 us
    all_to_all x1, starting transfers between devices, per_device(): blocks = lax.all_to_all(part.reshape(8, rows, 2 * hidden), 'z', 0, 0)  9.03 us
    all_to_all x1, starting transfers between devices, per_device(): grad_y = lax.all_to_all(pieces.reshape(8, half, width), ('yh', 'yl'), 0, 0)  7.65 us
    dot_general x2, matrix products, over_tokens(): lax.dot_general(left, right, (((0,), (0,)), ((), ())), preferred_element_...  7.35 us
    all_to_all x1, starting transfers between devices, per_device(): blocks = lax.all_to_all(part_y.reshape(8, half, width), ('yh', 'yl'), 0, 0)  5.5 us
  transfers between devices with their start and end apart: 20, of which 6 were waited for; matrix products, arithmetic and copies ran while one was open for 14% of the time, Pallas kernels for 0%

profile of v5, /device:TPU:1, one launch (start us, length us, event | category | flops | bytes accessed | tf_op | source)
XLA Modules:
  0.0 176.8 jit_solution(10684168854689640001)
XLA Ops:
  8.7 7.7 %all-to-all-start = ((bf16[8,24,640]{2,1,0:T(8,128)(2,1)}), bf16[8,24,640]{2,1,0:T(8,128)(2,1)S(1)}, u32[]{:S(2)}, u32[]{:S(2)}) async-start(bf16[8,24,640]{2,1,0:T(8,128)(2,1)} %bitcast.1), calls=%async_computation | async-start | bytes 491520 | tf_op jit(solution)/shard_map/all_to_all | solution.py:66
  17.1 4.6 %collective-permute-start = (bf16[640,640]{1,0:T(8,128)(2,1)}, bf16[640,640]{1,0:T(8,128)(2,1)}, u32[]{:S(2)}, u32[]{:S(2)}) collective-permute-start(bf16[640,640]{1,0:T(8,128)(2,1)} %param.9), channel_id=1, source_target_pairs={{0,16},{16,0},{1,17},{17,1},{2,18},{18,2},{3,19},{19,3},{4,20},{20... | collective-permute-start | bytes 2457608 | tf_op jit(solution)/shard_map/ppermute | solution.py:34
  21.7 3.5 %collective-permute-start.1 = (bf16[640,640]{1,0:T(8,128)(2,1)}, bf16[640,640]{1,0:T(8,128)(2,1)}, u32[]{:S(2)}, u32[]{:S(2)}) collective-permute-start(bf16[640,640]{1,0:T(8,128)(2,1)} %param.9), channel_id=1, source_target_pairs={{0,1},{1,0},{2,3},{3,2},{4,5},{5,4},{6,7},{7,6},{8,9},{9,8},{10,11... | collective-permute-start | bytes 2457608 | tf_op jit(solution)/shard_map/ppermute | solution.py:34
  26.7 4.9 %all-to-all-start.1 = ((bf16[4,4,24,1280]{3,2,1,0:T(8,128)(2,1)}), bf16[4,4,24,1280]{3,2,1,0:T(8,128)(2,1)S(1)}, u32[]{:S(2)}, u32[]{:S(2)}) async-start(bf16[4,4,24,1280]{3,2,1,0:T(8,128)(2,1)} %broadcast_in_dim.7), calls=%async_computation.1 | async-start | bytes 1966080 | tf_op jit(solution)/shard_map/all_to_all | solution.py:69
  31.6 12.5 %collective-permute-done.1 = bf16[640,640]{1,0:T(8,128)(2,1)} collective-permute-done((bf16[640,640]{1,0:T(8,128)(2,1)}, bf16[640,640]{1,0:T(8,128)(2,1)}, u32[]{:S(2)}, u32[]{:S(2)}) %collective-permute-start.1) | collective-permute-done | bytes 819232 | tf_op jit(solution)/shard_map/ppermute | solution.py:34
  44.1 2.9 %collective-permute-start.2 = (bf16[640,640]{1,0:T(8,128)(2,1)}, bf16[640,640]{1,0:T(8,128)(2,1)}, u32[]{:S(2)}, u32[]{:S(2)}) collective-permute-start(bf16[640,640]{1,0:T(8,128)(2,1)} %collective-permute-done.1), channel_id=1, source_target_pairs={{0,16},{16,0},{1,17},{17,1},{2,18},{18,2},{3,19},{19,3},{4,20},{20... | collective-permute-start | bytes 2457608 | tf_op jit(solution)/shard_map/ppermute | solution.py:34
  49.2 3.3 %fusion.8 = bf16[384,1280]{1,0:T(8,128)(2,1)} fusion(f32[384,1280]{1,0:T(8,128)S(1)} %fusion.12, bf16[640,640]{1,0:T(8,128)(2,1)} %collective-permute-done.2, bf16[640,640]{1,0:T(8,128)(2,1)} %collective-permute-done.1, bf16[384,1280]{1,0:T(8,128)(2,1)S(1)} %bitcast.89), kind=kOutput, calls=%fused_computation.9 | convolution fusion | flops 633405440 | bytes 5079040 | tf_op jit(solution)/shard_map/dot_general | solution.py:22
  52.5 9.0 %all-to-all-start.2 = ((bf16[8,48,1280]{2,1,0:T(8,128)(2,1)}), bf16[8,48,1280]{2,1,0:T(8,128)(2,1)S(1)}, u32[]{:S(2)}, u32[]{:S(2)}) async-start(bf16[8,48,1280]{2,1,0:T(8,128)(2,1)} %bitcast.11), calls=%async_computation.2 | async-start | bytes 1966080 | tf_op jit(solution)/shard_map/all_to_all | solution.py:82
  61.6 4.1 %collective-permute-start.3 = (bf16[96,640]{1,0:T(8,128)(2,1)S(1)}, bf16[96,640]{1,0:T(8,128)(2,1)S(1)}, u32[]{:S(2)}, u32[]{:S(2)}) collective-permute-start(bf16[96,640]{1,0:T(8,128)(2,1)S(1)} %copy-done.1), channel_id=1, source_target_pairs={{0,1},{1,0},{2,3},{3,2},{4,5},{5,4},{6,7},{7,6},{8,9},{9,8},{10,11... | collective-permute-start | bytes 368648 | tf_op jit(solution)/shard_map/ppermute | solution.py:34
  65.7 3.2 %collective-permute-done.3 = bf16[96,640]{1,0:T(8,128)(2,1)S(1)} collective-permute-done((bf16[96,640]{1,0:T(8,128)(2,1)S(1)}, bf16[96,640]{1,0:T(8,128)(2,1)S(1)}, u32[]{:S(2)}, u32[]{:S(2)}) %collective-permute-start.3) | collective-permute-done | bytes 122912 | tf_op jit(solution)/shard_map/ppermute | solution.py:34
  69.0 6.1 %collective-permute-start.4 = (bf16[2,24,640]{2,1,0:T(8,128)(2,1)S(1)}, bf16[2,24,640]{2,1,0:T(8,128)(2,1)S(1)}, u32[]{:S(2)}, u32[]{:S(2)}) collective-permute-start(bf16[2,24,640]{2,1,0:T(8,128)(2,1)S(1)} %fusion.38), channel_id=1, source_target_pairs={{0,16},{16,0},{1,17},{17,1},{2,18},{18,2},{3,19},{19,3},{4,20},{20... | collective-permute-start | bytes 184328 | tf_op jit(solution)/shard_map/ppermute | solution.py:34
  76.2 3.0 %collective-permute-start.7 = (bf16[640,640]{1,0:T(8,128)(2,1)}, bf16[640,640]{1,0:T(8,128)(2,1)}, u32[]{:S(2)}, u32[]{:S(2)}) collective-permute-start(bf16[640,640]{1,0:T(8,128)(2,1)} %param.8), channel_id=1, source_target_pairs={{0,17},{1,16},{16,1},{17,0},{2,19},{3,18},{18,3},{19,2},{4,21},{5,... | collective-permute-start | bytes 2457608 | tf_op jit(solution)/shard_map/ppermute | solution.py:42
  84.1 2.8 %collective-permute-start.11 = (bf16[4,4,24,640]{3,2,1,0:T(8,128)(2,1)S(1)}, bf16[4,4,24,640]{3,2,1,0:T(8,128)(2,1)}, u32[]{:S(2)}, u32[]{:S(2)}) collective-permute-start(bf16[4,4,24,640]{3,2,1,0:T(8,128)(2,1)S(1)} %slice.81), channel_id=1, source_target_pairs={{0,1},{1,0},{2,3},{3,2},{4,5},{5,4},{6,7},{7,6},{8,9},{9,8},{10,11... | collective-permute-start | bytes 1474568 | tf_op jit(solution)/shard_map/ppermute | solution.py:34
  89.6 25.3 %all_gather.9 = bf16[384,1280]{1,0:T(8,128)(2,1)} all-gather(bf16[48,1280]{1,0:T(8,128)(2,1)S(1)} %fusion.32), channel_id=1, replica_groups=mesh['yh'=4,'x'=4,'c'=2,'z'=8,'yl'=2] {'z'}, dimensions={0}, use_global_device_ids=true | all-gather | bytes 1105920 | tf_op jit(solution)/shard_map/all_gather | solution.py:105
  114.8 4.3 %collective-permute-start.8 = (bf16[384,1280]{1,0:T(8,128)(2,1)}, bf16[384,1280]{1,0:T(8,128)(2,1)}, u32[]{:S(2)}, u32[]{:S(2)}) collective-permute-start(bf16[384,1280]{1,0:T(8,128)(2,1)} %all_gather.9), channel_id=1, source_target_pairs={{0,1},{1,0},{2,3},{3,2},{4,5},{5,4},{6,7},{7,6},{8,9},{9,8},{10,11... | collective-permute-start | bytes 2949128 | tf_op jit(solution)/shard_map/ppermute | solution.py:34
  119.2 3.7 %fusion.9 = bf16[384,1280]{1,0:T(8,128)(2,1)S(1)} fusion(bf16[384,1280]{1,0:T(8,128)(2,1)} %all_gather.9, bf16[640,640]{1,0:T(8,128)(2,1)} %collective-permute-done.7, bf16[640,640]{1,0:T(8,128)(2,1)} %collective-permute-done.6, bf16[640,640]{1,0:T(8,128)(2,1)} %collective-permute-done.5, bf16[640,640]{1,0:T(8,128)(2,1)} %param.8), kind=kOutput, calls=%fused_computation.10 | convolution fusion | flops 1271889920 | bytes 5242880 | tf_op jit(solution)/shard_map/dot_general | solution.py:22
  123.9 3.9 %all-to-all-start.3 = ((bf16[4,4,24,1280]{3,2,1,0:T(8,128)(2,1)}), bf16[4,4,24,1280]{3,2,1,0:T(8,128)(2,1)S(1)}, u32[]{:S(2)}, u32[]{:S(2)}) async-start(bf16[4,4,24,1280]{3,2,1,0:T(8,128)(2,1)} %bitcast.83), calls=%async_computation.3 | async-start | bytes 1966080 | tf_op jit(solution)/shard_map/all_to_all | solution.py:109
  130.0 7.4 %collective-permute-start.12 = (bf16[4,4,2,24,640]{4,3,1,0,2:T(8,128)(2,1)}, bf16[4,4,2,24,640]{4,3,1,0,2:T(8,128)(2,1)}, u32[]{:S(2)}, u32[]{:S(2)}) collective-permute-start(bf16[4,4,2,24,640]{4,3,1,0,2:T(8,128)(2,1)} %pad_maximum_fusion.4), channel_id=1, source_target_pairs={{0,16},{16,0},{1,17},{17,1},{2,18},{18,2},{3,19},{19,3},{4,20},{20... | collective-permute-start | bytes 2949128 | tf_op jit(solution)/shard_map/ppermute | solution.py:34
  138.3 5.5 %all-to-all-start.4 = ((bf16[8,24,640]{2,1,0:T(8,128)(2,1)}), bf16[8,24,640]{2,1,0:T(8,128)(2,1)S(1)}, u32[]{:S(2)}, u32[]{:S(2)}) async-start(bf16[8,24,640]{2,1,0:T(8,128)(2,1)} %bitcast.27), calls=%async_computation.4 | async-start | bytes 491520 | tf_op jit(solution)/shard_map/all_to_all | solution.py:114
  143.9 5.7 %collective-permute-done.8 = bf16[384,1280]{1,0:T(8,128)(2,1)} collective-permute-done((bf16[384,1280]{1,0:T(8,128)(2,1)}, bf16[384,1280]{1,0:T(8,128)(2,1)}, u32[]{:S(2)}, u32[]{:S(2)}) %collective-permute-start.8) | collective-permute-done | bytes 983072 | tf_op jit(solution)/shard_map/ppermute | solution.py:34
  149.6 2.6 %broadcast_select_fusion.5 = (bf16[384,640]{1,0:T(8,128)(2,1)S(1)}, bf16[384,640]{1,0:T(8,128)(2,1)S(1)}, bf16[384,640]{1,0:T(8,128)(2,1)}, bf16[384,640]{1,0:T(8,128)(2,1)}) fusion(pred[]{:T(512)S(6)} %eq.4, bf16[384,1280]{1,0:T(8,128)(2,1)} %collective-permute-done.8, bf16[384,1280]{1,0:T(8,128)(2,1)} %all_gather.9), kind=kLoop, calls=%fused_computation.42 | loop fusion | flops 491520 | bytes 3932161 | tf_op jit(solution)/shard_map/jit(_where)/select_n | solution.py:38
  152.1 2.9 %collective-permute-start.9 = (bf16[384,640]{1,0:T(8,128)(2,1)}, bf16[384,640]{1,0:T(8,128)(2,1)}, u32[]{:S(2)}, u32[]{:S(2)}) collective-permute-start(bf16[384,640]{1,0:T(8,128)(2,1)} %get-tuple-element.23), channel_id=1, source_target_pairs={{0,16},{16,0},{1,17},{17,1},{2,18},{18,2},{3,19},{19,3},{4,20},{20... | collective-permute-start | bytes 1474568 | tf_op jit(solution)/shard_map/ppermute | solution.py:34
  158.9 4.4 %fusion.44 = f32[640,640]{1,0:T(8,128)} fusion(bf16[1536,640]{1,0:T(8,128)(2,1)} %all-gather.5.cloned.1.call-done, bf16[1536,640]{1,0:T(8,128)(2,1)S(1)} %bitcast.86), kind=kOutput, calls=%fused_computation.83 | convolution fusion | flops 1258291200 | bytes 5570560 | tf_op jit(solution)/shard_map/dot_general | solution.py:28
  167.1 2.9 %fusion.43 = f32[640,640]{1,0:T(8,128)} fusion(bf16[1536,640]{1,0:T(8,128)(2,1)S(1)} %copy-done, bf16[1536,640]{1,0:T(8,128)(2,1)S(1)} %bitcast.87), kind=kOutput, calls=%fused_computation.82 | convolution fusion | flops 1258291200 | bytes 5570560 | tf_op jit(solution)/shard_map/dot_general | solution.py:28
  (60 shorter events, 26.3 us)
Async XLA Ops:
  8.7 16.9 %all-to-all-start = ((bf16[8,24,640]{2,1,0:T(8,128)(2,1)}), bf16[8,24,640]{2,1,0:T(8,128)(2,1)S(1)}, u32[]{:S(2)}, u32[]{:S(2)}) async-start(bf16[8,24,640]{2,1,0:T(8,128)(2,1)} %bitcast.1), calls=%async_computation | async-start | bytes 491520 | tf_op jit(solution)/shard_map/all_to_all | solution.py:66
  16.4 127.5 %all-gather.3.cloned.1.call-start = ((), (), s32[]{:S(2)}) async-start(), calls=%async_computation.5 | async-start | bytes 2027520 | tf_op jit(solution)/shard_map/all_gather | solution.py:61
  17.1 29.9 %collective-permute-start = (bf16[640,640]{1,0:T(8,128)(2,1)}, bf16[640,640]{1,0:T(8,128)(2,1)}, u32[]{:S(2)}, u32[]{:S(2)}) collective-permute-start(bf16[640,640]{1,0:T(8,128)(2,1)} %param.9), channel_id=1, source_target_pairs={{0,16},{16,0},{1,17},{17,1},{2,18},{18,2},{3,19},{19,3},{4,20},{20... | collective-permute-start | bytes 2457608 | tf_op jit(solution)/shard_map/ppermute | solution.py:34
  21.7 22.4 %collective-permute-start.1 = (bf16[640,640]{1,0:T(8,128)(2,1)}, bf16[640,640]{1,0:T(8,128)(2,1)}, u32[]{:S(2)}, u32[]{:S(2)}) collective-permute-start(bf16[640,640]{1,0:T(8,128)(2,1)} %param.9), channel_id=1, source_target_pairs={{0,1},{1,0},{2,3},{3,2},{4,5},{5,4},{6,7},{7,6},{8,9},{9,8},{10,11... | collective-permute-start | bytes 2457608 | tf_op jit(solution)/shard_map/ppermute | solution.py:34
  26.7 20.4 %copy-start.2 = (bf16[640,640]{1,0:T(8,128)(2,1)S(1)}, bf16[640,640]{1,0:T(8,128)(2,1)}, u32[]{:S(2)}) copy-start(bf16[640,640]{1,0:T(8,128)(2,1)} %param.9) | copy-start | bytes 2457604
  26.7 20.3 %all-to-all-start.1 = ((bf16[4,4,24,1280]{3,2,1,0:T(8,128)(2,1)}), bf16[4,4,24,1280]{3,2,1,0:T(8,128)(2,1)S(1)}, u32[]{:S(2)}, u32[]{:S(2)}) async-start(bf16[4,4,24,1280]{3,2,1,0:T(8,128)(2,1)} %broadcast_in_dim.7), calls=%async_computation.1 | async-start | bytes 1966080 | tf_op jit(solution)/shard_map/all_to_all | solution.py:69
  44.1 5.2 %collective-permute-start.2 = (bf16[640,640]{1,0:T(8,128)(2,1)}, bf16[640,640]{1,0:T(8,128)(2,1)}, u32[]{:S(2)}, u32[]{:S(2)}) collective-permute-start(bf16[640,640]{1,0:T(8,128)(2,1)} %collective-permute-done.1), channel_id=1, source_target_pairs={{0,16},{16,0},{1,17},{17,1},{2,18},{18,2},{3,19},{19,3},{4,20},{20... | collective-permute-start | bytes 2457608 | tf_op jit(solution)/shard_map/ppermute | solution.py:34
  52.5 9.1 %copy-start.1 = (bf16[96,640]{1,0:T(8,128)(2,1)S(1)}, bf16[96,640]{1,0:T(8,128)(2,1)}, u32[]{:S(2)}) copy-start(bf16[96,640]{1,0:T(8,128)(2,1)} %param.7) | copy-start | bytes 368644
  52.5 36.8 %all-to-all-start.2 = ((bf16[8,48,1280]{2,1,0:T(8,128)(2,1)}), bf16[8,48,1280]{2,1,0:T(8,128)(2,1)S(1)}, u32[]{:S(2)}, u32[]{:S(2)}) async-start(bf16[8,48,1280]{2,1,0:T(8,128)(2,1)} %bitcast.11), calls=%async_computation.2 | async-start | bytes 1966080 | tf_op jit(solution)/shard_map/all_to_all | solution.py:82
  61.6 97.3 %all-gather.5.cloned.1.call-start = ((), (), s32[]{:S(2)}) async-start(), calls=%async_computation.6 | async-start | bytes 2211840 | tf_op jit(solution)/shard_map/all_gather | solution.py:101
  61.6 7.3 %collective-permute-start.3 = (bf16[96,640]{1,0:T(8,128)(2,1)S(1)}, bf16[96,640]{1,0:T(8,128)(2,1)S(1)}, u32[]{:S(2)}, u32[]{:S(2)}) collective-permute-start(bf16[96,640]{1,0:T(8,128)(2,1)S(1)} %copy-done.1), channel_id=1, source_target_pairs={{0,1},{1,0},{2,3},{3,2},{4,5},{5,4},{6,7},{7,6},{8,9},{9,8},{10,11... | collective-permute-start | bytes 368648 | tf_op jit(solution)/shard_map/ppermute | solution.py:34
  69.0 7.0 %collective-permute-start.4 = (bf16[2,24,640]{2,1,0:T(8,128)(2,1)S(1)}, bf16[2,24,640]{2,1,0:T(8,128)(2,1)S(1)}, u32[]{:S(2)}, u32[]{:S(2)}) collective-permute-start(bf16[2,24,640]{2,1,0:T(8,128)(2,1)S(1)} %fusion.38), channel_id=1, source_target_pairs={{0,16},{16,0},{1,17},{17,1},{2,18},{18,2},{3,19},{19,3},{4,20},{20... | collective-permute-start | bytes 184328 | tf_op jit(solution)/shard_map/ppermute | solution.py:34
  76.2 43.0 %collective-permute-start.7 = (bf16[640,640]{1,0:T(8,128)(2,1)}, bf16[640,640]{1,0:T(8,128)(2,1)}, u32[]{:S(2)}, u32[]{:S(2)}) collective-permute-start(bf16[640,640]{1,0:T(8,128)(2,1)} %param.8), channel_id=1, source_target_pairs={{0,17},{1,16},{16,1},{17,0},{2,19},{3,18},{18,3},{19,2},{4,21},{5,... | collective-permute-start | bytes 2457608 | tf_op jit(solution)/shard_map/ppermute | solution.py:42
  79.2 40.0 %collective-permute-start.6 = (bf16[640,640]{1,0:T(8,128)(2,1)}, bf16[640,640]{1,0:T(8,128)(2,1)}, u32[]{:S(2)}, u32[]{:S(2)}) collective-permute-start(bf16[640,640]{1,0:T(8,128)(2,1)} %param.8), channel_id=1, source_target_pairs={{0,1},{1,0},{2,3},{3,2},{4,5},{5,4},{6,7},{7,6},{8,9},{9,8},{10,11... | collective-permute-start | bytes 2457608 | tf_op jit(solution)/shard_map/ppermute | solution.py:34
  81.6 37.5 %collective-permute-start.5 = (bf16[640,640]{1,0:T(8,128)(2,1)}, bf16[640,640]{1,0:T(8,128)(2,1)}, u32[]{:S(2)}, u32[]{:S(2)}) collective-permute-start(bf16[640,640]{1,0:T(8,128)(2,1)} %param.8), channel_id=1, source_target_pairs={{0,16},{16,0},{1,17},{17,1},{2,18},{18,2},{3,19},{19,3},{4,20},{20... | collective-permute-start | bytes 2457608 | tf_op jit(solution)/shard_map/ppermute | solution.py:34
  84.1 43.8 %collective-permute-start.11 = (bf16[4,4,24,640]{3,2,1,0:T(8,128)(2,1)S(1)}, bf16[4,4,24,640]{3,2,1,0:T(8,128)(2,1)}, u32[]{:S(2)}, u32[]{:S(2)}) collective-permute-start(bf16[4,4,24,640]{3,2,1,0:T(8,128)(2,1)S(1)} %slice.81), channel_id=1, source_target_pairs={{0,1},{1,0},{2,3},{3,2},{4,5},{5,4},{6,7},{7,6},{8,9},{9,8},{10,11... | collective-permute-start | bytes 1474568 | tf_op jit(solution)/shard_map/ppermute | solution.py:34
  114.8 34.7 %collective-permute-start.8 = (bf16[384,1280]{1,0:T(8,128)(2,1)}, bf16[384,1280]{1,0:T(8,128)(2,1)}, u32[]{:S(2)}, u32[]{:S(2)}) collective-permute-start(bf16[384,1280]{1,0:T(8,128)(2,1)} %all_gather.9), channel_id=1, source_target_pairs={{0,1},{1,0},{2,3},{3,2},{4,5},{5,4},{6,7},{7,6},{8,9},{9,8},{10,11... | collective-permute-start | bytes 2949128 | tf_op jit(solution)/shard_map/ppermute | solution.py:34
  123.9 13.5 %all-to-all-start.3 = ((bf16[4,4,24,1280]{3,2,1,0:T(8,128)(2,1)}), bf16[4,4,24,1280]{3,2,1,0:T(8,128)(2,1)S(1)}, u32[]{:S(2)}, u32[]{:S(2)}) async-start(bf16[4,4,24,1280]{3,2,1,0:T(8,128)(2,1)} %bitcast.83), calls=%async_computation.3 | async-start | bytes 1966080 | tf_op jit(solution)/shard_map/all_to_all | solution.py:109
  130.0 27.0 %collective-permute-start.12 = (bf16[4,4,2,24,640]{4,3,1,0,2:T(8,128)(2,1)}, bf16[4,4,2,24,640]{4,3,1,0,2:T(8,128)(2,1)}, u32[]{:S(2)}, u32[]{:S(2)}) collective-permute-start(bf16[4,4,2,24,640]{4,3,1,0,2:T(8,128)(2,1)} %pad_maximum_fusion.4), channel_id=1, source_target_pairs={{0,16},{16,0},{1,17},{17,1},{2,18},{18,2},{3,19},{19,3},{4,20},{20... | collective-permute-start | bytes 2949128 | tf_op jit(solution)/shard_map/ppermute | solution.py:34
  138.3 25.0 %all-to-all-start.4 = ((bf16[8,24,640]{2,1,0:T(8,128)(2,1)}), bf16[8,24,640]{2,1,0:T(8,128)(2,1)S(1)}, u32[]{:S(2)}, u32[]{:S(2)}) async-start(bf16[8,24,640]{2,1,0:T(8,128)(2,1)} %bitcast.27), calls=%async_computation.4 | async-start | bytes 491520 | tf_op jit(solution)/shard_map/all_to_all | solution.py:114
  152.1 11.8 %collective-permute-start.9 = (bf16[384,640]{1,0:T(8,128)(2,1)}, bf16[384,640]{1,0:T(8,128)(2,1)}, u32[]{:S(2)}, u32[]{:S(2)}) collective-permute-start(bf16[384,640]{1,0:T(8,128)(2,1)} %get-tuple-element.23), channel_id=1, source_target_pairs={{0,16},{16,0},{1,17},{17,1},{2,18},{18,2},{3,19},{19,3},{4,20},{20... | collective-permute-start | bytes 1474568 | tf_op jit(solution)/shard_map/ppermute | solution.py:34
  155.1 8.9 %collective-permute-start.10 = (bf16[384,640]{1,0:T(8,128)(2,1)}, bf16[384,640]{1,0:T(8,128)(2,1)}, u32[]{:S(2)}, u32[]{:S(2)}) collective-permute-start(bf16[384,640]{1,0:T(8,128)(2,1)} %get-tuple-element.24), channel_id=1, source_target_pairs={{0,16},{16,0},{1,17},{17,1},{2,18},{18,2},{3,19},{19,3},{4,20},{20... | collective-permute-start | bytes 1474568 | tf_op jit(solution)/shard_map/ppermute | solution.py:34
  165.5 1.5 copy-start
Sparse Core Ops, SparseCore 0:
  20.4 65.9 all-gather.2
  88.4 40.4 all-gather.4

commit v6 on v5

--- a/solution.py
+++ b/solution.py
@@ -104,22 +104,23 @@
     slope_tile = (act_grad * slope_factor).astype(BF16)
     slopes = lax.all_gather(slope_tile, "z", axis=0, tiled=True)
 
+    grad_own, grad_pair = grad_xy[..., :width], grad_xy[..., width:]
+    grad_lane = swap(after(grad_pair, part), "yl")
+    grad_core = jnp.stack(in_order(lane, grad_own, grad_lane), axis=2)
+    grad_other = swap(grad_core, "c")
+    grad_all = jnp.stack(in_order(core, grad_core, grad_other), axis=2)
+    down_grad = over_tokens(act_all, after(grad_all, input_all).reshape(-1, width))
+
     part_in = times_transposed(slopes, up_cat).astype(BF16)
     part_in = jnp.swapaxes(part_in.reshape(4, 4, half, 2 * width), 0, 1)
     blocks = lax.all_to_all(part_in, "x", 0, 0)
+    blocks = after(blocks, down_grad)
     part_y = jnp.sum(blocks.astype(F32), axis=0).astype(BF16)
     part_y = jnp.stack(
         in_order(lane, part_y[..., :width], part_y[..., width:]), axis=1
     )
     blocks = lax.all_to_all(part_y.reshape(8, half, width), ("yh", "yl"), 0, 0)
     input_grad = jnp.sum(blocks.reshape(4, rows, width).astype(F32), axis=0).astype(BF16)
-
-    grad_own, grad_pair = grad_xy[..., :width], grad_xy[..., width:]
-    grad_lane = swap(after(grad_pair, part), "yl")
-    grad_core = jnp.stack(in_order(lane, grad_own, grad_lane), axis=2)
-    grad_other = swap(after(grad_core, slopes), "c")
-    grad_all = jnp.stack(in_order(core, grad_core, grad_other), axis=2)
-    down_grad = over_tokens(act_all, grad_all.reshape(-1, width))
 
     slopes_lane = swap(slopes, "yl")
     own = (slopes[:, :hidden], slopes_lane[:, :hidden])

time: 178 us -> 180 us (1.011)
  waiting for transfers between devices: 25.1 us -> 30.5 us
  starting transfers between devices: 79.4 us -> 75.4 us
  other arithmetic: 11 us -> 7.8 us
    all_to_all x1, waiting for transfers between devices: 2.43 us -> 7.37 us  [per_device(): blocks = lax.all_to_all(part.reshape(8, rows, 2 * hidden), 'z', 0, 0)]
    ppermute x12, starting transfers between devices: 45.3 us -> 41.2 us  [swap(): return lax.ppermute(values, axis, [(0, 1), (1, 0)])]
    select_n x4, other arithmetic: 4.15 us -> 2.02 us  [in_order(): jnp.where(index == 0, own, other)]
  transfers between devices with their start and end apart: 20 -> 20, of which waited for: 6 -> 7; matrix products, arithmetic and copies ran while one was open for 14% -> 15% of each run, Pallas kernels for 0% -> 0%
where the time goes in v6:
time: 180 us; the launch traced here: 178 us
  starting transfers between devices  75.4 us (42%)
  waiting for transfers between devices  30.5 us (17%)
  blocking collectives  26.1 us (14%)
  matrix products  17 us (9%)
  between operations  14.4 us (8%)
  other arithmetic  7.8 us (4%)
  local copies, waits for them, and re-layouts  6.47 us (4%)
    ppermute x12, starting transfers between devices, swap(): return lax.ppermute(values, axis, [(0, 1), (1, 0)])  41.2 us
    all_gather x1, blocking collectives, per_device(): slopes = lax.all_gather(slope_tile, 'z', axis=0, tiled=True)  26.1 us
    ppermute x12, waiting for transfers between devices, swap(): return lax.ppermute(values, axis, [(0, 1), (1, 0)])  20 us
    dot_general x3, matrix products, times_transposed(): lax.dot_general(left, right, (((1,), (1,)), ((), ())), preferred_element_...  9.09 us
    all_to_all x1, starting transfers between devices, per_device(): blocks = lax.all_to_all(part.reshape(8, rows, 2 * hidden), 'z', 0, 0)  8.67 us
    dot_general x2, matrix products, over_tokens(): lax.dot_general(left, right, (((0,), (0,)), ((), ())), preferred_element_...  7.94 us
    all_to_all x1, starting transfers between devices, per_device(): grad_y = lax.all_to_all(pieces.reshape(8, half, width), ('yh', 'yl'), 0, 0)  7.65 us
    all_to_all x1, waiting for transfers between devices, per_device(): blocks = lax.all_to_all(part.reshape(8, rows, 2 * hidden), 'z', 0, 0)  7.37 us
  transfers between devices with their start and end apart: 20, of which 7 were waited for; matrix products, arithmetic and copies ran while one was open for 15% of the time, Pallas kernels for 0%

profile of v6, /device:TPU:1, one launch (start us, length us, event | category | flops | bytes accessed | tf_op | source)
XLA Modules:
  0.0 177.6 jit_solution(13815473109675175334)
XLA Ops:
  9.4 7.7 %all-to-all-start = ((bf16[8,24,640]{2,1,0:T(8,128)(2,1)}), bf16[8,24,640]{2,1,0:T(8,128)(2,1)S(1)}, u32[]{:S(2)}, u32[]{:S(2)}) async-start(bf16[8,24,640]{2,1,0:T(8,128)(2,1)} %bitcast.1), calls=%async_computation | async-start | bytes 491520 | tf_op jit(solution)/shard_map/all_to_all | solution.py:66
  17.1 4.6 %collective-permute-start = (bf16[640,640]{1,0:T(8,128)(2,1)}, bf16[640,640]{1,0:T(8,128)(2,1)}, u32[]{:S(2)}, u32[]{:S(2)}) collective-permute-start(bf16[640,640]{1,0:T(8,128)(2,1)} %param.9), channel_id=1, source_target_pairs={{0,16},{16,0},{1,17},{17,1},{2,18},{18,2},{3,19},{19,3},{4,20},{20... | collective-permute-start | bytes 2457608 | tf_op jit(solution)/shard_map/ppermute | solution.py:34
  21.7 3.5 %collective-permute-start.1 = (bf16[640,640]{1,0:T(8,128)(2,1)}, bf16[640,640]{1,0:T(8,128)(2,1)}, u32[]{:S(2)}, u32[]{:S(2)}) collective-permute-start(bf16[640,640]{1,0:T(8,128)(2,1)} %param.9), channel_id=1, source_target_pairs={{0,1},{1,0},{2,3},{3,2},{4,5},{5,4},{6,7},{7,6},{8,9},{9,8},{10,11... | collective-permute-start | bytes 2457608 | tf_op jit(solution)/shard_map/ppermute | solution.py:34
  27.4 4.9 %all-to-all-start.1 = ((bf16[4,4,24,1280]{3,2,1,0:T(8,128)(2,1)}), bf16[4,4,24,1280]{3,2,1,0:T(8,128)(2,1)S(1)}, u32[]{:S(2)}, u32[]{:S(2)}) async-start(bf16[4,4,24,1280]{3,2,1,0:T(8,128)(2,1)} %broadcast_in_dim.7), calls=%async_computation.1 | async-start | bytes 1966080 | tf_op jit(solution)/shard_map/all_to_all | solution.py:69
  32.3 14.4 %collective-permute-done.1 = bf16[640,640]{1,0:T(8,128)(2,1)} collective-permute-done((bf16[640,640]{1,0:T(8,128)(2,1)}, bf16[640,640]{1,0:T(8,128)(2,1)}, u32[]{:S(2)}, u32[]{:S(2)}) %collective-permute-start.1) | collective-permute-done | bytes 819232 | tf_op jit(solution)/shard_map/ppermute | solution.py:34
  46.7 2.3 %collective-permute-start.2 = (bf16[640,640]{1,0:T(8,128)(2,1)}, bf16[640,640]{1,0:T(8,128)(2,1)}, u32[]{:S(2)}, u32[]{:S(2)}) collective-permute-start(bf16[640,640]{1,0:T(8,128)(2,1)} %collective-permute-done.1), channel_id=1, source_target_pairs={{0,16},{16,0},{1,17},{17,1},{2,18},{18,2},{3,19},{19,3},{4,20},{20... | collective-permute-start | bytes 2457608 | tf_op jit(solution)/shard_map/ppermute | solution.py:34
  49.1 3.1 %collective-permute-start.3 = (bf16[96,640]{1,0:T(8,128)(2,1)S(1)}, bf16[96,640]{1,0:T(8,128)(2,1)S(1)}, u32[]{:S(2)}, u32[]{:S(2)}) collective-permute-start(bf16[96,640]{1,0:T(8,128)(2,1)S(1)} %copy-done.1), channel_id=1, source_target_pairs={{0,1},{1,0},{2,3},{3,2},{4,5},{5,4},{6,7},{7,6},{8,9},{9,8},{10,11... | collective-permute-start | bytes 368648 | tf_op jit(solution)/shard_map/ppermute | solution.py:34
  52.2 3.6 %collective-permute-done.3 = bf16[96,640]{1,0:T(8,128)(2,1)S(1)} collective-permute-done((bf16[96,640]{1,0:T(8,128)(2,1)S(1)}, bf16[96,640]{1,0:T(8,128)(2,1)S(1)}, u32[]{:S(2)}, u32[]{:S(2)}) %collective-permute-start.3) | collective-permute-done | bytes 122912 | tf_op jit(solution)/shard_map/ppermute | solution.py:34
  58.1 3.3 %fusion.8 = bf16[384,1280]{1,0:T(8,128)(2,1)} fusion(f32[384,1280]{1,0:T(8,128)S(1)} %fusion.12, bf16[640,640]{1,0:T(8,128)(2,1)} %collective-permute-done.2, bf16[640,640]{1,0:T(8,128)(2,1)} %collective-permute-done.1, bf16[384,1280]{1,0:T(8,128)(2,1)S(1)} %bitcast.89), kind=kOutput, calls=%fused_computation.9 | convolution fusion | flops 633405440 | bytes 5079040 | tf_op jit(solution)/shard_map/dot_general | solution.py:22
  61.4 8.7 %all-to-all-start.2 = ((bf16[8,48,1280]{2,1,0:T(8,128)(2,1)}), bf16[8,48,1280]{2,1,0:T(8,128)(2,1)S(1)}, u32[]{:S(2)}, u32[]{:S(2)}) async-start(bf16[8,48,1280]{2,1,0:T(8,128)(2,1)} %bitcast.11), calls=%async_computation.2 | async-start | bytes 1966080 | tf_op jit(solution)/shard_map/all_to_all | solution.py:82
  71.1 3.2 %collective-permute-start.8 = (bf16[4,4,24,640]{3,2,1,0:T(8,128)(2,1)S(1)}, bf16[4,4,24,640]{3,2,1,0:T(8,128)(2,1)S(1)}, u32[]{:S(2)}, u32[]{:S(2)}) collective-permute-start(bf16[4,4,24,640]{3,2,1,0:T(8,128)(2,1)S(1)} %slice.75), channel_id=1, source_target_pairs={{0,1},{1,0},{2,3},{3,2},{4,5},{5,4},{6,7},{7,6},{8,9},{9,8},{10,11... | collective-permute-start | bytes 1474568 | tf_op jit(solution)/shard_map/ppermute | solution.py:34
  74.4 3.1 %collective-permute-start.4 = (bf16[2,24,640]{2,1,0:T(8,128)(2,1)S(1)}, bf16[2,24,640]{2,1,0:T(8,128)(2,1)S(1)}, u32[]{:S(2)}, u32[]{:S(2)}) collective-permute-start(bf16[2,24,640]{2,1,0:T(8,128)(2,1)S(1)} %fusion.38), channel_id=1, source_target_pairs={{0,16},{16,0},{1,17},{17,1},{2,18},{18,2},{3,19},{19,3},{4,20},{20... | collective-permute-start | bytes 184328 | tf_op jit(solution)/shard_map/ppermute | solution.py:34
  78.4 2.3 %collective-permute-start.5 = (bf16[640,640]{1,0:T(8,128)(2,1)}, bf16[640,640]{1,0:T(8,128)(2,1)}, u32[]{:S(2)}, u32[]{:S(2)}) collective-permute-start(bf16[640,640]{1,0:T(8,128)(2,1)} %param.8), channel_id=1, source_target_pairs={{0,16},{16,0},{1,17},{17,1},{2,18},{18,2},{3,19},{19,3},{4,20},{20... | collective-permute-start | bytes 2457608 | tf_op jit(solution)/shard_map/ppermute | solution.py:34
  82.6 3.7 %collective-permute-start.7 = (bf16[640,640]{1,0:T(8,128)(2,1)}, bf16[640,640]{1,0:T(8,128)(2,1)}, u32[]{:S(2)}, u32[]{:S(2)}) collective-permute-start(bf16[640,640]{1,0:T(8,128)(2,1)} %param.8), channel_id=1, source_target_pairs={{0,17},{1,16},{16,1},{17,0},{2,19},{3,18},{18,3},{19,2},{4,21},{5,... | collective-permute-start | bytes 2457608 | tf_op jit(solution)/shard_map/ppermute | solution.py:42
  87.5 3.0 %collective-permute-start.9 = (bf16[4,4,2,24,640]{4,3,1,0,2:T(8,128)(2,1)}, bf16[4,4,2,24,640]{4,3,1,0,2:T(8,128)(2,1)}, u32[]{:S(2)}, u32[]{:S(2)}) collective-permute-start(bf16[4,4,2,24,640]{4,3,1,0,2:T(8,128)(2,1)} %pad_maximum_fusion.2), channel_id=1, source_target_pairs={{0,16},{16,0},{1,17},{17,1},{2,18},{18,2},{3,19},{19,3},{4,20},{20... | collective-permute-start | bytes 2949128 | tf_op jit(solution)/shard_map/ppermute | solution.py:34
  90.5 7.4 %all-to-all-done.2 = bf16[8,48,1280]{2,1,0:T(8,128)(2,1)S(1)} async-done(((bf16[8,48,1280]{2,1,0:T(8,128)(2,1)}), bf16[8,48,1280]{2,1,0:T(8,128)(2,1)S(1)}, u32[]{:S(2)}, u32[]{:S(2)}) %all-to-all-start.2) | async-done | bytes 983072 | tf_op jit(solution)/shard_map/all_to_all | solution.py:82
  98.2 26.1 %all_gather.9 = bf16[384,1280]{1,0:T(8,128)(2,1)} all-gather(bf16[48,1280]{1,0:T(8,128)(2,1)S(1)} %fusion.32), channel_id=1, replica_groups=mesh['yh'=4,'x'=4,'c'=2,'z'=8,'yl'=2] {'z'}, dimensions={0}, use_global_device_ids=true | all-gather | bytes 1105920 | tf_op jit(solution)/shard_map/all_gather | solution.py:105
  124.2 3.1 %collective-permute-start.10 = (bf16[384,1280]{1,0:T(8,128)(2,1)}, bf16[384,1280]{1,0:T(8,128)(2,1)}, u32[]{:S(2)}, u32[]{:S(2)}) collective-permute-start(bf16[384,1280]{1,0:T(8,128)(2,1)} %all_gather.9), channel_id=1, source_target_pairs={{0,1},{1,0},{2,3},{3,2},{4,5},{5,4},{6,7},{7,6},{8,9},{9,8},{10,11... | collective-permute-start | bytes 2949128 | tf_op jit(solution)/shard_map/ppermute | solution.py:34
  127.3 3.6 %fusion.9 = bf16[384,1280]{1,0:T(8,128)(2,1)S(1)} fusion(bf16[384,1280]{1,0:T(8,128)(2,1)} %all_gather.9, bf16[640,640]{1,0:T(8,128)(2,1)} %collective-permute-done.7, bf16[640,640]{1,0:T(8,128)(2,1)} %collective-permute-done.6, bf16[640,640]{1,0:T(8,128)(2,1)} %collective-permute-done.5, bf16[640,640]{1,0:T(8,128)(2,1)} %param.8), kind=kOutput, calls=%fused_computation.10 | convolution fusion | flops 1271889920 | bytes 5242880 | tf_op jit(solution)/shard_map/dot_general | solution.py:22
  132.0 4.1 %all-to-all-start.3 = ((bf16[4,4,24,1280]{3,2,1,0:T(8,128)(2,1)}), bf16[4,4,24,1280]{3,2,1,0:T(8,128)(2,1)S(1)}, u32[]{:S(2)}, u32[]{:S(2)}) async-start(bf16[4,4,24,1280]{3,2,1,0:T(8,128)(2,1)} %bitcast.83), calls=%async_computation.3 | async-start | bytes 1966080 | tf_op jit(solution)/shard_map/all_to_all | solution.py:116
  139.3 5.0 %fusion.43 = f32[640,640]{1,0:T(8,128)} fusion(bf16[1536,640]{1,0:T(8,128)(2,1)} %all-gather.3.cloned.1.call-done, bf16[1536,640]{1,0:T(8,128)(2,1)} %bitcast.86), kind=kOutput, calls=%fused_computation.82 | convolution fusion | flops 1258291200 | bytes 5570560 | tf_op jit(solution)/shard_map/dot_general | solution.py:28
  146.5 5.0 %all-to-all-start.4 = ((bf16[8,24,640]{2,1,0:T(8,128)(2,1)}), bf16[8,24,640]{2,1,0:T(8,128)(2,1)S(1)}, u32[]{:S(2)}, u32[]{:S(2)}) async-start(bf16[8,24,640]{2,1,0:T(8,128)(2,1)} %bitcast.36), calls=%async_computation.4 | async-start | bytes 491520 | tf_op jit(solution)/shard_map/all_to_all | solution.py:122
  153.1 9.1 %collective-permute-start.11 = (bf16[384,640]{1,0:T(8,128)(2,1)S(1)}, bf16[384,640]{1,0:T(8,128)(2,1)S(1)}, u32[]{:S(2)}, u32[]{:S(2)}) collective-permute-start(bf16[384,640]{1,0:T(8,128)(2,1)S(1)} %get-tuple-element.23), channel_id=1, source_target_pairs={{0,16},{16,0},{1,17},{17,1},{2,18},{18,2},{3,19},{19,3},{4,20},{20... | collective-permute-start | bytes 1474568 | tf_op jit(solution)/shard_map/ppermute | solution.py:34
  167.9 2.9 %fusion.44 = f32[640,640]{1,0:T(8,128)} fusion(bf16[1536,640]{1,0:T(8,128)(2,1)S(1)} %copy-done, bf16[1536,640]{1,0:T(8,128)(2,1)S(1)} %bitcast.87), kind=kOutput, calls=%fused_computation.83 | convolution fusion | flops 1258291200 | bytes 5570560 | tf_op jit(solution)/shard_map/dot_general | solution.py:28
  (60 shorter events, 25.4 us)
Async XLA Ops:
  7.2 130.6 %all-gather.5.cloned.1.call-start = ((), (), s32[]{:S(2)}) async-start(), calls=%async_computation.6 | async-start | bytes 2027520 | tf_op jit(solution)/shard_map/all_gather | solution.py:61
  9.4 16.9 %all-to-all-start = ((bf16[8,24,640]{2,1,0:T(8,128)(2,1)}), bf16[8,24,640]{2,1,0:T(8,128)(2,1)S(1)}, u32[]{:S(2)}, u32[]{:S(2)}) async-start(bf16[8,24,640]{2,1,0:T(8,128)(2,1)} %bitcast.1), calls=%async_computation | async-start | bytes 491520 | tf_op jit(solution)/shard_map/all_to_all | solution.py:66
  17.1 38.9 %collective-permute-start = (bf16[640,640]{1,0:T(8,128)(2,1)}, bf16[640,640]{1,0:T(8,128)(2,1)}, u32[]{:S(2)}, u32[]{:S(2)}) collective-permute-start(bf16[640,640]{1,0:T(8,128)(2,1)} %param.9), channel_id=1, source_target_pairs={{0,16},{16,0},{1,17},{17,1},{2,18},{18,2},{3,19},{19,3},{4,20},{20... | collective-permute-start | bytes 2457608 | tf_op jit(solution)/shard_map/ppermute | solution.py:34
  21.7 25.1 %collective-permute-start.1 = (bf16[640,640]{1,0:T(8,128)(2,1)}, bf16[640,640]{1,0:T(8,128)(2,1)}, u32[]{:S(2)}, u32[]{:S(2)}) collective-permute-start(bf16[640,640]{1,0:T(8,128)(2,1)} %param.9), channel_id=1, source_target_pairs={{0,1},{1,0},{2,3},{3,2},{4,5},{5,4},{6,7},{7,6},{8,9},{9,8},{10,11... | collective-permute-start | bytes 2457608 | tf_op jit(solution)/shard_map/ppermute | solution.py:34
  26.3 22.7 %copy-start.1 = (bf16[96,640]{1,0:T(8,128)(2,1)S(1)}, bf16[96,640]{1,0:T(8,128)(2,1)}, u32[]{:S(2)}) copy-start(bf16[96,640]{1,0:T(8,128)(2,1)} %param.7) | copy-start | bytes 368644
  27.4 28.6 %copy-start.2 = (bf16[640,640]{1,0:T(8,128)(2,1)S(1)}, bf16[640,640]{1,0:T(8,128)(2,1)}, u32[]{:S(2)}) copy-start(bf16[640,640]{1,0:T(8,128)(2,1)} %param.9) | copy-start | bytes 2457604
  27.4 28.5 %all-to-all-start.1 = ((bf16[4,4,24,1280]{3,2,1,0:T(8,128)(2,1)}), bf16[4,4,24,1280]{3,2,1,0:T(8,128)(2,1)S(1)}, u32[]{:S(2)}, u32[]{:S(2)}) async-start(bf16[4,4,24,1280]{3,2,1,0:T(8,128)(2,1)} %broadcast_in_dim.7), calls=%async_computation.1 | async-start | bytes 1966080 | tf_op jit(solution)/shard_map/all_to_all | solution.py:69
  46.7 11.4 %collective-permute-start.2 = (bf16[640,640]{1,0:T(8,128)(2,1)}, bf16[640,640]{1,0:T(8,128)(2,1)}, u32[]{:S(2)}, u32[]{:S(2)}) collective-permute-start(bf16[640,640]{1,0:T(8,128)(2,1)} %collective-permute-done.1), channel_id=1, source_target_pairs={{0,16},{16,0},{1,17},{17,1},{2,18},{18,2},{3,19},{19,3},{4,20},{20... | collective-permute-start | bytes 2457608 | tf_op jit(solution)/shard_map/ppermute | solution.py:34
  49.1 6.8 %collective-permute-start.3 = (bf16[96,640]{1,0:T(8,128)(2,1)S(1)}, bf16[96,640]{1,0:T(8,128)(2,1)S(1)}, u32[]{:S(2)}, u32[]{:S(2)}) collective-permute-start(bf16[96,640]{1,0:T(8,128)(2,1)S(1)} %copy-done.1), channel_id=1, source_target_pairs={{0,1},{1,0},{2,3},{3,2},{4,5},{5,4},{6,7},{7,6},{8,9},{9,8},{10,11... | collective-permute-start | bytes 368648 | tf_op jit(solution)/shard_map/ppermute | solution.py:34
  61.4 36.5 %all-to-all-start.2 = ((bf16[8,48,1280]{2,1,0:T(8,128)(2,1)}), bf16[8,48,1280]{2,1,0:T(8,128)(2,1)S(1)}, u32[]{:S(2)}, u32[]{:S(2)}) async-start(bf16[8,48,1280]{2,1,0:T(8,128)(2,1)} %bitcast.11), calls=%async_computation.2 | async-start | bytes 1966080 | tf_op jit(solution)/shard_map/all_to_all | solution.py:82
  70.1 69.2 %all-gather.3.cloned.1.call-start = ((), (), s32[]{:S(2)}) async-start(), calls=%async_computation.5 | async-start | bytes 2211840 | tf_op jit(solution)/shard_map/all_gather | solution.py:101
  71.1 15.2 %collective-permute-start.8 = (bf16[4,4,24,640]{3,2,1,0:T(8,128)(2,1)S(1)}, bf16[4,4,24,640]{3,2,1,0:T(8,128)(2,1)S(1)}, u32[]{:S(2)}, u32[]{:S(2)}) collective-permute-start(bf16[4,4,24,640]{3,2,1,0:T(8,128)(2,1)S(1)} %slice.75), channel_id=1, source_target_pairs={{0,1},{1,0},{2,3},{3,2},{4,5},{5,4},{6,7},{7,6},{8,9},{9,8},{10,11... | collective-permute-start | bytes 1474568 | tf_op jit(solution)/shard_map/ppermute | solution.py:34
  74.4 4.0 %collective-permute-start.4 = (bf16[2,24,640]{2,1,0:T(8,128)(2,1)S(1)}, bf16[2,24,640]{2,1,0:T(8,128)(2,1)S(1)}, u32[]{:S(2)}, u32[]{:S(2)}) collective-permute-start(bf16[2,24,640]{2,1,0:T(8,128)(2,1)S(1)} %fusion.38), channel_id=1, source_target_pairs={{0,16},{16,0},{1,17},{17,1},{2,18},{18,2},{3,19},{19,3},{4,20},{20... | collective-permute-start | bytes 184328 | tf_op jit(solution)/shard_map/ppermute | solution.py:34
  78.4 48.9 %collective-permute-start.5 = (bf16[640,640]{1,0:T(8,128)(2,1)}, bf16[640,640]{1,0:T(8,128)(2,1)}, u32[]{:S(2)}, u32[]{:S(2)}) collective-permute-start(bf16[640,640]{1,0:T(8,128)(2,1)} %param.8), channel_id=1, source_target_pairs={{0,16},{16,0},{1,17},{17,1},{2,18},{18,2},{3,19},{19,3},{4,20},{20... | collective-permute-start | bytes 2457608 | tf_op jit(solution)/shard_map/ppermute | solution.py:34
  80.7 46.6 %collective-permute-start.6 = (bf16[640,640]{1,0:T(8,128)(2,1)}, bf16[640,640]{1,0:T(8,128)(2,1)}, u32[]{:S(2)}, u32[]{:S(2)}) collective-permute-start(bf16[640,640]{1,0:T(8,128)(2,1)} %param.8), channel_id=1, source_target_pairs={{0,1},{1,0},{2,3},{3,2},{4,5},{5,4},{6,7},{7,6},{8,9},{9,8},{10,11... | collective-permute-start | bytes 2457608 | tf_op jit(solution)/shard_map/ppermute | solution.py:34
  82.6 44.7 %collective-permute-start.7 = (bf16[640,640]{1,0:T(8,128)(2,1)}, bf16[640,640]{1,0:T(8,128)(2,1)}, u32[]{:S(2)}, u32[]{:S(2)}) collective-permute-start(bf16[640,640]{1,0:T(8,128)(2,1)} %param.8), channel_id=1, source_target_pairs={{0,17},{1,16},{16,1},{17,0},{2,19},{3,18},{18,3},{19,2},{4,21},{5,... | collective-permute-start | bytes 2457608 | tf_op jit(solution)/shard_map/ppermute | solution.py:42
  87.5 48.7 %collective-permute-start.9 = (bf16[4,4,2,24,640]{4,3,1,0,2:T(8,128)(2,1)}, bf16[4,4,2,24,640]{4,3,1,0,2:T(8,128)(2,1)}, u32[]{:S(2)}, u32[]{:S(2)}) collective-permute-start(bf16[4,4,2,24,640]{4,3,1,0,2:T(8,128)(2,1)} %pad_maximum_fusion.2), channel_id=1, source_target_pairs={{0,16},{16,0},{1,17},{17,1},{2,18},{18,2},{3,19},{19,3},{4,20},{20... | collective-permute-start | bytes 2949128 | tf_op jit(solution)/shard_map/ppermute | solution.py:34
  124.2 27.2 %collective-permute-start.10 = (bf16[384,1280]{1,0:T(8,128)(2,1)}, bf16[384,1280]{1,0:T(8,128)(2,1)}, u32[]{:S(2)}, u32[]{:S(2)}) collective-permute-start(bf16[384,1280]{1,0:T(8,128)(2,1)} %all_gather.9), channel_id=1, source_target_pairs={{0,1},{1,0},{2,3},{3,2},{4,5},{5,4},{6,7},{7,6},{8,9},{9,8},{10,11... | collective-permute-start | bytes 2949128 | tf_op jit(solution)/shard_map/ppermute | solution.py:34
  132.0 13.5 %all-to-all-start.3 = ((bf16[4,4,24,1280]{3,2,1,0:T(8,128)(2,1)}), bf16[4,4,24,1280]{3,2,1,0:T(8,128)(2,1)S(1)}, u32[]{:S(2)}, u32[]{:S(2)}) async-start(bf16[4,4,24,1280]{3,2,1,0:T(8,128)(2,1)} %bitcast.83), calls=%async_computation.3 | async-start | bytes 1966080 | tf_op jit(solution)/shard_map/all_to_all | solution.py:116
  146.5 17.7 %all-to-all-start.4 = ((bf16[8,24,640]{2,1,0:T(8,128)(2,1)}), bf16[8,24,640]{2,1,0:T(8,128)(2,1)S(1)}, u32[]{:S(2)}, u32[]{:S(2)}) async-start(bf16[8,24,640]{2,1,0:T(8,128)(2,1)} %bitcast.36), calls=%async_computation.4 | async-start | bytes 491520 | tf_op jit(solution)/shard_map/all_to_all | solution.py:122
  153.1 11.7 %collective-permute-start.11 = (bf16[384,640]{1,0:T(8,128)(2,1)S(1)}, bf16[384,640]{1,0:T(8,128)(2,1)S(1)}, u32[]{:S(2)}, u32[]{:S(2)}) collective-permute-start(bf16[384,640]{1,0:T(8,128)(2,1)S(1)} %get-tuple-element.23), channel_id=1, source_target_pairs={{0,16},{16,0},{1,17},{17,1},{2,18},{18,2},{3,19},{19,3},{4,20},{20... | collective-permute-start | bytes 1474568 | tf_op jit(solution)/shard_map/ppermute | solution.py:34
  162.2 3.8 %collective-permute-start.12 = (bf16[384,640]{1,0:T(8,128)(2,1)S(1)}, bf16[384,640]{1,0:T(8,128)(2,1)S(1)}, u32[]{:S(2)}, u32[]{:S(2)}) collective-permute-start(bf16[384,640]{1,0:T(8,128)(2,1)S(1)} %get-tuple-element.24), channel_id=1, source_target_pairs={{0,16},{16,0},{1,17},{17,1},{2,18},{18,2},{3,19},{19,3},{4,20},{20... | collective-permute-start | bytes 1474568 | tf_op jit(solution)/shard_map/ppermute | solution.py:34
  166.3 1.5 copy-start
Sparse Core Ops, SparseCore 0:
  11.2 66.7 all-gather.4
  80.1 43.6 all-gather.2

commit v7 on v6

--- a/solution.py
+++ b/solution.py
@@ -64,7 +64,8 @@
     down_lane = swap(w_down, "yl")
     pieces = jnp.broadcast_to(output_grad.reshape(2, half, width), (4, 2, half, width))
     grad_y = lax.all_to_all(pieces.reshape(8, half, width), ("yh", "yl"), 0, 0)
-    grad_y = grad_y.reshape(4, 2, half, width)
+    pre_lane = swap(pre_activation, "yl")
+    grad_y = after(grad_y, pre_lane).reshape(4, 2, half, width)
     grad_y = jnp.concatenate(in_order(lane, grad_y[:, 0], grad_y[:, 1]), axis=-1)
     grad_xy = lax.all_to_all(
         jnp.broadcast_to(grad_y, (4, 4, half, 2 * width)), "x", 0, 0
@@ -87,8 +88,7 @@
     up_both = opposite(up_after)
     up_cat = tiled((w_up, up_core), (up_lane, up_both))
 
-    pre_lane = swap(pre_activation, "yl")
-    pre_both = jnp.stack(in_order(lane, pre_activation, after(pre_lane, grad_y)))
+    pre_both = jnp.stack(in_order(lane, pre_activation, pre_lane))
     pre_cut = pre_both.reshape(2, 2, 2, half, hidden)
     pre_half = jnp.where(lane == 0, pre_cut[:, :, 0], pre_cut[:, :, 1])
     pre_own, pre_sent = (

time: 180 us -> 176 us (0.978)
  starting transfers between devices: 75.4 us -> 72.7 us
    ppermute x12, starting transfers between devices: 41.2 us -> 39.3 us  [swap(): return lax.ppermute(values, axis, [(0, 1), (1, 0)])]
  transfers between devices with their start and end apart: 20 -> 20, of which waited for: 7 -> 6; matrix products, arithmetic and copies ran while one was open for 15% -> 15% of each run, Pallas kernels for 0% -> 0%
where the time goes in v7:
time: 176 us; the launch traced here: 174 us
  starting transfers between devices  72.7 us (41%)
  waiting for transfers between devices  29.4 us (17%)
  blocking collectives  26.3 us (15%)
  matrix products  17 us (10%)
  between operations  14.4 us (8%)
  other arithmetic  7.81 us (4%)
  local copies, waits for them, and re-layouts  6.47 us (4%)
    ppermute x12, starting transfers between devices, swap(): return lax.ppermute(values, axis, [(0, 1), (1, 0)])  39.3 us
    all_gather x1, blocking collectives, per_device(): slopes = lax.all_gather(slope_tile, 'z', axis=0, tiled=True)  26.3 us
    ppermute x12, waiting for transfers between devices, swap(): return lax.ppermute(values, axis, [(0, 1), (1, 0)])  20.9 us
    dot_general x3, matrix products, times_transposed(): lax.dot_general(left, right, (((1,), (1,)), ((), ())), preferred_element_...  9.1 us
    all_to_all x1, starting transfers between devices, per_device(): blocks = lax.all_to_all(part.reshape(8, rows, 2 * hidden), 'z', 0, 0)  8.61 us
    dot_general x2, matrix products, over_tokens(): lax.dot_general(left, right, (((0,), (0,)), ((), ())), preferred_element_...  7.95 us
    all_to_all x1, starting transfers between devices, per_device(): grad_y = lax.all_to_all(pieces.reshape(8, half, width), ('yh', 'yl'), 0, 0)  7.65 us
    all_to_all x1, starting transfers between devices, per_device(): blocks = lax.all_to_all(part_y.reshape(8, half, width), ('yh', 'yl'), 0, 0)  6.67 us
  transfers between devices with their start and end apart: 20, of which 6 were waited for; matrix products, arithmetic and copies ran while one was open for 15% of the time, Pallas kernels for 0%

profile of v7, /device:TPU:1, one launch (start us, length us, event | category | flops | bytes accessed | tf_op | source)
XLA Modules:
  0.0 174.1 jit_solution(4790548450769779502)
XLA Ops:
  9.4 7.7 %all-to-all-start = ((bf16[8,24,640]{2,1,0:T(8,128)(2,1)}), bf16[8,24,640]{2,1,0:T(8,128)(2,1)S(1)}, u32[]{:S(2)}, u32[]{:S(2)}) async-start(bf16[8,24,640]{2,1,0:T(8,128)(2,1)} %bitcast.1), calls=%async_computation | async-start | bytes 491520 | tf_op jit(solution)/shard_map/all_to_all | solution.py:66
  17.1 3.4 %collective-permute-start = (bf16[96,640]{1,0:T(8,128)(2,1)}, bf16[96,640]{1,0:T(8,128)(2,1)S(1)}, u32[]{:S(2)}, u32[]{:S(2)}) collective-permute-start(bf16[96,640]{1,0:T(8,128)(2,1)} %param.7), channel_id=1, source_target_pairs={{0,1},{1,0},{2,3},{3,2},{4,5},{5,4},{6,7},{7,6},{8,9},{9,8},{10,11... | collective-permute-start | bytes 368648 | tf_op jit(solution)/shard_map/ppermute | solution.py:34
  20.5 5.0 %collective-permute-start.1 = (bf16[640,640]{1,0:T(8,128)(2,1)}, bf16[640,640]{1,0:T(8,128)(2,1)}, u32[]{:S(2)}, u32[]{:S(2)}) collective-permute-start(bf16[640,640]{1,0:T(8,128)(2,1)} %param.9), channel_id=1, source_target_pairs={{0,16},{16,0},{1,17},{17,1},{2,18},{18,2},{3,19},{19,3},{4,20},{20... | collective-permute-start | bytes 2457608 | tf_op jit(solution)/shard_map/ppermute | solution.py:34
  25.5 1.9 %collective-permute-start.2 = (bf16[640,640]{1,0:T(8,128)(2,1)}, bf16[640,640]{1,0:T(8,128)(2,1)}, u32[]{:S(2)}, u32[]{:S(2)}) collective-permute-start(bf16[640,640]{1,0:T(8,128)(2,1)} %param.9), channel_id=1, source_target_pairs={{0,1},{1,0},{2,3},{3,2},{4,5},{5,4},{6,7},{7,6},{8,9},{9,8},{10,11... | collective-permute-start | bytes 2457608 | tf_op jit(solution)/shard_map/ppermute | solution.py:34
  28.5 3.8 %all-to-all-start.1 = ((bf16[4,4,24,1280]{3,2,1,0:T(8,128)(2,1)}), bf16[4,4,24,1280]{3,2,1,0:T(8,128)(2,1)S(1)}, u32[]{:S(2)}, u32[]{:S(2)}) async-start(bf16[4,4,24,1280]{3,2,1,0:T(8,128)(2,1)} %broadcast_in_dim.7), calls=%async_computation.1 | async-start | bytes 1966080 | tf_op jit(solution)/shard_map/all_to_all | solution.py:70
  32.3 17.2 %collective-permute-done.2 = bf16[640,640]{1,0:T(8,128)(2,1)} collective-permute-done((bf16[640,640]{1,0:T(8,128)(2,1)}, bf16[640,640]{1,0:T(8,128)(2,1)}, u32[]{:S(2)}, u32[]{:S(2)}) %collective-permute-start.2) | collective-permute-done | bytes 819232 | tf_op jit(solution)/shard_map/ppermute | solution.py:34
  49.5 2.7 %collective-permute-start.3 = (bf16[640,640]{1,0:T(8,128)(2,1)}, bf16[640,640]{1,0:T(8,128)(2,1)}, u32[]{:S(2)}, u32[]{:S(2)}) collective-permute-start(bf16[640,640]{1,0:T(8,128)(2,1)} %collective-permute-done.2), channel_id=1, source_target_pairs={{0,16},{16,0},{1,17},{17,1},{2,18},{18,2},{3,19},{19,3},{4,20},{20... | collective-permute-start | bytes 2457608 | tf_op jit(solution)/shard_map/ppermute | solution.py:34
  52.4 2.1 %fusion.12 = f32[384,1280]{1,0:T(8,128)S(1)} fusion(bf16[640,640]{1,0:T(8,128)(2,1)} %collective-permute-done.1, bf16[640,640]{1,0:T(8,128)(2,1)S(1)} %copy-done.2, bf16[384,1280]{1,0:T(8,128)(2,1)S(1)} %bitcast.88), kind=kOutput, calls=%fused_computation.14 | convolution fusion | flops 632422400 | bytes 4096000 | tf_op jit(solution)/shard_map/dot_general | solution.py:22
  54.5 3.3 %fusion.8 = bf16[384,1280]{1,0:T(8,128)(2,1)} fusion(f32[384,1280]{1,0:T(8,128)S(1)} %fusion.12, bf16[640,640]{1,0:T(8,128)(2,1)} %collective-permute-done.3, bf16[640,640]{1,0:T(8,128)(2,1)} %collective-permute-done.2, bf16[384,1280]{1,0:T(8,128)(2,1)S(1)} %bitcast.89), kind=kOutput, calls=%fused_computation.9 | convolution fusion | flops 633405440 | bytes 5079040 | tf_op jit(solution)/shard_map/dot_general | solution.py:22
  57.9 8.6 %all-to-all-start.2 = ((bf16[8,48,1280]{2,1,0:T(8,128)(2,1)}), bf16[8,48,1280]{2,1,0:T(8,128)(2,1)S(1)}, u32[]{:S(2)}, u32[]{:S(2)}) async-start(bf16[8,48,1280]{2,1,0:T(8,128)(2,1)} %bitcast.11), calls=%async_computation.2 | async-start | bytes 1966080 | tf_op jit(solution)/shard_map/all_to_all | solution.py:83
  67.5 2.0 %collective-permute-start.8 = (bf16[4,4,24,640]{3,2,1,0:T(8,128)(2,1)S(1)}, bf16[4,4,24,640]{3,2,1,0:T(8,128)(2,1)S(1)}, u32[]{:S(2)}, u32[]{:S(2)}) collective-permute-start(bf16[4,4,24,640]{3,2,1,0:T(8,128)(2,1)S(1)} %slice.75), channel_id=1, source_target_pairs={{0,1},{1,0},{2,3},{3,2},{4,5},{5,4},{6,7},{7,6},{8,9},{9,8},{10,11... | collective-permute-start | bytes 1474568 | tf_op jit(solution)/shard_map/ppermute | solution.py:34
  69.6 2.8 %collective-permute-start.4 = (bf16[2,24,640]{2,1,0:T(8,128)(2,1)S(1)}, bf16[2,24,640]{2,1,0:T(8,128)(2,1)S(1)}, u32[]{:S(2)}, u32[]{:S(2)}) collective-permute-start(bf16[2,24,640]{2,1,0:T(8,128)(2,1)S(1)} %fusion.38), channel_id=1, source_target_pairs={{0,16},{16,0},{1,17},{17,1},{2,18},{18,2},{3,19},{19,3},{4,20},{20... | collective-permute-start | bytes 184328 | tf_op jit(solution)/shard_map/ppermute | solution.py:34
  73.3 2.3 %collective-permute-start.5 = (bf16[640,640]{1,0:T(8,128)(2,1)}, bf16[640,640]{1,0:T(8,128)(2,1)}, u32[]{:S(2)}, u32[]{:S(2)}) collective-permute-start(bf16[640,640]{1,0:T(8,128)(2,1)} %param.8), channel_id=1, source_target_pairs={{0,16},{16,0},{1,17},{17,1},{2,18},{18,2},{3,19},{19,3},{4,20},{20... | collective-permute-start | bytes 2457608 | tf_op jit(solution)/shard_map/ppermute | solution.py:34
  75.6 3.3 %collective-permute-start.6 = (bf16[640,640]{1,0:T(8,128)(2,1)}, bf16[640,640]{1,0:T(8,128)(2,1)}, u32[]{:S(2)}, u32[]{:S(2)}) collective-permute-start(bf16[640,640]{1,0:T(8,128)(2,1)} %param.8), channel_id=1, source_target_pairs={{0,1},{1,0},{2,3},{3,2},{4,5},{5,4},{6,7},{7,6},{8,9},{9,8},{10,11... | collective-permute-start | bytes 2457608 | tf_op jit(solution)/shard_map/ppermute | solution.py:34
  78.8 2.4 %collective-permute-start.7 = (bf16[640,640]{1,0:T(8,128)(2,1)}, bf16[640,640]{1,0:T(8,128)(2,1)}, u32[]{:S(2)}, u32[]{:S(2)}) collective-permute-start(bf16[640,640]{1,0:T(8,128)(2,1)} %param.8), channel_id=1, source_target_pairs={{0,17},{1,16},{16,1},{17,0},{2,19},{3,18},{18,3},{19,2},{4,21},{5,... | collective-permute-start | bytes 2457608 | tf_op jit(solution)/shard_map/ppermute | solution.py:42
  84.0 3.6 %collective-permute-start.9 = (bf16[4,4,2,24,640]{4,3,1,0,2:T(8,128)(2,1)}, bf16[4,4,2,24,640]{4,3,1,0,2:T(8,128)(2,1)}, u32[]{:S(2)}, u32[]{:S(2)}) collective-permute-start(bf16[4,4,2,24,640]{4,3,1,0,2:T(8,128)(2,1)} %pad_maximum_fusion.2), channel_id=1, source_target_pairs={{0,16},{16,0},{1,17},{17,1},{2,18},{18,2},{3,19},{19,3},{4,20},{20... | collective-permute-start | bytes 2949128 | tf_op jit(solution)/shard_map/ppermute | solution.py:34
  87.6 6.6 %all-to-all-done.2 = bf16[8,48,1280]{2,1,0:T(8,128)(2,1)S(1)} async-done(((bf16[8,48,1280]{2,1,0:T(8,128)(2,1)}), bf16[8,48,1280]{2,1,0:T(8,128)(2,1)S(1)}, u32[]{:S(2)}, u32[]{:S(2)}) %all-to-all-start.2) | async-done | bytes 983072 | tf_op jit(solution)/shard_map/all_to_all | solution.py:83
  94.5 26.3 %all_gather.9 = bf16[384,1280]{1,0:T(8,128)(2,1)} all-gather(bf16[48,1280]{1,0:T(8,128)(2,1)S(1)} %fusion.32), channel_id=1, replica_groups=mesh['yh'=4,'x'=4,'c'=2,'z'=8,'yl'=2] {'z'}, dimensions={0}, use_global_device_ids=true | all-gather | bytes 1105920 | tf_op jit(solution)/shard_map/all_gather | solution.py:105
  122.7 3.6 %fusion.9 = bf16[384,1280]{1,0:T(8,128)(2,1)S(1)} fusion(bf16[384,1280]{1,0:T(8,128)(2,1)} %all_gather.9, bf16[640,640]{1,0:T(8,128)(2,1)} %collective-permute-done.7, bf16[640,640]{1,0:T(8,128)(2,1)} %collective-permute-done.6, bf16[640,640]{1,0:T(8,128)(2,1)} %collective-permute-done.5, bf16[640,640]{1,0:T(8,128)(2,1)} %param.8), kind=kOutput, calls=%fused_computation.10 | convolution fusion | flops 1271889920 | bytes 5242880 | tf_op jit(solution)/shard_map/dot_general | solution.py:22
  127.4 4.2 %all-to-all-start.3 = ((bf16[4,4,24,1280]{3,2,1,0:T(8,128)(2,1)}), bf16[4,4,24,1280]{3,2,1,0:T(8,128)(2,1)S(1)}, u32[]{:S(2)}, u32[]{:S(2)}) async-start(bf16[4,4,24,1280]{3,2,1,0:T(8,128)(2,1)} %bitcast.83), calls=%async_computation.3 | async-start | bytes 1966080 | tf_op jit(solution)/shard_map/all_to_all | solution.py:116
  134.7 5.0 %fusion.43 = f32[640,640]{1,0:T(8,128)} fusion(bf16[1536,640]{1,0:T(8,128)(2,1)} %all-gather.3.cloned.1.call-done, bf16[1536,640]{1,0:T(8,128)(2,1)} %bitcast.86), kind=kOutput, calls=%fused_computation.82 | convolution fusion | flops 1258291200 | bytes 5570560 | tf_op jit(solution)/shard_map/dot_general | solution.py:28
  141.9 6.7 %all-to-all-start.4 = ((bf16[8,24,640]{2,1,0:T(8,128)(2,1)}), bf16[8,24,640]{2,1,0:T(8,128)(2,1)S(1)}, u32[]{:S(2)}, u32[]{:S(2)}) async-start(bf16[8,24,640]{2,1,0:T(8,128)(2,1)} %bitcast.36), calls=%async_computation.4 | async-start | bytes 491520 | tf_op jit(solution)/shard_map/all_to_all | solution.py:122
  150.2 8.5 %collective-permute-start.11 = (bf16[384,640]{1,0:T(8,128)(2,1)S(1)}, bf16[384,640]{1,0:T(8,128)(2,1)S(1)}, u32[]{:S(2)}, u32[]{:S(2)}) collective-permute-start(bf16[384,640]{1,0:T(8,128)(2,1)S(1)} %get-tuple-element.23), channel_id=1, source_target_pairs={{0,16},{16,0},{1,17},{17,1},{2,18},{18,2},{3,19},{19,3},{4,20},{20... | collective-permute-start | bytes 1474568 | tf_op jit(solution)/shard_map/ppermute | solution.py:34
  164.4 2.9 %fusion.44 = f32[640,640]{1,0:T(8,128)} fusion(bf16[1536,640]{1,0:T(8,128)(2,1)S(1)} %copy-done, bf16[1536,640]{1,0:T(8,128)(2,1)S(1)} %bitcast.87), kind=kOutput, calls=%fused_computation.83 | convolution fusion | flops 1258291200 | bytes 5570560 | tf_op jit(solution)/shard_map/dot_general | solution.py:28
  (60 shorter events, 23.8 us)
Async XLA Ops:
  7.2 126.0 %all-gather.5.cloned.1.call-start = ((), (), s32[]{:S(2)}) async-start(), calls=%async_computation.6 | async-start | bytes 2027520 | tf_op jit(solution)/shard_map/all_gather | solution.py:61
  9.4 18.0 %all-to-all-start = ((bf16[8,24,640]{2,1,0:T(8,128)(2,1)}), bf16[8,24,640]{2,1,0:T(8,128)(2,1)S(1)}, u32[]{:S(2)}, u32[]{:S(2)}) async-start(bf16[8,24,640]{2,1,0:T(8,128)(2,1)} %bitcast.1), calls=%async_computation | async-start | bytes 491520 | tf_op jit(solution)/shard_map/all_to_all | solution.py:66
  17.1 10.3 %collective-permute-start = (bf16[96,640]{1,0:T(8,128)(2,1)}, bf16[96,640]{1,0:T(8,128)(2,1)S(1)}, u32[]{:S(2)}, u32[]{:S(2)}) collective-permute-start(bf16[96,640]{1,0:T(8,128)(2,1)} %param.7), channel_id=1, source_target_pairs={{0,1},{1,0},{2,3},{3,2},{4,5},{5,4},{6,7},{7,6},{8,9},{9,8},{10,11... | collective-permute-start | bytes 368648 | tf_op jit(solution)/shard_map/ppermute | solution.py:34
  20.5 31.9 %collective-permute-start.1 = (bf16[640,640]{1,0:T(8,128)(2,1)}, bf16[640,640]{1,0:T(8,128)(2,1)}, u32[]{:S(2)}, u32[]{:S(2)}) collective-permute-start(bf16[640,640]{1,0:T(8,128)(2,1)} %param.9), channel_id=1, source_target_pairs={{0,16},{16,0},{1,17},{17,1},{2,18},{18,2},{3,19},{19,3},{4,20},{20... | collective-permute-start | bytes 2457608 | tf_op jit(solution)/shard_map/ppermute | solution.py:34
  25.5 24.1 %collective-permute-start.2 = (bf16[640,640]{1,0:T(8,128)(2,1)}, bf16[640,640]{1,0:T(8,128)(2,1)}, u32[]{:S(2)}, u32[]{:S(2)}) collective-permute-start(bf16[640,640]{1,0:T(8,128)(2,1)} %param.9), channel_id=1, source_target_pairs={{0,1},{1,0},{2,3},{3,2},{4,5},{5,4},{6,7},{7,6},{8,9},{9,8},{10,11... | collective-permute-start | bytes 2457608 | tf_op jit(solution)/shard_map/ppermute | solution.py:34
  27.5 24.8 %copy-start.1 = (bf16[96,640]{1,0:T(8,128)(2,1)S(1)}, bf16[96,640]{1,0:T(8,128)(2,1)}, u32[]{:S(2)}) copy-start(bf16[96,640]{1,0:T(8,128)(2,1)} %param.7) | copy-start | bytes 368644
  28.5 23.8 %copy-start.2 = (bf16[640,640]{1,0:T(8,128)(2,1)S(1)}, bf16[640,640]{1,0:T(8,128)(2,1)}, u32[]{:S(2)}) copy-start(bf16[640,640]{1,0:T(8,128)(2,1)} %param.9) | copy-start | bytes 2457604
  28.5 23.7 %all-to-all-start.1 = ((bf16[4,4,24,1280]{3,2,1,0:T(8,128)(2,1)}), bf16[4,4,24,1280]{3,2,1,0:T(8,128)(2,1)S(1)}, u32[]{:S(2)}, u32[]{:S(2)}) async-start(bf16[4,4,24,1280]{3,2,1,0:T(8,128)(2,1)} %broadcast_in_dim.7), calls=%async_computation.1 | async-start | bytes 1966080 | tf_op jit(solution)/shard_map/all_to_all | solution.py:70
  49.5 5.0 %collective-permute-start.3 = (bf16[640,640]{1,0:T(8,128)(2,1)}, bf16[640,640]{1,0:T(8,128)(2,1)}, u32[]{:S(2)}, u32[]{:S(2)}) collective-permute-start(bf16[640,640]{1,0:T(8,128)(2,1)} %collective-permute-done.2), channel_id=1, source_target_pairs={{0,16},{16,0},{1,17},{17,1},{2,18},{18,2},{3,19},{19,3},{4,20},{20... | collective-permute-start | bytes 2457608 | tf_op jit(solution)/shard_map/ppermute | solution.py:34
  57.9 36.4 %all-to-all-start.2 = ((bf16[8,48,1280]{2,1,0:T(8,128)(2,1)}), bf16[8,48,1280]{2,1,0:T(8,128)(2,1)S(1)}, u32[]{:S(2)}, u32[]{:S(2)}) async-start(bf16[8,48,1280]{2,1,0:T(8,128)(2,1)} %bitcast.11), calls=%async_computation.2 | async-start | bytes 1966080 | tf_op jit(solution)/shard_map/all_to_all | solution.py:83
  66.5 68.2 %all-gather.3.cloned.1.call-start = ((), (), s32[]{:S(2)}) async-start(), calls=%async_computation.5 | async-start | bytes 2211840 | tf_op jit(solution)/shard_map/all_gather | solution.py:101
  67.5 15.3 %collective-permute-start.8 = (bf16[4,4,24,640]{3,2,1,0:T(8,128)(2,1)S(1)}, bf16[4,4,24,640]{3,2,1,0:T(8,128)(2,1)S(1)}, u32[]{:S(2)}, u32[]{:S(2)}) collective-permute-start(bf16[4,4,24,640]{3,2,1,0:T(8,128)(2,1)S(1)} %slice.75), channel_id=1, source_target_pairs={{0,1},{1,0},{2,3},{3,2},{4,5},{5,4},{6,7},{7,6},{8,9},{9,8},{10,11... | collective-permute-start | bytes 1474568 | tf_op jit(solution)/shard_map/ppermute | solution.py:34
  69.6 3.7 %collective-permute-start.4 = (bf16[2,24,640]{2,1,0:T(8,128)(2,1)S(1)}, bf16[2,24,640]{2,1,0:T(8,128)(2,1)S(1)}, u32[]{:S(2)}, u32[]{:S(2)}) collective-permute-start(bf16[2,24,640]{2,1,0:T(8,128)(2,1)S(1)} %fusion.38), channel_id=1, source_target_pairs={{0,16},{16,0},{1,17},{17,1},{2,18},{18,2},{3,19},{19,3},{4,20},{20... | collective-permute-start | bytes 184328 | tf_op jit(solution)/shard_map/ppermute | solution.py:34
  73.3 49.4 %collective-permute-start.5 = (bf16[640,640]{1,0:T(8,128)(2,1)}, bf16[640,640]{1,0:T(8,128)(2,1)}, u32[]{:S(2)}, u32[]{:S(2)}) collective-permute-start(bf16[640,640]{1,0:T(8,128)(2,1)} %param.8), channel_id=1, source_target_pairs={{0,16},{16,0},{1,17},{17,1},{2,18},{18,2},{3,19},{19,3},{4,20},{20... | collective-permute-start | bytes 2457608 | tf_op jit(solution)/shard_map/ppermute | solution.py:34
  75.6 47.1 %collective-permute-start.6 = (bf16[640,640]{1,0:T(8,128)(2,1)}, bf16[640,640]{1,0:T(8,128)(2,1)}, u32[]{:S(2)}, u32[]{:S(2)}) collective-permute-start(bf16[640,640]{1,0:T(8,128)(2,1)} %param.8), channel_id=1, source_target_pairs={{0,1},{1,0},{2,3},{3,2},{4,5},{5,4},{6,7},{7,6},{8,9},{9,8},{10,11... | collective-permute-start | bytes 2457608 | tf_op jit(solution)/shard_map/ppermute | solution.py:34
  78.8 43.9 %collective-permute-start.7 = (bf16[640,640]{1,0:T(8,128)(2,1)}, bf16[640,640]{1,0:T(8,128)(2,1)}, u32[]{:S(2)}, u32[]{:S(2)}) collective-permute-start(bf16[640,640]{1,0:T(8,128)(2,1)} %param.8), channel_id=1, source_target_pairs={{0,17},{1,16},{16,1},{17,0},{2,19},{3,18},{18,3},{19,2},{4,21},{5,... | collective-permute-start | bytes 2457608 | tf_op jit(solution)/shard_map/ppermute | solution.py:42
  84.0 47.6 %collective-permute-start.9 = (bf16[4,4,2,24,640]{4,3,1,0,2:T(8,128)(2,1)}, bf16[4,4,2,24,640]{4,3,1,0,2:T(8,128)(2,1)}, u32[]{:S(2)}, u32[]{:S(2)}) collective-permute-start(bf16[4,4,2,24,640]{4,3,1,0,2:T(8,128)(2,1)} %pad_maximum_fusion.2), channel_id=1, source_target_pairs={{0,16},{16,0},{1,17},{17,1},{2,18},{18,2},{3,19},{19,3},{4,20},{20... | collective-permute-start | bytes 2949128 | tf_op jit(solution)/shard_map/ppermute | solution.py:34
  120.8 27.8 %collective-permute-start.10 = (bf16[384,1280]{1,0:T(8,128)(2,1)}, bf16[384,1280]{1,0:T(8,128)(2,1)}, u32[]{:S(2)}, u32[]{:S(2)}) collective-permute-start(bf16[384,1280]{1,0:T(8,128)(2,1)} %all_gather.9), channel_id=1, source_target_pairs={{0,1},{1,0},{2,3},{3,2},{4,5},{5,4},{6,7},{7,6},{8,9},{9,8},{10,11... | collective-permute-start | bytes 2949128 | tf_op jit(solution)/shard_map/ppermute | solution.py:34
  127.4 13.6 %all-to-all-start.3 = ((bf16[4,4,24,1280]{3,2,1,0:T(8,128)(2,1)}), bf16[4,4,24,1280]{3,2,1,0:T(8,128)(2,1)S(1)}, u32[]{:S(2)}, u32[]{:S(2)}) async-start(bf16[4,4,24,1280]{3,2,1,0:T(8,128)(2,1)} %bitcast.83), calls=%async_computation.3 | async-start | bytes 1966080 | tf_op jit(solution)/shard_map/all_to_all | solution.py:116
  141.9 18.7 %all-to-all-start.4 = ((bf16[8,24,640]{2,1,0:T(8,128)(2,1)}), bf16[8,24,640]{2,1,0:T(8,128)(2,1)S(1)}, u32[]{:S(2)}, u32[]{:S(2)}) async-start(bf16[8,24,640]{2,1,0:T(8,128)(2,1)} %bitcast.36), calls=%async_computation.4 | async-start | bytes 491520 | tf_op jit(solution)/shard_map/all_to_all | solution.py:122
  150.2 11.1 %collective-permute-start.11 = (bf16[384,640]{1,0:T(8,128)(2,1)S(1)}, bf16[384,640]{1,0:T(8,128)(2,1)S(1)}, u32[]{:S(2)}, u32[]{:S(2)}) collective-permute-start(bf16[384,640]{1,0:T(8,128)(2,1)S(1)} %get-tuple-element.23), channel_id=1, source_target_pairs={{0,16},{16,0},{1,17},{17,1},{2,18},{18,2},{3,19},{19,3},{4,20},{20... | collective-permute-start | bytes 1474568 | tf_op jit(solution)/shard_map/ppermute | solution.py:34
  158.7 3.8 %collective-permute-start.12 = (bf16[384,640]{1,0:T(8,128)(2,1)S(1)}, bf16[384,640]{1,0:T(8,128)(2,1)S(1)}, u32[]{:S(2)}, u32[]{:S(2)}) collective-permute-start(bf16[384,640]{1,0:T(8,128)(2,1)S(1)} %get-tuple-element.24), channel_id=1, source_target_pairs={{0,16},{16,0},{1,17},{17,1},{2,18},{18,2},{3,19},{19,3},{4,20},{20... | collective-permute-start | bytes 1474568 | tf_op jit(solution)/shard_map/ppermute | solution.py:34
  162.8 1.5 copy-start
Sparse Core Ops, SparseCore 0:
  11.2 65.5 all-gather.4
  78.8 43.8 all-gather.2

commit v8 on v6

--- a/solution.py
+++ b/solution.py
@@ -60,8 +60,9 @@
 
     input_all = lax.all_gather(layer_input, WIDE, axis=0, tiled=True)
 
-    down_core = swap(w_down, "c")
-    down_lane = swap(w_down, "yl")
+    packed = jnp.concatenate([w_down, pre_activation], axis=0)
+    pack_lane = swap(packed, "yl")
+    down_lane, pre_lane = pack_lane[:hidden], pack_lane[hidden:]
     pieces = jnp.broadcast_to(output_grad.reshape(2, half, width), (4, 2, half, width))
     grad_y = lax.all_to_all(pieces.reshape(8, half, width), ("yh", "yl"), 0, 0)
     grad_y = grad_y.reshape(4, 2, half, width)
@@ -70,7 +71,10 @@
         jnp.broadcast_to(grad_y, (4, 4, half, 2 * width)), "x", 0, 0
     )
     grad_xy = jnp.swapaxes(grad_xy, 0, 1)
-    down_both = swap(down_lane, "c")
+    pack_core = swap(packed, "c")
+    pack_both = swap(pack_lane, "c")
+    down_core, pre_core = pack_core[:hidden], pack_core[hidden:]
+    down_both, pre_diag = pack_both[:hidden], pack_both[hidden:]
     grad_rows = grad_xy.reshape(-1, 2 * width)
     part = times_transposed(
         grad_rows[:, :width], jnp.concatenate([w_down, down_core], axis=0)
@@ -81,21 +85,23 @@
     part = part.astype(BF16)
     blocks = lax.all_to_all(part.reshape(8, rows, 2 * hidden), "z", 0, 0)
 
-    up_after = after(w_up, part)
+    grad_own, grad_pair = grad_xy[..., :width], grad_xy[..., width:]
+    grad_lane = swap(after(grad_pair, part), "yl")
+    up_after = after(w_up, grad_lane)
     up_lane = swap(up_after, "yl")
     up_core = swap(up_after, "c")
     up_both = opposite(up_after)
     up_cat = tiled((w_up, up_core), (up_lane, up_both))
 
-    pre_lane = swap(pre_activation, "yl")
-    pre_both = jnp.stack(in_order(lane, pre_activation, after(pre_lane, grad_y)))
-    pre_cut = pre_both.reshape(2, 2, 2, half, hidden)
-    pre_half = jnp.where(lane == 0, pre_cut[:, :, 0], pre_cut[:, :, 1])
-    pre_own, pre_sent = (
-        jnp.where(core == 0, pre_half[:, i], pre_half[:, 1 - i]) for i in range(2)
+    def share(own, pair):
+        cut = jnp.stack(in_order(lane, own, pair)).reshape(2, 2, 2, half, hidden)
+        cut = jnp.where(lane == 0, cut[:, :, 0], cut[:, :, 1])
+        return jnp.where(core == 0, cut[:, 0], cut[:, 1]).reshape(rows, hidden)
+
+    pre_tile = jnp.concatenate(
+        [share(pre_activation, pre_lane), share(pre_core, pre_diag)], axis=-1
     )
-    pre_pair = swap(pre_sent, "c")
-    pre_tile = jnp.concatenate([pre_own, pre_pair], axis=-1).reshape(rows, 2 * hidden)
+    pre_both = jnp.stack(in_order(lane, pre_activation, pre_lane))
     slope_factor = gelu_parts(pre_tile)[1]
     act_tile = gelu_parts(pre_both)[0].astype(BF16).reshape(-1, hidden)
     act_all = lax.all_gather(act_tile, "z", axis=0, tiled=True)
@@ -104,8 +110,6 @@
     slope_tile = (act_grad * slope_factor).astype(BF16)
     slopes = lax.all_gather(slope_tile, "z", axis=0, tiled=True)
 
-    grad_own, grad_pair = grad_xy[..., :width], grad_xy[..., width:]
-    grad_lane = swap(after(grad_pair, part), "yl")
     grad_core = jnp.stack(in_order(lane, grad_own, grad_lane), axis=2)
     grad_other = swap(grad_core, "c")
     grad_all = jnp.stack(in_order(core, grad_core, grad_other), axis=2)

time: 180 us -> 182 us (1.011)
  local copies, waits for them, and re-layouts: 6.47 us -> 13.2 us
  starting transfers between devices: 75.4 us -> 69 us
  other arithmetic: 7.8 us -> 9.72 us
    ppermute x12 -> x10, starting transfers between devices: 41.2 us -> 34.1 us  [swap(): return lax.ppermute(values, axis, [(0, 1), (1, 0)])]
    all_to_all x1, waiting for transfers between devices: 7.37 us -> 0.56 us  [per_device(): blocks = lax.all_to_all(part.reshape(8, rows, 2 * hidden), 'z', 0, 0)]
    ppermute x12 -> x10, waiting for transfers between devices: 20 us -> 26.8 us  [swap(): return lax.ppermute(values, axis, [(0, 1), (1, 0)])]
    slice x0 -> x3, local copies, waits for them, and re-layouts: none -> 4.44 us  [the longest x1 2.12 us: per_device(): down_lane, pre_lane = (pack_lane[:hidden], pack_lane[hidden:])]
    unnamed x6 -> x11, local copies, waits for them, and re-layouts: 1.33 us -> 3.61 us
    select_n x2 -> x3, other arithmetic: 0.05 us -> 1.95 us  [in_order(): jnp.where(index == 0, other, own)]
  transfers between devices with their start and end apart: 20 -> 18, of which waited for: 7 -> 6; matrix products, arithmetic and copies ran while one was open for 15% -> 18% of each run, Pallas kernels for 0% -> 0%
where the time goes in v8:
time: 182 us; the launch traced here: 179 us
  starting transfers between devices  69 us (38%)
  waiting for transfers between devices  29.7 us (16%)
  blocking collectives  27.4 us (15%)
  matrix products  15.8 us (9%)
  between operations  14.4 us (8%)
  local copies, waits for them, and re-layouts  13.2 us (7%)
  other arithmetic  9.72 us (5%)
    ppermute x10, starting transfers between devices, swap(): return lax.ppermute(values, axis, [(0, 1), (1, 0)])  34.1 us
    all_gather x1, blocking collectives, per_device(): slopes = lax.all_gather(slope_tile, 'z', axis=0, tiled=True)  27.4 us
    ppermute x10, waiting for transfers between devices, swap(): return lax.ppermute(values, axis, [(0, 1), (1, 0)])  26.8 us
    all_to_all x1, starting transfers between devices, per_device(): blocks = lax.all_to_all(part.reshape(8, rows, 2 * hidden), 'z', 0, 0)  9.69 us
    dot_general x2, matrix products, over_tokens(): lax.dot_general(left, right, (((0,), (0,)), ((), ())), preferred_element_...  7.95 us
    dot_general x3, matrix products, times_transposed(): lax.dot_general(left, right, (((1,), (1,)), ((), ())), preferred_element_...  7.8 us
    all_to_all x1, starting transfers between devices, per_device(): grad_y = lax.all_to_all(pieces.reshape(8, half, width), ('yh', 'yl'), 0, 0)  7.65 us
    all_to_all x1, starting transfers between devices, per_device(): blocks = lax.all_to_all(part_y.reshape(8, half, width), ('yh', 'yl'), 0, 0)  6.08 us
  transfers between devices with their start and end apart: 18, of which 6 were waited for; matrix products, arithmetic and copies ran while one was open for 18% of the time, Pallas kernels for 0%

profile of v8, /device:TPU:1, one launch (start us, length us, event | category | flops | bytes accessed | tf_op | source)
XLA Modules:
  0.0 179.2 jit_solution(3142048072688618959)
XLA Ops:
  9.5 7.7 %all-to-all-start = ((bf16[8,24,640]{2,1,0:T(8,128)(2,1)}), bf16[8,24,640]{2,1,0:T(8,128)(2,1)S(1)}, u32[]{:S(2)}, u32[]{:S(2)}) async-start(bf16[8,24,640]{2,1,0:T(8,128)(2,1)} %bitcast.1), calls=%async_computation | async-start | bytes 491520 | tf_op jit(solution)/shard_map/all_to_all | solution.py:67
  18.4 3.4 %collective-permute-start.1 = (bf16[736,640]{1,0:T(8,128)(2,1)S(1)}, bf16[736,640]{1,0:T(8,128)(2,1)}, u32[]{:S(2)}, u32[]{:S(2)}) collective-permute-start(bf16[736,640]{1,0:T(8,128)(2,1)S(1)} %constant_dynamic-update-slice_fusion), channel_id=1, source_target_pairs={{0,1},{1,0},{2,3},{3,2},{4,5},{5,4},{6,7},{7,6},{8,9},{9,8},{10,11... | collective-permute-start | bytes 2826248 | tf_op jit(solution)/shard_map/ppermute | solution.py:34
  21.7 5.0 %collective-permute-start = (bf16[736,640]{1,0:T(8,128)(2,1)S(1)}, bf16[736,640]{1,0:T(8,128)(2,1)S(1)}, u32[]{:S(2)}, u32[]{:S(2)}) collective-permute-start(bf16[736,640]{1,0:T(8,128)(2,1)S(1)} %constant_dynamic-update-slice_fusion), channel_id=1, source_target_pairs={{0,16},{16,0},{1,17},{17,1},{2,18},{18,2},{3,19},{19,3},{4,20},{20... | collective-permute-start | bytes 2826248 | tf_op jit(solution)/shard_map/ppermute | solution.py:34
  27.9 4.3 %all-to-all-start.1 = ((bf16[4,4,24,1280]{3,2,1,0:T(8,128)(2,1)}), bf16[4,4,24,1280]{3,2,1,0:T(8,128)(2,1)S(1)}, u32[]{:S(2)}, u32[]{:S(2)}) async-start(bf16[4,4,24,1280]{3,2,1,0:T(8,128)(2,1)} %broadcast_in_dim.7), calls=%async_computation.1 | async-start | bytes 1966080 | tf_op jit(solution)/shard_map/all_to_all | solution.py:70
  32.2 14.4 %collective-permute-done.1 = bf16[736,640]{1,0:T(8,128)(2,1)} collective-permute-done((bf16[736,640]{1,0:T(8,128)(2,1)S(1)}, bf16[736,640]{1,0:T(8,128)(2,1)}, u32[]{:S(2)}, u32[]{:S(2)}) %collective-permute-start.1) | collective-permute-done | bytes 942112 | tf_op jit(solution)/shard_map/ppermute | solution.py:34
  46.6 3.7 %collective-permute-start.2 = (bf16[736,640]{1,0:T(8,128)(2,1)}, bf16[736,640]{1,0:T(8,128)(2,1)}, u32[]{:S(2)}, u32[]{:S(2)}) collective-permute-start(bf16[736,640]{1,0:T(8,128)(2,1)} %collective-permute-done.1), channel_id=1, source_target_pairs={{0,16},{16,0},{1,17},{17,1},{2,18},{18,2},{3,19},{19,3},{4,20},{20... | collective-permute-start | bytes 2826248 | tf_op jit(solution)/shard_map/ppermute | solution.py:34
  50.3 2.1 %slice.109 = bf16[640,640]{1,0:T(8,128)(2,1)} slice(bf16[736,640]{1,0:T(8,128)(2,1)} %collective-permute-done.1), slice={[0:640], [0:640]} | slice | bytes 1638400 | tf_op jit(solution)/shard_map/slice | solution.py:65
  55.7 2.2 %fusion.12 = f32[384,1280]{1,0:T(8,128)S(1)} fusion(bf16[640,640]{1,0:T(8,128)(2,1)S(1)} %copy-done.3, bf16[640,640]{1,0:T(8,128)(2,1)} %param.9, bf16[384,1280]{1,0:T(8,128)(2,1)S(1)} %bitcast.89), kind=kOutput, calls=%fused_computation.14 | convolution fusion | flops 632422400 | bytes 4096000 | tf_op jit(solution)/shard_map/dot_general | solution.py:22
  59.1 2.0 %fusion.8 = bf16[384,1280]{1,0:T(8,128)(2,1)} fusion(f32[384,1280]{1,0:T(8,128)S(1)} %fusion.12, bf16[640,640]{1,0:T(8,128)(2,1)S(1)} %slice.110, bf16[640,640]{1,0:T(8,128)(2,1)S(1)} %copy-done.2, bf16[384,1280]{1,0:T(8,128)(2,1)S(1)} %bitcast.90), kind=kOutput, calls=%fused_computation.9 | convolution fusion | flops 633405440 | bytes 5079040 | tf_op jit(solution)/shard_map/dot_general | solution.py:22
  61.1 9.7 %all-to-all-start.2 = ((bf16[8,48,1280]{2,1,0:T(8,128)(2,1)}), bf16[8,48,1280]{2,1,0:T(8,128)(2,1)S(1)}, u32[]{:S(2)}, u32[]{:S(2)}) async-start(bf16[8,48,1280]{2,1,0:T(8,128)(2,1)} %bitcast.11), calls=%async_computation.2 | async-start | bytes 1966080 | tf_op jit(solution)/shard_map/all_to_all | solution.py:86
  71.8 2.4 %collective-permute-start.3 = (bf16[4,4,24,640]{3,2,1,0:T(8,128)(2,1)S(1)}, bf16[4,4,24,640]{3,2,1,0:T(8,128)(2,1)S(1)}, u32[]{:S(2)}, u32[]{:S(2)}) collective-permute-start(bf16[4,4,24,640]{3,2,1,0:T(8,128)(2,1)S(1)} %slice.122), channel_id=1, source_target_pairs={{0,1},{1,0},{2,3},{3,2},{4,5},{5,4},{6,7},{7,6},{8,9},{9,8},{10,11... | collective-permute-start | bytes 1474568 | tf_op jit(solution)/shard_map/ppermute | solution.py:34
  75.3 11.2 %collective-permute-done.3 = bf16[4,4,24,640]{3,2,1,0:T(8,128)(2,1)S(1)} collective-permute-done((bf16[4,4,24,640]{3,2,1,0:T(8,128)(2,1)S(1)}, bf16[4,4,24,640]{3,2,1,0:T(8,128)(2,1)S(1)}, u32[]{:S(2)}, u32[]{:S(2)}) %collective-permute-start.3) | collective-permute-done | bytes 491552 | tf_op jit(solution)/shard_map/ppermute | solution.py:34
  86.5 2.8 %collective-permute-start.4 = (bf16[640,640]{1,0:T(8,128)(2,1)}, bf16[640,640]{1,0:T(8,128)(2,1)}, u32[]{:S(2)}, u32[]{:S(2)}) collective-permute-start(bf16[640,640]{1,0:T(8,128)(2,1)} %param.8), channel_id=1, source_target_pairs={{0,16},{16,0},{1,17},{17,1},{2,18},{18,2},{3,19},{19,3},{4,20},{20... | collective-permute-start | bytes 2457608 | tf_op jit(solution)/shard_map/ppermute | solution.py:34
  89.3 2.3 %collective-permute-start.5 = (bf16[640,640]{1,0:T(8,128)(2,1)}, bf16[640,640]{1,0:T(8,128)(2,1)}, u32[]{:S(2)}, u32[]{:S(2)}) collective-permute-start(bf16[640,640]{1,0:T(8,128)(2,1)} %param.8), channel_id=1, source_target_pairs={{0,1},{1,0},{2,3},{3,2},{4,5},{5,4},{6,7},{7,6},{8,9},{9,8},{10,11... | collective-permute-start | bytes 2457608 | tf_op jit(solution)/shard_map/ppermute | solution.py:34
  91.6 3.1 %collective-permute-start.6 = (bf16[640,640]{1,0:T(8,128)(2,1)}, bf16[640,640]{1,0:T(8,128)(2,1)}, u32[]{:S(2)}, u32[]{:S(2)}) collective-permute-start(bf16[640,640]{1,0:T(8,128)(2,1)} %param.8), channel_id=1, source_target_pairs={{0,17},{1,16},{16,1},{17,0},{2,19},{3,18},{18,3},{19,2},{4,21},{5,... | collective-permute-start | bytes 2457608 | tf_op jit(solution)/shard_map/ppermute | solution.py:42
  95.9 2.1 %collective-permute-start.7 = (bf16[4,4,2,24,640]{4,3,1,0,2:T(8,128)(2,1)}, bf16[4,4,2,24,640]{4,3,1,0,2:T(8,128)(2,1)}, u32[]{:S(2)}, u32[]{:S(2)}) collective-permute-start(bf16[4,4,2,24,640]{4,3,1,0,2:T(8,128)(2,1)} %pad_maximum_fusion.2), channel_id=1, source_target_pairs={{0,16},{16,0},{1,17},{17,1},{2,18},{18,2},{3,19},{19,3},{4,20},{20... | collective-permute-start | bytes 2949128 | tf_op jit(solution)/shard_map/ppermute | solution.py:34
  98.9 27.4 %all_gather.9 = bf16[384,1280]{1,0:T(8,128)(2,1)} all-gather(bf16[48,1280]{1,0:T(8,128)(2,1)S(1)} %fusion.32), channel_id=1, replica_groups=mesh['yh'=4,'x'=4,'c'=2,'z'=8,'yl'=2] {'z'}, dimensions={0}, use_global_device_ids=true | all-gather | bytes 1105920 | tf_op jit(solution)/shard_map/all_gather | solution.py:111
  126.3 2.7 %collective-permute-start.8 = (bf16[384,1280]{1,0:T(8,128)(2,1)}, bf16[384,1280]{1,0:T(8,128)(2,1)}, u32[]{:S(2)}, u32[]{:S(2)}) collective-permute-start(bf16[384,1280]{1,0:T(8,128)(2,1)} %all_gather.9), channel_id=1, source_target_pairs={{0,1},{1,0},{2,3},{3,2},{4,5},{5,4},{6,7},{7,6},{8,9},{9,8},{10,11... | collective-permute-start | bytes 2949128 | tf_op jit(solution)/shard_map/ppermute | solution.py:34
  129.3 3.6 %fusion.9 = bf16[384,1280]{1,0:T(8,128)(2,1)S(1)} fusion(bf16[384,1280]{1,0:T(8,128)(2,1)} %all_gather.9, bf16[640,640]{1,0:T(8,128)(2,1)} %collective-permute-done.6, bf16[640,640]{1,0:T(8,128)(2,1)} %collective-permute-done.5, bf16[640,640]{1,0:T(8,128)(2,1)} %collective-permute-done.4, bf16[640,640]{1,0:T(8,128)(2,1)} %param.8), kind=kOutput, calls=%fused_computation.10 | convolution fusion | flops 1271889920 | bytes 5242880 | tf_op jit(solution)/shard_map/dot_general | solution.py:22
  134.0 3.9 %all-to-all-start.3 = ((bf16[4,4,24,1280]{3,2,1,0:T(8,128)(2,1)}), bf16[4,4,24,1280]{3,2,1,0:T(8,128)(2,1)S(1)}, u32[]{:S(2)}, u32[]{:S(2)}) async-start(bf16[4,4,24,1280]{3,2,1,0:T(8,128)(2,1)} %bitcast.84), calls=%async_computation.3 | async-start | bytes 1966080 | tf_op jit(solution)/shard_map/all_to_all | solution.py:120
  141.0 5.0 %fusion.45 = f32[640,640]{1,0:T(8,128)} fusion(bf16[1536,640]{1,0:T(8,128)(2,1)} %all-gather.3.cloned.1.call-done, bf16[1536,640]{1,0:T(8,128)(2,1)} %bitcast.87), kind=kOutput, calls=%fused_computation.91 | convolution fusion | flops 1258291200 | bytes 5570560 | tf_op jit(solution)/shard_map/dot_general | solution.py:28
  148.3 6.1 %all-to-all-start.4 = ((bf16[8,24,640]{2,1,0:T(8,128)(2,1)}), bf16[8,24,640]{2,1,0:T(8,128)(2,1)S(1)}, u32[]{:S(2)}, u32[]{:S(2)}) async-start(bf16[8,24,640]{2,1,0:T(8,128)(2,1)} %bitcast.35), calls=%async_computation.4 | async-start | bytes 491520 | tf_op jit(solution)/shard_map/all_to_all | solution.py:126
  156.0 7.7 %collective-permute-start.10 = (bf16[384,640]{1,0:T(8,128)(2,1)S(1)}, bf16[384,640]{1,0:T(8,128)(2,1)S(1)}, u32[]{:S(2)}, u32[]{:S(2)}) collective-permute-start(bf16[384,640]{1,0:T(8,128)(2,1)S(1)} %get-tuple-element.26), channel_id=1, source_target_pairs={{0,16},{16,0},{1,17},{17,1},{2,18},{18,2},{3,19},{19,3},{4,20},{20... | collective-permute-start | bytes 1474568 | tf_op jit(solution)/shard_map/ppermute | solution.py:34
  169.5 2.9 %fusion.46 = f32[640,640]{1,0:T(8,128)} fusion(bf16[1536,640]{1,0:T(8,128)(2,1)S(1)} %copy-done, bf16[1536,640]{1,0:T(8,128)(2,1)S(1)} %bitcast.88), kind=kOutput, calls=%fused_computation.92 | convolution fusion | flops 1258291200 | bytes 5570560 | tf_op jit(solution)/shard_map/dot_general | solution.py:28
  (65 shorter events, 26.9 us)
Async XLA Ops:
  7.2 11.2 %copy-start.4 = (bf16[96,640]{1,0:T(8,128)(2,1)S(1)}, bf16[96,640]{1,0:T(8,128)(2,1)}, u32[]{:S(2)}) copy-start(bf16[96,640]{1,0:T(8,128)(2,1)} %param.7) | copy-start | bytes 368644
  7.2 132.4 %all-gather.5.cloned.1.call-start = ((), (), s32[]{:S(2)}) async-start(), calls=%async_computation.6 | async-start | bytes 2027520 | tf_op jit(solution)/shard_map/all_gather | solution.py:61
  9.5 17.3 %all-to-all-start = ((bf16[8,24,640]{2,1,0:T(8,128)(2,1)}), bf16[8,24,640]{2,1,0:T(8,128)(2,1)S(1)}, u32[]{:S(2)}, u32[]{:S(2)}) async-start(bf16[8,24,640]{2,1,0:T(8,128)(2,1)} %bitcast.1), calls=%async_computation | async-start | bytes 491520 | tf_op jit(solution)/shard_map/all_to_all | solution.py:67
  18.4 28.2 %collective-permute-start.1 = (bf16[736,640]{1,0:T(8,128)(2,1)S(1)}, bf16[736,640]{1,0:T(8,128)(2,1)}, u32[]{:S(2)}, u32[]{:S(2)}) collective-permute-start(bf16[736,640]{1,0:T(8,128)(2,1)S(1)} %constant_dynamic-update-slice_fusion), channel_id=1, source_target_pairs={{0,1},{1,0},{2,3},{3,2},{4,5},{5,4},{6,7},{7,6},{8,9},{9,8},{10,11... | collective-permute-start | bytes 2826248 | tf_op jit(solution)/shard_map/ppermute | solution.py:34
  21.7 30.7 %collective-permute-start = (bf16[736,640]{1,0:T(8,128)(2,1)S(1)}, bf16[736,640]{1,0:T(8,128)(2,1)S(1)}, u32[]{:S(2)}, u32[]{:S(2)}) collective-permute-start(bf16[736,640]{1,0:T(8,128)(2,1)S(1)} %constant_dynamic-update-slice_fusion), channel_id=1, source_target_pairs={{0,16},{16,0},{1,17},{17,1},{2,18},{18,2},{3,19},{19,3},{4,20},{20... | collective-permute-start | bytes 2826248 | tf_op jit(solution)/shard_map/ppermute | solution.py:34
  27.9 26.6 %all-to-all-start.1 = ((bf16[4,4,24,1280]{3,2,1,0:T(8,128)(2,1)}), bf16[4,4,24,1280]{3,2,1,0:T(8,128)(2,1)S(1)}, u32[]{:S(2)}, u32[]{:S(2)}) async-start(bf16[4,4,24,1280]{3,2,1,0:T(8,128)(2,1)} %broadcast_in_dim.7), calls=%async_computation.1 | async-start | bytes 1966080 | tf_op jit(solution)/shard_map/all_to_all | solution.py:70
  46.6 11.3 %collective-permute-start.2 = (bf16[736,640]{1,0:T(8,128)(2,1)}, bf16[736,640]{1,0:T(8,128)(2,1)}, u32[]{:S(2)}, u32[]{:S(2)}) collective-permute-start(bf16[736,640]{1,0:T(8,128)(2,1)} %collective-permute-done.1), channel_id=1, source_target_pairs={{0,16},{16,0},{1,17},{17,1},{2,18},{18,2},{3,19},{19,3},{4,20},{20... | collective-permute-start | bytes 2826248 | tf_op jit(solution)/shard_map/ppermute | solution.py:34
  52.5 2.1 %copy-start.1 = (bf16[736,640]{1,0:T(8,128)(2,1)}, bf16[736,640]{1,0:T(8,128)(2,1)S(1)}, u32[]{:S(2)}) copy-start(bf16[736,640]{1,0:T(8,128)(2,1)S(1)} %collective-permute-done) | copy-start | bytes 2826244
  54.5 1.1 copy-start.3
  55.7 3.4 %copy-start.2 = (bf16[640,640]{1,0:T(8,128)(2,1)S(1)}, bf16[640,640]{1,0:T(8,128)(2,1)}, u32[]{:S(2)}) copy-start(bf16[640,640]{1,0:T(8,128)(2,1)} %slice.109) | copy-start | bytes 2457604
  61.1 37.6 %all-to-all-start.2 = ((bf16[8,48,1280]{2,1,0:T(8,128)(2,1)}), bf16[8,48,1280]{2,1,0:T(8,128)(2,1)S(1)}, u32[]{:S(2)}, u32[]{:S(2)}) async-start(bf16[8,48,1280]{2,1,0:T(8,128)(2,1)} %bitcast.11), calls=%async_computation.2 | async-start | bytes 1966080 | tf_op jit(solution)/shard_map/all_to_all | solution.py:86
  70.8 70.3 %all-gather.3.cloned.1.call-start = ((), (), s32[]{:S(2)}) async-start(), calls=%async_computation.5 | async-start | bytes 2211840 | tf_op jit(solution)/shard_map/all_gather | solution.py:107
  71.8 14.7 %collective-permute-start.3 = (bf16[4,4,24,640]{3,2,1,0:T(8,128)(2,1)S(1)}, bf16[4,4,24,640]{3,2,1,0:T(8,128)(2,1)S(1)}, u32[]{:S(2)}, u32[]{:S(2)}) collective-permute-start(bf16[4,4,24,640]{3,2,1,0:T(8,128)(2,1)S(1)} %slice.122), channel_id=1, source_target_pairs={{0,1},{1,0},{2,3},{3,2},{4,5},{5,4},{6,7},{7,6},{8,9},{9,8},{10,11... | collective-permute-start | bytes 1474568 | tf_op jit(solution)/shard_map/ppermute | solution.py:34
  86.5 42.5 %collective-permute-start.4 = (bf16[640,640]{1,0:T(8,128)(2,1)}, bf16[640,640]{1,0:T(8,128)(2,1)}, u32[]{:S(2)}, u32[]{:S(2)}) collective-permute-start(bf16[640,640]{1,0:T(8,128)(2,1)} %param.8), channel_id=1, source_target_pairs={{0,16},{16,0},{1,17},{17,1},{2,18},{18,2},{3,19},{19,3},{4,20},{20... | collective-permute-start | bytes 2457608 | tf_op jit(solution)/shard_map/ppermute | solution.py:34
  89.3 39.8 %collective-permute-start.5 = (bf16[640,640]{1,0:T(8,128)(2,1)}, bf16[640,640]{1,0:T(8,128)(2,1)}, u32[]{:S(2)}, u32[]{:S(2)}) collective-permute-start(bf16[640,640]{1,0:T(8,128)(2,1)} %param.8), channel_id=1, source_target_pairs={{0,1},{1,0},{2,3},{3,2},{4,5},{5,4},{6,7},{7,6},{8,9},{9,8},{10,11... | collective-permute-start | bytes 2457608 | tf_op jit(solution)/shard_map/ppermute | solution.py:34
  91.6 37.7 %collective-permute-start.6 = (bf16[640,640]{1,0:T(8,128)(2,1)}, bf16[640,640]{1,0:T(8,128)(2,1)}, u32[]{:S(2)}, u32[]{:S(2)}) collective-permute-start(bf16[640,640]{1,0:T(8,128)(2,1)} %param.8), channel_id=1, source_target_pairs={{0,17},{1,16},{16,1},{17,0},{2,19},{3,18},{18,3},{19,2},{4,21},{5,... | collective-permute-start | bytes 2457608 | tf_op jit(solution)/shard_map/ppermute | solution.py:42
  95.9 42.0 %collective-permute-start.7 = (bf16[4,4,2,24,640]{4,3,1,0,2:T(8,128)(2,1)}, bf16[4,4,2,24,640]{4,3,1,0,2:T(8,128)(2,1)}, u32[]{:S(2)}, u32[]{:S(2)}) collective-permute-start(bf16[4,4,2,24,640]{4,3,1,0,2:T(8,128)(2,1)} %pad_maximum_fusion.2), channel_id=1, source_target_pairs={{0,16},{16,0},{1,17},{17,1},{2,18},{18,2},{3,19},{19,3},{4,20},{20... | collective-permute-start | bytes 2949128 | tf_op jit(solution)/shard_map/ppermute | solution.py:34
  126.3 28.1 %collective-permute-start.8 = (bf16[384,1280]{1,0:T(8,128)(2,1)}, bf16[384,1280]{1,0:T(8,128)(2,1)}, u32[]{:S(2)}, u32[]{:S(2)}) collective-permute-start(bf16[384,1280]{1,0:T(8,128)(2,1)} %all_gather.9), channel_id=1, source_target_pairs={{0,1},{1,0},{2,3},{3,2},{4,5},{5,4},{6,7},{7,6},{8,9},{9,8},{10,11... | collective-permute-start | bytes 2949128 | tf_op jit(solution)/shard_map/ppermute | solution.py:34
  134.0 13.4 %all-to-all-start.3 = ((bf16[4,4,24,1280]{3,2,1,0:T(8,128)(2,1)}), bf16[4,4,24,1280]{3,2,1,0:T(8,128)(2,1)S(1)}, u32[]{:S(2)}, u32[]{:S(2)}) async-start(bf16[4,4,24,1280]{3,2,1,0:T(8,128)(2,1)} %bitcast.84), calls=%async_computation.3 | async-start | bytes 1966080 | tf_op jit(solution)/shard_map/all_to_all | solution.py:120
  148.3 17.4 %all-to-all-start.4 = ((bf16[8,24,640]{2,1,0:T(8,128)(2,1)}), bf16[8,24,640]{2,1,0:T(8,128)(2,1)S(1)}, u32[]{:S(2)}, u32[]{:S(2)}) async-start(bf16[8,24,640]{2,1,0:T(8,128)(2,1)} %bitcast.35), calls=%async_computation.4 | async-start | bytes 491520 | tf_op jit(solution)/shard_map/all_to_all | solution.py:126
  156.0 10.3 %collective-permute-start.10 = (bf16[384,640]{1,0:T(8,128)(2,1)S(1)}, bf16[384,640]{1,0:T(8,128)(2,1)S(1)}, u32[]{:S(2)}, u32[]{:S(2)}) collective-permute-start(bf16[384,640]{1,0:T(8,128)(2,1)S(1)} %get-tuple-element.26), channel_id=1, source_target_pairs={{0,16},{16,0},{1,17},{17,1},{2,18},{18,2},{3,19},{19,3},{4,20},{20... | collective-permute-start | bytes 1474568 | tf_op jit(solution)/shard_map/ppermute | solution.py:34
  163.8 3.8 %collective-permute-start.9 = (bf16[384,640]{1,0:T(8,128)(2,1)S(1)}, bf16[384,640]{1,0:T(8,128)(2,1)S(1)}, u32[]{:S(2)}, u32[]{:S(2)}) collective-permute-start(bf16[384,640]{1,0:T(8,128)(2,1)S(1)} %get-tuple-element.25), channel_id=1, source_target_pairs={{0,16},{16,0},{1,17},{17,1},{2,18},{18,2},{3,19},{19,3},{4,20},{20... | collective-permute-start | bytes 1474568 | tf_op jit(solution)/shard_map/ppermute | solution.py:34
  167.9 1.5 copy-start
Sparse Core Ops, SparseCore 0:
  11.2 67.4 all-gather.4
  80.8 43.3 all-gather.2

commit v9 on v7

--- a/solution.py
+++ b/solution.py
@@ -112,6 +112,7 @@
     down_grad = over_tokens(act_all, after(grad_all, input_all).reshape(-1, width))
 
     part_in = times_transposed(slopes, up_cat).astype(BF16)
+    slopes_core = swap(after(slopes, part_in), "c")
     part_in = jnp.swapaxes(part_in.reshape(4, 4, half, 2 * width), 0, 1)
     blocks = lax.all_to_all(part_in, "x", 0, 0)
     blocks = after(blocks, down_grad)
@@ -119,13 +120,10 @@
     part_y = jnp.stack(
         in_order(lane, part_y[..., :width], part_y[..., width:]), axis=1
     )
-    blocks = lax.all_to_all(part_y.reshape(8, half, width), ("yh", "yl"), 0, 0)
-    input_grad = jnp.sum(blocks.reshape(4, rows, width).astype(F32), axis=0).astype(BF16)
-
-    slopes_lane = swap(slopes, "yl")
+    slopes_lane = after(swap(slopes, "yl"), part_y)
     own = (slopes[:, :hidden], slopes_lane[:, :hidden])
     other = (
-        swap(slopes[:, hidden:], "c"),
+        slopes_core[:, hidden:],
         swap(slopes_lane[:, hidden:], "c"),
     )
     by_core = [
@@ -134,6 +132,8 @@
     ]
     slopes_all = jnp.stack(in_order(core, by_core[0], by_core[1]), axis=1)
     up_grad = over_tokens(after(input_all, slopes_lane), slopes_all.reshape(-1, hidden))
+    blocks = lax.all_to_all(part_y.reshape(8, half, width), ("yh", "yl"), 0, 0)
+    input_grad = jnp.sum(after(blocks, up_grad).reshape(4, rows, width).astype(F32), axis=0).astype(BF16)
     return (input_grad, up_grad, down_grad)
 
 

time: 176 us -> 179 us (1.017)
  waiting for transfers between devices: 29.4 us -> 33.2 us
    all_to_all x1, waiting for transfers between devices: 0.01 us -> 6.1 us  [per_device(): blocks = lax.all_to_all(part_y.reshape(8, half, width), ('yh', 'yl'), 0, 0)]
  transfers between devices with their start and end apart: 20 -> 20, of which waited for: 6 -> 5; matrix products, arithmetic and copies ran while one was open for 15% -> 17% of each run, Pallas kernels for 0% -> 0%
where the time goes in v9:
time: 179 us; the launch traced here: 178 us
  starting transfers between devices  71.7 us (40%)
  waiting for transfers between devices  33.2 us (19%)
  blocking collectives  26.3 us (15%)
  matrix products  17 us (9%)
  between operations  14.4 us (8%)
  other arithmetic  8.64 us (5%)
  local copies, waits for them, and re-layouts  6.47 us (4%)
    ppermute x12, starting transfers between devices, swap(): return lax.ppermute(values, axis, [(0, 1), (1, 0)])  38.8 us
    all_gather x1, blocking collectives, per_device(): slopes = lax.all_gather(slope_tile, 'z', axis=0, tiled=True)  26.3 us
    ppermute x12, waiting for transfers between devices, swap(): return lax.ppermute(values, axis, [(0, 1), (1, 0)])  19.7 us
    dot_general x3, matrix products, times_transposed(): lax.dot_general(left, right, (((1,), (1,)), ((), ())), preferred_element_...  9.1 us
    all_to_all x1, starting transfers between devices, per_device(): blocks = lax.all_to_all(part.reshape(8, rows, 2 * hidden), 'z', 0, 0)  8.61 us
    dot_general x2, matrix products, over_tokens(): lax.dot_general(left, right, (((0,), (0,)), ((), ())), preferred_element_...  7.94 us
    all_to_all x1, starting transfers between devices, per_device(): grad_y = lax.all_to_all(pieces.reshape(8, half, width), ('yh', 'yl'), 0, 0)  7.65 us
    all_to_all x1, waiting for transfers between devices, per_device(): blocks = lax.all_to_all(part.reshape(8, rows, 2 * hidden), 'z', 0, 0)  6.63 us
  transfers between devices with their start and end apart: 20, of which 5 were waited for; matrix products, arithmetic and copies ran while one was open for 17% of the time, Pallas kernels for 0%

profile of v9, /device:TPU:1, one launch (start us, length us, event | category | flops | bytes accessed | tf_op | source)
XLA Modules:
  0.0 177.7 jit_solution(229400028993419696)
XLA Ops:
  9.4 7.7 %all-to-all-start = ((bf16[8,24,640]{2,1,0:T(8,128)(2,1)}), bf16[8,24,640]{2,1,0:T(8,128)(2,1)S(1)}, u32[]{:S(2)}, u32[]{:S(2)}) async-start(bf16[8,24,640]{2,1,0:T(8,128)(2,1)} %bitcast.1), calls=%async_computation | async-start | bytes 491520 | tf_op jit(solution)/shard_map/all_to_all | solution.py:66
  17.1 3.4 %collective-permute-start = (bf16[96,640]{1,0:T(8,128)(2,1)}, bf16[96,640]{1,0:T(8,128)(2,1)S(1)}, u32[]{:S(2)}, u32[]{:S(2)}) collective-permute-start(bf16[96,640]{1,0:T(8,128)(2,1)} %param.7), channel_id=1, source_target_pairs={{0,1},{1,0},{2,3},{3,2},{4,5},{5,4},{6,7},{7,6},{8,9},{9,8},{10,11... | collective-permute-start | bytes 368648 | tf_op jit(solution)/shard_map/ppermute | solution.py:34
  20.5 5.0 %collective-permute-start.1 = (bf16[640,640]{1,0:T(8,128)(2,1)}, bf16[640,640]{1,0:T(8,128)(2,1)}, u32[]{:S(2)}, u32[]{:S(2)}) collective-permute-start(bf16[640,640]{1,0:T(8,128)(2,1)} %param.9), channel_id=1, source_target_pairs={{0,16},{16,0},{1,17},{17,1},{2,18},{18,2},{3,19},{19,3},{4,20},{20... | collective-permute-start | bytes 2457608 | tf_op jit(solution)/shard_map/ppermute | solution.py:34
  28.5 3.8 %all-to-all-start.1 = ((bf16[4,4,24,1280]{3,2,1,0:T(8,128)(2,1)}), bf16[4,4,24,1280]{3,2,1,0:T(8,128)(2,1)S(1)}, u32[]{:S(2)}, u32[]{:S(2)}) async-start(bf16[4,4,24,1280]{3,2,1,0:T(8,128)(2,1)} %broadcast_in_dim.7), calls=%async_computation.1 | async-start | bytes 1966080 | tf_op jit(solution)/shard_map/all_to_all | solution.py:70
  32.3 17.2 %collective-permute-done.2 = bf16[640,640]{1,0:T(8,128)(2,1)} collective-permute-done((bf16[640,640]{1,0:T(8,128)(2,1)}, bf16[640,640]{1,0:T(8,128)(2,1)}, u32[]{:S(2)}, u32[]{:S(2)}) %collective-permute-start.2) | collective-permute-done | bytes 819232 | tf_op jit(solution)/shard_map/ppermute | solution.py:34
  49.5 2.7 %collective-permute-start.3 = (bf16[640,640]{1,0:T(8,128)(2,1)}, bf16[640,640]{1,0:T(8,128)(2,1)}, u32[]{:S(2)}, u32[]{:S(2)}) collective-permute-start(bf16[640,640]{1,0:T(8,128)(2,1)} %collective-permute-done.2), channel_id=1, source_target_pairs={{0,16},{16,0},{1,17},{17,1},{2,18},{18,2},{3,19},{19,3},{4,20},{20... | collective-permute-start | bytes 2457608 | tf_op jit(solution)/shard_map/ppermute | solution.py:34
  52.4 2.1 %fusion.12 = f32[384,1280]{1,0:T(8,128)S(1)} fusion(bf16[640,640]{1,0:T(8,128)(2,1)} %collective-permute-done.1, bf16[640,640]{1,0:T(8,128)(2,1)S(1)} %copy-done.2, bf16[384,1280]{1,0:T(8,128)(2,1)S(1)} %bitcast.88), kind=kOutput, calls=%fused_computation.14 | convolution fusion | flops 632422400 | bytes 4096000 | tf_op jit(solution)/shard_map/dot_general | solution.py:22
  54.5 3.3 %fusion.8 = bf16[384,1280]{1,0:T(8,128)(2,1)} fusion(f32[384,1280]{1,0:T(8,128)S(1)} %fusion.12, bf16[640,640]{1,0:T(8,128)(2,1)} %collective-permute-done.3, bf16[640,640]{1,0:T(8,128)(2,1)} %collective-permute-done.2, bf16[384,1280]{1,0:T(8,128)(2,1)S(1)} %bitcast.89), kind=kOutput, calls=%fused_computation.9 | convolution fusion | flops 633405440 | bytes 5079040 | tf_op jit(solution)/shard_map/dot_general | solution.py:22
  57.9 8.6 %all-to-all-start.2 = ((bf16[8,48,1280]{2,1,0:T(8,128)(2,1)}), bf16[8,48,1280]{2,1,0:T(8,128)(2,1)S(1)}, u32[]{:S(2)}, u32[]{:S(2)}) async-start(bf16[8,48,1280]{2,1,0:T(8,128)(2,1)} %bitcast.11), calls=%async_computation.2 | async-start | bytes 1966080 | tf_op jit(solution)/shard_map/all_to_all | solution.py:83
  69.6 2.8 %collective-permute-start.4 = (bf16[2,24,640]{2,1,0:T(8,128)(2,1)S(1)}, bf16[2,24,640]{2,1,0:T(8,128)(2,1)S(1)}, u32[]{:S(2)}, u32[]{:S(2)}) collective-permute-start(bf16[2,24,640]{2,1,0:T(8,128)(2,1)S(1)} %fusion.38), channel_id=1, source_target_pairs={{0,16},{16,0},{1,17},{17,1},{2,18},{18,2},{3,19},{19,3},{4,20},{20... | collective-permute-start | bytes 184328 | tf_op jit(solution)/shard_map/ppermute | solution.py:34
  73.3 2.3 %collective-permute-start.5 = (bf16[640,640]{1,0:T(8,128)(2,1)}, bf16[640,640]{1,0:T(8,128)(2,1)}, u32[]{:S(2)}, u32[]{:S(2)}) collective-permute-start(bf16[640,640]{1,0:T(8,128)(2,1)} %param.8), channel_id=1, source_target_pairs={{0,16},{16,0},{1,17},{17,1},{2,18},{18,2},{3,19},{19,3},{4,20},{20... | collective-permute-start | bytes 2457608 | tf_op jit(solution)/shard_map/ppermute | solution.py:34
  75.6 3.3 %collective-permute-start.6 = (bf16[640,640]{1,0:T(8,128)(2,1)}, bf16[640,640]{1,0:T(8,128)(2,1)}, u32[]{:S(2)}, u32[]{:S(2)}) collective-permute-start(bf16[640,640]{1,0:T(8,128)(2,1)} %param.8), channel_id=1, source_target_pairs={{0,1},{1,0},{2,3},{3,2},{4,5},{5,4},{6,7},{7,6},{8,9},{9,8},{10,11... | collective-permute-start | bytes 2457608 | tf_op jit(solution)/shard_map/ppermute | solution.py:34
  78.8 2.4 %collective-permute-start.7 = (bf16[640,640]{1,0:T(8,128)(2,1)}, bf16[640,640]{1,0:T(8,128)(2,1)}, u32[]{:S(2)}, u32[]{:S(2)}) collective-permute-start(bf16[640,640]{1,0:T(8,128)(2,1)} %param.8), channel_id=1, source_target_pairs={{0,17},{1,16},{16,1},{17,0},{2,19},{3,18},{18,3},{19,2},{4,21},{5,... | collective-permute-start | bytes 2457608 | tf_op jit(solution)/shard_map/ppermute | solution.py:42
  84.0 3.6 %collective-permute-start.9 = (bf16[4,4,2,24,640]{4,3,1,0,2:T(8,128)(2,1)}, bf16[4,4,2,24,640]{4,3,1,0,2:T(8,128)(2,1)}, u32[]{:S(2)}, u32[]{:S(2)}) collective-permute-start(bf16[4,4,2,24,640]{4,3,1,0,2:T(8,128)(2,1)} %pad_maximum_fusion.2), channel_id=1, source_target_pairs={{0,16},{16,0},{1,17},{17,1},{2,18},{18,2},{3,19},{19,3},{4,20},{20... | collective-permute-start | bytes 2949128 | tf_op jit(solution)/shard_map/ppermute | solution.py:34
  87.6 6.6 %all-to-all-done.2 = bf16[8,48,1280]{2,1,0:T(8,128)(2,1)S(1)} async-done(((bf16[8,48,1280]{2,1,0:T(8,128)(2,1)}), bf16[8,48,1280]{2,1,0:T(8,128)(2,1)S(1)}, u32[]{:S(2)}, u32[]{:S(2)}) %all-to-all-start.2) | async-done | bytes 983072 | tf_op jit(solution)/shard_map/all_to_all | solution.py:83
  94.5 26.3 %all_gather.9 = bf16[384,1280]{1,0:T(8,128)(2,1)} all-gather(bf16[48,1280]{1,0:T(8,128)(2,1)S(1)} %fusion.32), channel_id=1, replica_groups=mesh['yh'=4,'x'=4,'c'=2,'z'=8,'yl'=2] {'z'}, dimensions={0}, use_global_device_ids=true | all-gather | bytes 1105920 | tf_op jit(solution)/shard_map/all_gather | solution.py:105
  122.7 3.6 %fusion.9 = bf16[384,1280]{1,0:T(8,128)(2,1)S(1)} fusion(bf16[384,1280]{1,0:T(8,128)(2,1)} %all_gather.9, bf16[640,640]{1,0:T(8,128)(2,1)} %collective-permute-done.7, bf16[640,640]{1,0:T(8,128)(2,1)} %collective-permute-done.6, bf16[640,640]{1,0:T(8,128)(2,1)} %collective-permute-done.5, bf16[640,640]{1,0:T(8,128)(2,1)} %param.8), kind=kOutput, calls=%fused_computation.10 | convolution fusion | flops 1271889920 | bytes 5242880 | tf_op jit(solution)/shard_map/dot_general | solution.py:22
  127.4 4.2 %all-to-all-start.3 = ((bf16[4,4,24,1280]{3,2,1,0:T(8,128)(2,1)}), bf16[4,4,24,1280]{3,2,1,0:T(8,128)(2,1)S(1)}, u32[]{:S(2)}, u32[]{:S(2)}) async-start(bf16[4,4,24,1280]{3,2,1,0:T(8,128)(2,1)} %bitcast.83), calls=%async_computation.3 | async-start | bytes 1966080 | tf_op jit(solution)/shard_map/all_to_all | solution.py:117
  133.2 7.5 %collective-permute-start.11 = (bf16[384,1280]{1,0:T(8,128)(2,1)}, bf16[384,1280]{1,0:T(8,128)(2,1)}, u32[]{:S(2)}, u32[]{:S(2)}) collective-permute-start(bf16[384,1280]{1,0:T(8,128)(2,1)} %all_gather.9), channel_id=1, source_target_pairs={{0,16},{16,0},{1,17},{17,1},{2,18},{18,2},{3,19},{19,3},{4,20},{20... | collective-permute-start | bytes 2949128 | tf_op jit(solution)/shard_map/ppermute | solution.py:34
  142.2 5.0 %fusion.43 = f32[640,640]{1,0:T(8,128)} fusion(bf16[1536,640]{1,0:T(8,128)(2,1)} %all-gather.3.cloned.1.call-done, bf16[1536,640]{1,0:T(8,128)(2,1)} %bitcast.86), kind=kOutput, calls=%fused_computation.82 | convolution fusion | flops 1258291200 | bytes 5570560 | tf_op jit(solution)/shard_map/dot_general | solution.py:28
  149.6 2.4 %collective-permute-start.12 = (bf16[384,640]{1,0:T(8,128)(2,1)S(1)}, bf16[384,640]{1,0:T(8,128)(2,1)S(1)}, u32[]{:S(2)}, u32[]{:S(2)}) collective-permute-start(bf16[384,640]{1,0:T(8,128)(2,1)S(1)} %get-tuple-element.31), channel_id=1, source_target_pairs={{0,16},{16,0},{1,17},{17,1},{2,18},{18,2},{3,19},{19,3},{4,20},{20... | collective-permute-start | bytes 1474568 | tf_op jit(solution)/shard_map/ppermute | solution.py:34
  151.9 6.3 %all-to-all-start.4 = ((bf16[8,24,640]{2,1,0:T(8,128)(2,1)}), bf16[8,24,640]{2,1,0:T(8,128)(2,1)S(1)}, u32[]{:S(2)}, u32[]{:S(2)}) async-start(bf16[8,24,640]{2,1,0:T(8,128)(2,1)} %bitcast.36), calls=%async_computation.4 | async-start | bytes 491520 | tf_op jit(solution)/shard_map/all_to_all | solution.py:135
  161.2 2.9 %fusion.44 = f32[640,640]{1,0:T(8,128)} fusion(bf16[1536,640]{1,0:T(8,128)(2,1)S(1)} %copy-done, bf16[1536,640]{1,0:T(8,128)(2,1)S(1)} %bitcast.87), kind=kOutput, calls=%fused_computation.83 | convolution fusion | flops 1258291200 | bytes 5570560 | tf_op jit(solution)/shard_map/dot_general | solution.py:28
  164.1 6.1 %all-to-all-done.4 = bf16[8,24,640]{2,1,0:T(8,128)(2,1)S(1)} async-done(((bf16[8,24,640]{2,1,0:T(8,128)(2,1)}), bf16[8,24,640]{2,1,0:T(8,128)(2,1)S(1)}, u32[]{:S(2)}, u32[]{:S(2)}) %all-to-all-start.4) | async-done | bytes 245792 | tf_op jit(solution)/shard_map/all_to_all | solution.py:135
  (60 shorter events, 24.3 us)
Async XLA Ops:
  7.2 133.5 %all-gather.5.cloned.1.call-start = ((), (), s32[]{:S(2)}) async-start(), calls=%async_computation.6 | async-start | bytes 2027520 | tf_op jit(solution)/shard_map/all_gather | solution.py:61
  9.4 18.0 %all-to-all-start = ((bf16[8,24,640]{2,1,0:T(8,128)(2,1)}), bf16[8,24,640]{2,1,0:T(8,128)(2,1)S(1)}, u32[]{:S(2)}, u32[]{:S(2)}) async-start(bf16[8,24,640]{2,1,0:T(8,128)(2,1)} %bitcast.1), calls=%async_computation | async-start | bytes 491520 | tf_op jit(solution)/shard_map/all_to_all | solution.py:66
  17.1 10.3 %collective-permute-start = (bf16[96,640]{1,0:T(8,128)(2,1)}, bf16[96,640]{1,0:T(8,128)(2,1)S(1)}, u32[]{:S(2)}, u32[]{:S(2)}) collective-permute-start(bf16[96,640]{1,0:T(8,128)(2,1)} %param.7), channel_id=1, source_target_pairs={{0,1},{1,0},{2,3},{3,2},{4,5},{5,4},{6,7},{7,6},{8,9},{9,8},{10,11... | collective-permute-start | bytes 368648 | tf_op jit(solution)/shard_map/ppermute | solution.py:34
  20.5 31.9 %collective-permute-start.1 = (bf16[640,640]{1,0:T(8,128)(2,1)}, bf16[640,640]{1,0:T(8,128)(2,1)}, u32[]{:S(2)}, u32[]{:S(2)}) collective-permute-start(bf16[640,640]{1,0:T(8,128)(2,1)} %param.9), channel_id=1, source_target_pairs={{0,16},{16,0},{1,17},{17,1},{2,18},{18,2},{3,19},{19,3},{4,20},{20... | collective-permute-start | bytes 2457608 | tf_op jit(solution)/shard_map/ppermute | solution.py:34
  25.5 24.1 %collective-permute-start.2 = (bf16[640,640]{1,0:T(8,128)(2,1)}, bf16[640,640]{1,0:T(8,128)(2,1)}, u32[]{:S(2)}, u32[]{:S(2)}) collective-permute-start(bf16[640,640]{1,0:T(8,128)(2,1)} %param.9), channel_id=1, source_target_pairs={{0,1},{1,0},{2,3},{3,2},{4,5},{5,4},{6,7},{7,6},{8,9},{9,8},{10,11... | collective-permute-start | bytes 2457608 | tf_op jit(solution)/shard_map/ppermute | solution.py:34
  27.5 24.8 %copy-start.1 = (bf16[96,640]{1,0:T(8,128)(2,1)S(1)}, bf16[96,640]{1,0:T(8,128)(2,1)}, u32[]{:S(2)}) copy-start(bf16[96,640]{1,0:T(8,128)(2,1)} %param.7) | copy-start | bytes 368644
  28.5 23.8 %copy-start.2 = (bf16[640,640]{1,0:T(8,128)(2,1)S(1)}, bf16[640,640]{1,0:T(8,128)(2,1)}, u32[]{:S(2)}) copy-start(bf16[640,640]{1,0:T(8,128)(2,1)} %param.9) | copy-start | bytes 2457604
  28.5 23.7 %all-to-all-start.1 = ((bf16[4,4,24,1280]{3,2,1,0:T(8,128)(2,1)}), bf16[4,4,24,1280]{3,2,1,0:T(8,128)(2,1)S(1)}, u32[]{:S(2)}, u32[]{:S(2)}) async-start(bf16[4,4,24,1280]{3,2,1,0:T(8,128)(2,1)} %broadcast_in_dim.7), calls=%async_computation.1 | async-start | bytes 1966080 | tf_op jit(solution)/shard_map/all_to_all | solution.py:70
  49.5 5.0 %collective-permute-start.3 = (bf16[640,640]{1,0:T(8,128)(2,1)}, bf16[640,640]{1,0:T(8,128)(2,1)}, u32[]{:S(2)}, u32[]{:S(2)}) collective-permute-start(bf16[640,640]{1,0:T(8,128)(2,1)} %collective-permute-done.2), channel_id=1, source_target_pairs={{0,16},{16,0},{1,17},{17,1},{2,18},{18,2},{3,19},{19,3},{4,20},{20... | collective-permute-start | bytes 2457608 | tf_op jit(solution)/shard_map/ppermute | solution.py:34
  57.9 36.4 %all-to-all-start.2 = ((bf16[8,48,1280]{2,1,0:T(8,128)(2,1)}), bf16[8,48,1280]{2,1,0:T(8,128)(2,1)S(1)}, u32[]{:S(2)}, u32[]{:S(2)}) async-start(bf16[8,48,1280]{2,1,0:T(8,128)(2,1)} %bitcast.11), calls=%async_computation.2 | async-start | bytes 1966080 | tf_op jit(solution)/shard_map/all_to_all | solution.py:83
  66.5 75.7 %all-gather.3.cloned.1.call-start = ((), (), s32[]{:S(2)}) async-start(), calls=%async_computation.5 | async-start | bytes 2211840 | tf_op jit(solution)/shard_map/all_gather | solution.py:101
  67.5 15.3 %collective-permute-start.8 = (bf16[4,4,24,640]{3,2,1,0:T(8,128)(2,1)S(1)}, bf16[4,4,24,640]{3,2,1,0:T(8,128)(2,1)S(1)}, u32[]{:S(2)}, u32[]{:S(2)}) collective-permute-start(bf16[4,4,24,640]{3,2,1,0:T(8,128)(2,1)S(1)} %slice.75), channel_id=1, source_target_pairs={{0,1},{1,0},{2,3},{3,2},{4,5},{5,4},{6,7},{7,6},{8,9},{9,8},{10,11... | collective-permute-start | bytes 1474568 | tf_op jit(solution)/shard_map/ppermute | solution.py:34
  69.6 3.7 %collective-permute-start.4 = (bf16[2,24,640]{2,1,0:T(8,128)(2,1)S(1)}, bf16[2,24,640]{2,1,0:T(8,128)(2,1)S(1)}, u32[]{:S(2)}, u32[]{:S(2)}) collective-permute-start(bf16[2,24,640]{2,1,0:T(8,128)(2,1)S(1)} %fusion.38), channel_id=1, source_target_pairs={{0,16},{16,0},{1,17},{17,1},{2,18},{18,2},{3,19},{19,3},{4,20},{20... | collective-permute-start | bytes 184328 | tf_op jit(solution)/shard_map/ppermute | solution.py:34
  73.3 49.4 %collective-permute-start.5 = (bf16[640,640]{1,0:T(8,128)(2,1)}, bf16[640,640]{1,0:T(8,128)(2,1)}, u32[]{:S(2)}, u32[]{:S(2)}) collective-permute-start(bf16[640,640]{1,0:T(8,128)(2,1)} %param.8), channel_id=1, source_target_pairs={{0,16},{16,0},{1,17},{17,1},{2,18},{18,2},{3,19},{19,3},{4,20},{20... | collective-permute-start | bytes 2457608 | tf_op jit(solution)/shard_map/ppermute | solution.py:34
  75.6 47.1 %collective-permute-start.6 = (bf16[640,640]{1,0:T(8,128)(2,1)}, bf16[640,640]{1,0:T(8,128)(2,1)}, u32[]{:S(2)}, u32[]{:S(2)}) collective-permute-start(bf16[640,640]{1,0:T(8,128)(2,1)} %param.8), channel_id=1, source_target_pairs={{0,1},{1,0},{2,3},{3,2},{4,5},{5,4},{6,7},{7,6},{8,9},{9,8},{10,11... | collective-permute-start | bytes 2457608 | tf_op jit(solution)/shard_map/ppermute | solution.py:34
  78.8 43.9 %collective-permute-start.7 = (bf16[640,640]{1,0:T(8,128)(2,1)}, bf16[640,640]{1,0:T(8,128)(2,1)}, u32[]{:S(2)}, u32[]{:S(2)}) collective-permute-start(bf16[640,640]{1,0:T(8,128)(2,1)} %param.8), channel_id=1, source_target_pairs={{0,17},{1,16},{16,1},{17,0},{2,19},{3,18},{18,3},{19,2},{4,21},{5,... | collective-permute-start | bytes 2457608 | tf_op jit(solution)/shard_map/ppermute | solution.py:42
  84.0 47.6 %collective-permute-start.9 = (bf16[4,4,2,24,640]{4,3,1,0,2:T(8,128)(2,1)}, bf16[4,4,2,24,640]{4,3,1,0,2:T(8,128)(2,1)}, u32[]{:S(2)}, u32[]{:S(2)}) collective-permute-start(bf16[4,4,2,24,640]{4,3,1,0,2:T(8,128)(2,1)} %pad_maximum_fusion.2), channel_id=1, source_target_pairs={{0,16},{16,0},{1,17},{17,1},{2,18},{18,2},{3,19},{19,3},{4,20},{20... | collective-permute-start | bytes 2949128 | tf_op jit(solution)/shard_map/ppermute | solution.py:34
  120.8 27.4 %collective-permute-start.10 = (bf16[384,1280]{1,0:T(8,128)(2,1)}, bf16[384,1280]{1,0:T(8,128)(2,1)}, u32[]{:S(2)}, u32[]{:S(2)}) collective-permute-start(bf16[384,1280]{1,0:T(8,128)(2,1)} %all_gather.9), channel_id=1, source_target_pairs={{0,1},{1,0},{2,3},{3,2},{4,5},{5,4},{6,7},{7,6},{8,9},{9,8},{10,11... | collective-permute-start | bytes 2949128 | tf_op jit(solution)/shard_map/ppermute | solution.py:34
  127.4 19.8 %all-to-all-start.3 = ((bf16[4,4,24,1280]{3,2,1,0:T(8,128)(2,1)}), bf16[4,4,24,1280]{3,2,1,0:T(8,128)(2,1)S(1)}, u32[]{:S(2)}, u32[]{:S(2)}) async-start(bf16[4,4,24,1280]{3,2,1,0:T(8,128)(2,1)} %bitcast.83), calls=%async_computation.3 | async-start | bytes 1966080 | tf_op jit(solution)/shard_map/all_to_all | solution.py:117
  133.2 25.0 %collective-permute-start.11 = (bf16[384,1280]{1,0:T(8,128)(2,1)}, bf16[384,1280]{1,0:T(8,128)(2,1)}, u32[]{:S(2)}, u32[]{:S(2)}) collective-permute-start(bf16[384,1280]{1,0:T(8,128)(2,1)} %all_gather.9), channel_id=1, source_target_pairs={{0,16},{16,0},{1,17},{17,1},{2,18},{18,2},{3,19},{19,3},{4,20},{20... | collective-permute-start | bytes 2949128 | tf_op jit(solution)/shard_map/ppermute | solution.py:34
  149.6 8.6 %collective-permute-start.12 = (bf16[384,640]{1,0:T(8,128)(2,1)S(1)}, bf16[384,640]{1,0:T(8,128)(2,1)S(1)}, u32[]{:S(2)}, u32[]{:S(2)}) collective-permute-start(bf16[384,640]{1,0:T(8,128)(2,1)S(1)} %get-tuple-element.31), channel_id=1, source_target_pairs={{0,16},{16,0},{1,17},{17,1},{2,18},{18,2},{3,19},{19,3},{4,20},{20... | collective-permute-start | bytes 1474568 | tf_op jit(solution)/shard_map/ppermute | solution.py:34
  151.9 18.3 %all-to-all-start.4 = ((bf16[8,24,640]{2,1,0:T(8,128)(2,1)}), bf16[8,24,640]{2,1,0:T(8,128)(2,1)S(1)}, u32[]{:S(2)}, u32[]{:S(2)}) async-start(bf16[8,24,640]{2,1,0:T(8,128)(2,1)} %bitcast.36), calls=%async_computation.4 | async-start | bytes 491520 | tf_op jit(solution)/shard_map/all_to_all | solution.py:135
  159.6 1.5 copy-start
Sparse Core Ops, SparseCore 0:
  11.2 65.5 all-gather.4
  78.8 43.8 all-gather.2

commit v10 on v7

--- a/solution.py
+++ b/solution.py
@@ -60,7 +60,6 @@
 
     input_all = lax.all_gather(layer_input, WIDE, axis=0, tiled=True)
 
-    down_core = swap(w_down, "c")
     down_lane = swap(w_down, "yl")
     pieces = jnp.broadcast_to(output_grad.reshape(2, half, width), (4, 2, half, width))
     grad_y = lax.all_to_all(pieces.reshape(8, half, width), ("yh", "yl"), 0, 0)
@@ -71,6 +70,7 @@
         jnp.broadcast_to(grad_y, (4, 4, half, 2 * width)), "x", 0, 0
     )
     grad_xy = jnp.swapaxes(grad_xy, 0, 1)
+    down_core = swap(after(w_down, grad_y), "c")
     down_both = swap(down_lane, "c")
     grad_rows = grad_xy.reshape(-1, 2 * width)
     part = times_transposed(
@@ -112,6 +112,7 @@
     down_grad = over_tokens(act_all, after(grad_all, input_all).reshape(-1, width))
 
     part_in = times_transposed(slopes, up_cat).astype(BF16)
+    slopes_core = swap(after(slopes, part_in), "c")
     part_in = jnp.swapaxes(part_in.reshape(4, 4, half, 2 * width), 0, 1)
     blocks = lax.all_to_all(part_in, "x", 0, 0)
     blocks = after(blocks, down_grad)
@@ -125,7 +126,7 @@
     slopes_lane = swap(slopes, "yl")
     own = (slopes[:, :hidden], slopes_lane[:, :hidden])
     other = (
-        swap(slopes[:, hidden:], "c"),
+        slopes_core[:, hidden:],
         swap(slopes_lane[:, hidden:], "c"),
     )
     by_core = [

time: 176 us -> 180 us (1.023)
  starting transfers between devices: 72.7 us -> 75.7 us
    ppermute x12, waiting for transfers between devices: 20.9 us -> 11.4 us  [swap(): return lax.ppermute(values, axis, [(0, 1), (1, 0)])]
    all_to_all x1, waiting for transfers between devices: 0.01 us -> 6.3 us  [per_device(): blocks = lax.all_to_all(part_y.reshape(8, half, width), ('yh', 'yl'), 0, 0)]
    ppermute x12, starting transfers between devices: 39.3 us -> 44.4 us  [swap(): return lax.ppermute(values, axis, [(0, 1), (1, 0)])]
    all_to_all x1, waiting for transfers between devices: 0.01 us -> 3.03 us  [per_device(): lax.all_to_all(jnp.broadcast_to(grad_y, (4, 4, half, 2 * width)), 'x', 0, 0)]
  transfers between devices with their start and end apart: 20 -> 20, of which waited for: 6 -> 7; matrix products, arithmetic and copies ran while one was open for 15% -> 15% of each run, Pallas kernels for 0% -> 0%
where the time goes in v10:
time: 180 us; the launch traced here: 177 us
  starting transfers between devices  75.7 us (42%)
  waiting for transfers between devices  28.7 us (16%)
  blocking collectives  26.3 us (15%)
  matrix products  17 us (9%)
  between operations  14.4 us (8%)
  other arithmetic  8.65 us (5%)
  local copies, waits for them, and re-layouts  6.47 us (4%)
    ppermute x12, starting transfers between devices, swap(): return lax.ppermute(values, axis, [(0, 1), (1, 0)])  44.4 us
    all_gather x1, blocking collectives, per_device(): slopes = lax.all_gather(slope_tile, 'z', axis=0, tiled=True)  26.3 us
    ppermute x12, waiting for transfers between devices, swap(): return lax.ppermute(values, axis, [(0, 1), (1, 0)])  11.4 us
    all_to_all x1, starting transfers between devices, per_device(): blocks = lax.all_to_all(part.reshape(8, rows, 2 * hidden), 'z', 0, 0)  9.13 us
    dot_general x3, matrix products, times_transposed(): lax.dot_general(left, right, (((1,), (1,)), ((), ())), preferred_element_...  9.1 us
    dot_general x2, matrix products, over_tokens(): lax.dot_general(left, right, (((0,), (0,)), ((), ())), preferred_element_...  7.95 us
    all_to_all x1, starting transfers between devices, per_device(): grad_y = lax.all_to_all(pieces.reshape(8, half, width), ('yh', 'yl'), 0, 0)  7.65 us
    all_to_all x1, waiting for transfers between devices, per_device(): blocks = lax.all_to_all(part_y.reshape(8, half, width), ('yh', 'yl'), 0, 0)  6.3 us
  transfers between devices with their start and end apart: 20, of which 7 were waited for; matrix products, arithmetic and copies ran while one was open for 15% of the time, Pallas kernels for 0%

profile of v10, /device:TPU:1, one launch (start us, length us, event | category | flops | bytes accessed | tf_op | source)
XLA Modules:
  0.0 177.2 jit_solution(16680576362863032628)
XLA Ops:
  9.5 7.7 %all-to-all-start = ((bf16[8,24,640]{2,1,0:T(8,128)(2,1)}), bf16[8,24,640]{2,1,0:T(8,128)(2,1)S(1)}, u32[]{:S(2)}, u32[]{:S(2)}) async-start(bf16[8,24,640]{2,1,0:T(8,128)(2,1)} %bitcast.1), calls=%async_computation | async-start | bytes 491520 | tf_op jit(solution)/shard_map/all_to_all | solution.py:65
  17.1 3.4 %collective-permute-start = (bf16[96,640]{1,0:T(8,128)(2,1)}, bf16[96,640]{1,0:T(8,128)(2,1)S(1)}, u32[]{:S(2)}, u32[]{:S(2)}) collective-permute-start(bf16[96,640]{1,0:T(8,128)(2,1)} %param.7), channel_id=1, source_target_pairs={{0,1},{1,0},{2,3},{3,2},{4,5},{5,4},{6,7},{7,6},{8,9},{9,8},{10,11... | collective-permute-start | bytes 368648 | tf_op jit(solution)/shard_map/ppermute | solution.py:34
  22.4 3.0 %collective-permute-done = bf16[96,640]{1,0:T(8,128)(2,1)S(1)} collective-permute-done((bf16[96,640]{1,0:T(8,128)(2,1)}, bf16[96,640]{1,0:T(8,128)(2,1)S(1)}, u32[]{:S(2)}, u32[]{:S(2)}) %collective-permute-start) | collective-permute-done | bytes 122912 | tf_op jit(solution)/shard_map/ppermute | solution.py:34
  26.4 6.9 %collective-permute-start.1 = (bf16[640,640]{1,0:T(8,128)(2,1)S(1)}, bf16[640,640]{1,0:T(8,128)(2,1)}, u32[]{:S(2)}, u32[]{:S(2)}) collective-permute-start(bf16[640,640]{1,0:T(8,128)(2,1)S(1)} %copy-done.2), channel_id=1, source_target_pairs={{0,16},{16,0},{1,17},{17,1},{2,18},{18,2},{3,19},{19,3},{4,20},{20... | collective-permute-start | bytes 2457608 | tf_op jit(solution)/shard_map/ppermute | solution.py:34
  34.4 3.5 %all-to-all-start.1 = ((bf16[4,4,24,1280]{3,2,1,0:T(8,128)(2,1)}), bf16[4,4,24,1280]{3,2,1,0:T(8,128)(2,1)S(1)}, u32[]{:S(2)}, u32[]{:S(2)}) async-start(bf16[4,4,24,1280]{3,2,1,0:T(8,128)(2,1)} %broadcast_in_dim.7), calls=%async_computation.1 | async-start | bytes 1966080 | tf_op jit(solution)/shard_map/all_to_all | solution.py:69
  37.9 7.6 %collective-permute-done.2 = bf16[640,640]{1,0:T(8,128)(2,1)} collective-permute-done((bf16[640,640]{1,0:T(8,128)(2,1)}, bf16[640,640]{1,0:T(8,128)(2,1)}, u32[]{:S(2)}, u32[]{:S(2)}) %collective-permute-start.2) | collective-permute-done | bytes 819232 | tf_op jit(solution)/shard_map/ppermute | solution.py:34
  45.5 4.4 %collective-permute-start.3 = (bf16[640,640]{1,0:T(8,128)(2,1)}, bf16[640,640]{1,0:T(8,128)(2,1)}, u32[]{:S(2)}, u32[]{:S(2)}) collective-permute-start(bf16[640,640]{1,0:T(8,128)(2,1)} %collective-permute-done.2), channel_id=1, source_target_pairs={{0,16},{16,0},{1,17},{17,1},{2,18},{18,2},{3,19},{19,3},{4,20},{20... | collective-permute-start | bytes 2457608 | tf_op jit(solution)/shard_map/ppermute | solution.py:34
  49.9 3.0 %all-to-all-done.1 = bf16[4,4,24,1280]{3,2,1,0:T(8,128)(2,1)S(1)} async-done(((bf16[4,4,24,1280]{3,2,1,0:T(8,128)(2,1)}), bf16[4,4,24,1280]{3,2,1,0:T(8,128)(2,1)S(1)}, u32[]{:S(2)}, u32[]{:S(2)}) %all-to-all-start.1) | async-done | bytes 983072 | tf_op jit(solution)/shard_map/all_to_all | solution.py:69
  55.1 3.3 %fusion.8 = bf16[384,1280]{1,0:T(8,128)(2,1)} fusion(f32[384,1280]{1,0:T(8,128)S(1)} %fusion.12, bf16[640,640]{1,0:T(8,128)(2,1)} %collective-permute-done.3, bf16[640,640]{1,0:T(8,128)(2,1)} %collective-permute-done.2, bf16[384,1280]{1,0:T(8,128)(2,1)S(1)} %bitcast.89), kind=kOutput, calls=%fused_computation.9 | convolution fusion | flops 633405440 | bytes 5079040 | tf_op jit(solution)/shard_map/dot_general | solution.py:22
  58.5 9.1 %all-to-all-start.2 = ((bf16[8,48,1280]{2,1,0:T(8,128)(2,1)}), bf16[8,48,1280]{2,1,0:T(8,128)(2,1)S(1)}, u32[]{:S(2)}, u32[]{:S(2)}) async-start(bf16[8,48,1280]{2,1,0:T(8,128)(2,1)} %bitcast.11), calls=%async_computation.2 | async-start | bytes 1966080 | tf_op jit(solution)/shard_map/all_to_all | solution.py:83
  70.7 3.6 %collective-permute-start.4 = (bf16[2,24,640]{2,1,0:T(8,128)(2,1)S(1)}, bf16[2,24,640]{2,1,0:T(8,128)(2,1)S(1)}, u32[]{:S(2)}, u32[]{:S(2)}) collective-permute-start(bf16[2,24,640]{2,1,0:T(8,128)(2,1)S(1)} %fusion.38), channel_id=1, source_target_pairs={{0,16},{16,0},{1,17},{17,1},{2,18},{18,2},{3,19},{19,3},{4,20},{20... | collective-permute-start | bytes 184328 | tf_op jit(solution)/shard_map/ppermute | solution.py:34
  77.5 3.2 %collective-permute-start.6 = (bf16[640,640]{1,0:T(8,128)(2,1)}, bf16[640,640]{1,0:T(8,128)(2,1)}, u32[]{:S(2)}, u32[]{:S(2)}) collective-permute-start(bf16[640,640]{1,0:T(8,128)(2,1)} %param.8), channel_id=1, source_target_pairs={{0,1},{1,0},{2,3},{3,2},{4,5},{5,4},{6,7},{7,6},{8,9},{9,8},{10,11... | collective-permute-start | bytes 2457608 | tf_op jit(solution)/shard_map/ppermute | solution.py:34
  80.7 2.4 %collective-permute-start.7 = (bf16[640,640]{1,0:T(8,128)(2,1)}, bf16[640,640]{1,0:T(8,128)(2,1)}, u32[]{:S(2)}, u32[]{:S(2)}) collective-permute-start(bf16[640,640]{1,0:T(8,128)(2,1)} %param.8), channel_id=1, source_target_pairs={{0,17},{1,16},{16,1},{17,0},{2,19},{3,18},{18,3},{19,2},{4,21},{5,... | collective-permute-start | bytes 2457608 | tf_op jit(solution)/shard_map/ppermute | solution.py:42
  84.3 4.8 %collective-permute-start.9 = (bf16[4,4,2,24,640]{4,3,1,0,2:T(8,128)(2,1)}, bf16[4,4,2,24,640]{4,3,1,0,2:T(8,128)(2,1)}, u32[]{:S(2)}, u32[]{:S(2)}) collective-permute-start(bf16[4,4,2,24,640]{4,3,1,0,2:T(8,128)(2,1)} %pad_maximum_fusion.2), channel_id=1, source_target_pairs={{0,16},{16,0},{1,17},{17,1},{2,18},{18,2},{3,19},{19,3},{4,20},{20... | collective-permute-start | bytes 2949128 | tf_op jit(solution)/shard_map/ppermute | solution.py:34
  89.1 6.3 %all-to-all-done.2 = bf16[8,48,1280]{2,1,0:T(8,128)(2,1)S(1)} async-done(((bf16[8,48,1280]{2,1,0:T(8,128)(2,1)}), bf16[8,48,1280]{2,1,0:T(8,128)(2,1)S(1)}, u32[]{:S(2)}, u32[]{:S(2)}) %all-to-all-start.2) | async-done | bytes 983072 | tf_op jit(solution)/shard_map/all_to_all | solution.py:83
  95.7 26.3 %all_gather.9 = bf16[384,1280]{1,0:T(8,128)(2,1)} all-gather(bf16[48,1280]{1,0:T(8,128)(2,1)S(1)} %fusion.32), channel_id=1, replica_groups=mesh['yh'=4,'x'=4,'c'=2,'z'=8,'yl'=2] {'z'}, dimensions={0}, use_global_device_ids=true | all-gather | bytes 1105920 | tf_op jit(solution)/shard_map/all_gather | solution.py:105
  124.3 3.7 %fusion.9 = bf16[384,1280]{1,0:T(8,128)(2,1)S(1)} fusion(bf16[384,1280]{1,0:T(8,128)(2,1)} %all_gather.9, bf16[640,640]{1,0:T(8,128)(2,1)} %collective-permute-done.7, bf16[640,640]{1,0:T(8,128)(2,1)} %collective-permute-done.6, bf16[640,640]{1,0:T(8,128)(2,1)} %collective-permute-done.5, bf16[640,640]{1,0:T(8,128)(2,1)} %param.8), kind=kOutput, calls=%fused_computation.10 | convolution fusion | flops 1271889920 | bytes 5242880 | tf_op jit(solution)/shard_map/dot_general | solution.py:22
  128.9 3.5 %all-to-all-start.3 = ((bf16[4,4,24,1280]{3,2,1,0:T(8,128)(2,1)}), bf16[4,4,24,1280]{3,2,1,0:T(8,128)(2,1)S(1)}, u32[]{:S(2)}, u32[]{:S(2)}) async-start(bf16[4,4,24,1280]{3,2,1,0:T(8,128)(2,1)} %bitcast.83), calls=%async_computation.3 | async-start | bytes 1966080 | tf_op jit(solution)/shard_map/all_to_all | solution.py:117
  134.1 6.9 %collective-permute-start.11 = (bf16[384,1280]{1,0:T(8,128)(2,1)}, bf16[384,1280]{1,0:T(8,128)(2,1)}, u32[]{:S(2)}, u32[]{:S(2)}) collective-permute-start(bf16[384,1280]{1,0:T(8,128)(2,1)} %all_gather.9), channel_id=1, source_target_pairs={{0,16},{16,0},{1,17},{17,1},{2,18},{18,2},{3,19},{19,3},{4,20},{20... | collective-permute-start | bytes 2949128 | tf_op jit(solution)/shard_map/ppermute | solution.py:34
  142.5 5.0 %fusion.43 = f32[640,640]{1,0:T(8,128)} fusion(bf16[1536,640]{1,0:T(8,128)(2,1)} %all-gather.3.cloned.1.call-done, bf16[1536,640]{1,0:T(8,128)(2,1)} %bitcast.86), kind=kOutput, calls=%fused_computation.82 | convolution fusion | flops 1258291200 | bytes 5570560 | tf_op jit(solution)/shard_map/dot_general | solution.py:28
  148.5 5.0 %all-to-all-start.4 = ((bf16[8,24,640]{2,1,0:T(8,128)(2,1)}), bf16[8,24,640]{2,1,0:T(8,128)(2,1)S(1)}, u32[]{:S(2)}, u32[]{:S(2)}) async-start(bf16[8,24,640]{2,1,0:T(8,128)(2,1)} %bitcast.36), calls=%async_computation.4 | async-start | bytes 491520 | tf_op jit(solution)/shard_map/all_to_all | solution.py:123
  154.9 2.6 %collective-permute-start.12 = (bf16[384,640]{1,0:T(8,128)(2,1)S(1)}, bf16[384,640]{1,0:T(8,128)(2,1)S(1)}, u32[]{:S(2)}, u32[]{:S(2)}) collective-permute-start(bf16[384,640]{1,0:T(8,128)(2,1)S(1)} %get-tuple-element.29), channel_id=1, source_target_pairs={{0,16},{16,0},{1,17},{17,1},{2,18},{18,2},{3,19},{19,3},{4,20},{20... | collective-permute-start | bytes 1474568 | tf_op jit(solution)/shard_map/ppermute | solution.py:34
  157.6 6.3 %all-to-all-done.4 = bf16[8,24,640]{2,1,0:T(8,128)(2,1)S(1)} async-done(((bf16[8,24,640]{2,1,0:T(8,128)(2,1)}), bf16[8,24,640]{2,1,0:T(8,128)(2,1)S(1)}, u32[]{:S(2)}, u32[]{:S(2)}) %all-to-all-start.4) | async-done | bytes 245792 | tf_op jit(solution)/shard_map/all_to_all | solution.py:123
  167.5 2.9 %fusion.44 = f32[640,640]{1,0:T(8,128)} fusion(bf16[1536,640]{1,0:T(8,128)(2,1)S(1)} %copy-done, bf16[1536,640]{1,0:T(8,128)(2,1)S(1)} %bitcast.87), kind=kOutput, calls=%fused_computation.83 | convolution fusion | flops 1258291200 | bytes 5570560 | tf_op jit(solution)/shard_map/dot_general | solution.py:28
  (60 shorter events, 28.4 us)
Async XLA Ops:
  7.2 19.2 %copy-start.2 = (bf16[640,640]{1,0:T(8,128)(2,1)S(1)}, bf16[640,640]{1,0:T(8,128)(2,1)}, u32[]{:S(2)}) copy-start(bf16[640,640]{1,0:T(8,128)(2,1)} %param.9) | copy-start | bytes 2457604
  7.2 133.9 %all-gather.5.cloned.1.call-start = ((), (), s32[]{:S(2)}) async-start(), calls=%async_computation.6 | async-start | bytes 2027520 | tf_op jit(solution)/shard_map/all_gather | solution.py:61
  9.5 16.9 %all-to-all-start = ((bf16[8,24,640]{2,1,0:T(8,128)(2,1)}), bf16[8,24,640]{2,1,0:T(8,128)(2,1)S(1)}, u32[]{:S(2)}, u32[]{:S(2)}) async-start(bf16[8,24,640]{2,1,0:T(8,128)(2,1)} %bitcast.1), calls=%async_computation | async-start | bytes 491520 | tf_op jit(solution)/shard_map/all_to_all | solution.py:65
  17.1 8.3 %collective-permute-start = (bf16[96,640]{1,0:T(8,128)(2,1)}, bf16[96,640]{1,0:T(8,128)(2,1)S(1)}, u32[]{:S(2)}, u32[]{:S(2)}) collective-permute-start(bf16[96,640]{1,0:T(8,128)(2,1)} %param.7), channel_id=1, source_target_pairs={{0,1},{1,0},{2,3},{3,2},{4,5},{5,4},{6,7},{7,6},{8,9},{9,8},{10,11... | collective-permute-start | bytes 368648 | tf_op jit(solution)/shard_map/ppermute | solution.py:34
  20.5 25.0 %collective-permute-start.2 = (bf16[640,640]{1,0:T(8,128)(2,1)}, bf16[640,640]{1,0:T(8,128)(2,1)}, u32[]{:S(2)}, u32[]{:S(2)}) collective-permute-start(bf16[640,640]{1,0:T(8,128)(2,1)} %param.9), channel_id=1, source_target_pairs={{0,1},{1,0},{2,3},{3,2},{4,5},{5,4},{6,7},{7,6},{8,9},{9,8},{10,11... | collective-permute-start | bytes 2457608 | tf_op jit(solution)/shard_map/ppermute | solution.py:34
  26.3 23.5 %copy-start.1 = (bf16[96,640]{1,0:T(8,128)(2,1)S(1)}, bf16[96,640]{1,0:T(8,128)(2,1)}, u32[]{:S(2)}) copy-start(bf16[96,640]{1,0:T(8,128)(2,1)} %param.7) | copy-start | bytes 368644
  26.4 26.6 %collective-permute-start.1 = (bf16[640,640]{1,0:T(8,128)(2,1)S(1)}, bf16[640,640]{1,0:T(8,128)(2,1)}, u32[]{:S(2)}, u32[]{:S(2)}) collective-permute-start(bf16[640,640]{1,0:T(8,128)(2,1)S(1)} %copy-done.2), channel_id=1, source_target_pairs={{0,16},{16,0},{1,17},{17,1},{2,18},{18,2},{3,19},{19,3},{4,20},{20... | collective-permute-start | bytes 2457608 | tf_op jit(solution)/shard_map/ppermute | solution.py:34
  34.4 18.5 %all-to-all-start.1 = ((bf16[4,4,24,1280]{3,2,1,0:T(8,128)(2,1)}), bf16[4,4,24,1280]{3,2,1,0:T(8,128)(2,1)S(1)}, u32[]{:S(2)}, u32[]{:S(2)}) async-start(bf16[4,4,24,1280]{3,2,1,0:T(8,128)(2,1)} %broadcast_in_dim.7), calls=%async_computation.1 | async-start | bytes 1966080 | tf_op jit(solution)/shard_map/all_to_all | solution.py:69
  45.5 9.7 %collective-permute-start.3 = (bf16[640,640]{1,0:T(8,128)(2,1)}, bf16[640,640]{1,0:T(8,128)(2,1)}, u32[]{:S(2)}, u32[]{:S(2)}) collective-permute-start(bf16[640,640]{1,0:T(8,128)(2,1)} %collective-permute-done.2), channel_id=1, source_target_pairs={{0,16},{16,0},{1,17},{17,1},{2,18},{18,2},{3,19},{19,3},{4,20},{20... | collective-permute-start | bytes 2457608 | tf_op jit(solution)/shard_map/ppermute | solution.py:34
  58.5 36.9 %all-to-all-start.2 = ((bf16[8,48,1280]{2,1,0:T(8,128)(2,1)}), bf16[8,48,1280]{2,1,0:T(8,128)(2,1)S(1)}, u32[]{:S(2)}, u32[]{:S(2)}) async-start(bf16[8,48,1280]{2,1,0:T(8,128)(2,1)} %bitcast.11), calls=%async_computation.2 | async-start | bytes 1966080 | tf_op jit(solution)/shard_map/all_to_all | solution.py:83
  67.6 74.9 %all-gather.3.cloned.1.call-start = ((), (), s32[]{:S(2)}) async-start(), calls=%async_computation.5 | async-start | bytes 2211840 | tf_op jit(solution)/shard_map/all_gather | solution.py:101
  68.6 14.5 %collective-permute-start.8 = (bf16[4,4,24,640]{3,2,1,0:T(8,128)(2,1)S(1)}, bf16[4,4,24,640]{3,2,1,0:T(8,128)(2,1)S(1)}, u32[]{:S(2)}, u32[]{:S(2)}) collective-permute-start(bf16[4,4,24,640]{3,2,1,0:T(8,128)(2,1)S(1)} %slice.75), channel_id=1, source_target_pairs={{0,1},{1,0},{2,3},{3,2},{4,5},{5,4},{6,7},{7,6},{8,9},{9,8},{10,11... | collective-permute-start | bytes 1474568 | tf_op jit(solution)/shard_map/ppermute | solution.py:34
  70.7 4.5 %collective-permute-start.4 = (bf16[2,24,640]{2,1,0:T(8,128)(2,1)S(1)}, bf16[2,24,640]{2,1,0:T(8,128)(2,1)S(1)}, u32[]{:S(2)}, u32[]{:S(2)}) collective-permute-start(bf16[2,24,640]{2,1,0:T(8,128)(2,1)S(1)} %fusion.38), channel_id=1, source_target_pairs={{0,16},{16,0},{1,17},{17,1},{2,18},{18,2},{3,19},{19,3},{4,20},{20... | collective-permute-start | bytes 184328 | tf_op jit(solution)/shard_map/ppermute | solution.py:34
  75.2 49.0 %collective-permute-start.5 = (bf16[640,640]{1,0:T(8,128)(2,1)}, bf16[640,640]{1,0:T(8,128)(2,1)}, u32[]{:S(2)}, u32[]{:S(2)}) collective-permute-start(bf16[640,640]{1,0:T(8,128)(2,1)} %param.8), channel_id=1, source_target_pairs={{0,16},{16,0},{1,17},{17,1},{2,18},{18,2},{3,19},{19,3},{4,20},{20... | collective-permute-start | bytes 2457608 | tf_op jit(solution)/shard_map/ppermute | solution.py:34
  77.5 46.8 %collective-permute-start.6 = (bf16[640,640]{1,0:T(8,128)(2,1)}, bf16[640,640]{1,0:T(8,128)(2,1)}, u32[]{:S(2)}, u32[]{:S(2)}) collective-permute-start(bf16[640,640]{1,0:T(8,128)(2,1)} %param.8), channel_id=1, source_target_pairs={{0,1},{1,0},{2,3},{3,2},{4,5},{5,4},{6,7},{7,6},{8,9},{9,8},{10,11... | collective-permute-start | bytes 2457608 | tf_op jit(solution)/shard_map/ppermute | solution.py:34
  80.7 43.6 %collective-permute-start.7 = (bf16[640,640]{1,0:T(8,128)(2,1)}, bf16[640,640]{1,0:T(8,128)(2,1)}, u32[]{:S(2)}, u32[]{:S(2)}) collective-permute-start(bf16[640,640]{1,0:T(8,128)(2,1)} %param.8), channel_id=1, source_target_pairs={{0,17},{1,16},{16,1},{17,0},{2,19},{3,18},{18,3},{19,2},{4,21},{5,... | collective-permute-start | bytes 2457608 | tf_op jit(solution)/shard_map/ppermute | solution.py:42
  84.3 48.2 %collective-permute-start.9 = (bf16[4,4,2,24,640]{4,3,1,0,2:T(8,128)(2,1)}, bf16[4,4,2,24,640]{4,3,1,0,2:T(8,128)(2,1)}, u32[]{:S(2)}, u32[]{:S(2)}) collective-permute-start(bf16[4,4,2,24,640]{4,3,1,0,2:T(8,128)(2,1)} %pad_maximum_fusion.2), channel_id=1, source_target_pairs={{0,16},{16,0},{1,17},{17,1},{2,18},{18,2},{3,19},{19,3},{4,20},{20... | collective-permute-start | bytes 2949128 | tf_op jit(solution)/shard_map/ppermute | solution.py:34
  121.9 31.5 %collective-permute-start.10 = (bf16[384,1280]{1,0:T(8,128)(2,1)}, bf16[384,1280]{1,0:T(8,128)(2,1)}, u32[]{:S(2)}, u32[]{:S(2)}) collective-permute-start(bf16[384,1280]{1,0:T(8,128)(2,1)} %all_gather.9), channel_id=1, source_target_pairs={{0,1},{1,0},{2,3},{3,2},{4,5},{5,4},{6,7},{7,6},{8,9},{9,8},{10,11... | collective-permute-start | bytes 2949128 | tf_op jit(solution)/shard_map/ppermute | solution.py:34
  128.9 18.6 %all-to-all-start.3 = ((bf16[4,4,24,1280]{3,2,1,0:T(8,128)(2,1)}), bf16[4,4,24,1280]{3,2,1,0:T(8,128)(2,1)S(1)}, u32[]{:S(2)}, u32[]{:S(2)}) async-start(bf16[4,4,24,1280]{3,2,1,0:T(8,128)(2,1)} %bitcast.83), calls=%async_computation.3 | async-start | bytes 1966080 | tf_op jit(solution)/shard_map/all_to_all | solution.py:117
  134.1 30.4 %collective-permute-start.11 = (bf16[384,1280]{1,0:T(8,128)(2,1)}, bf16[384,1280]{1,0:T(8,128)(2,1)}, u32[]{:S(2)}, u32[]{:S(2)}) collective-permute-start(bf16[384,1280]{1,0:T(8,128)(2,1)} %all_gather.9), channel_id=1, source_target_pairs={{0,16},{16,0},{1,17},{17,1},{2,18},{18,2},{3,19},{19,3},{4,20},{20... | collective-permute-start | bytes 2949128 | tf_op jit(solution)/shard_map/ppermute | solution.py:34
  148.5 15.4 %all-to-all-start.4 = ((bf16[8,24,640]{2,1,0:T(8,128)(2,1)}), bf16[8,24,640]{2,1,0:T(8,128)(2,1)S(1)}, u32[]{:S(2)}, u32[]{:S(2)}) async-start(bf16[8,24,640]{2,1,0:T(8,128)(2,1)} %bitcast.36), calls=%async_computation.4 | async-start | bytes 491520 | tf_op jit(solution)/shard_map/all_to_all | solution.py:123
  154.9 9.6 %collective-permute-start.12 = (bf16[384,640]{1,0:T(8,128)(2,1)S(1)}, bf16[384,640]{1,0:T(8,128)(2,1)S(1)}, u32[]{:S(2)}, u32[]{:S(2)}) collective-permute-start(bf16[384,640]{1,0:T(8,128)(2,1)S(1)} %get-tuple-element.29), channel_id=1, source_target_pairs={{0,16},{16,0},{1,17},{17,1},{2,18},{18,2},{3,19},{19,3},{4,20},{20... | collective-permute-start | bytes 1474568 | tf_op jit(solution)/shard_map/ppermute | solution.py:34
  165.9 1.5 copy-start
Sparse Core Ops, SparseCore 0:
  11.2 65.2 all-gather.4
  78.6 44.7 all-gather.2
